TPU v7x, 256 devices: a whole 4x4x8 slice. The times are simulated.
256 devices in a mesh: op: 16 (over x_hi, z), qn: 16 (over y, x_lo, core).
Axes of the slice: x: 4 (x_hi: 2, x_lo: 2; x = x_hi * 2 + x_lo), y: 4, z: 8, core: 2. Of those that a mesh axis runs over, the one named last changes fastest.
Arguments:
- psi_start: float32 [32, 256, 256], P('qn'), may hold values from -150 to 150
- left_ops: bfloat16 [512, 256, 256], P('op'), may hold values from -1 to 1
- right_ops: bfloat16 [512, 256, 256], P('op'), may hold values from -1 to 1
- sources: int32 [512, 32, 3], P('op', 'qn'), may hold values from 0 to 31, as said below
Outputs:
- ritz: float32 [32, 256, 256], P('qn')
- ritz_residual: float32 [32, 256, 256], P('qn')
Inputs may be any that keep to these rules, and one draw needn't show every extreme that they name: The first source of every operator and target block is the block itself: sources[k, b, 0] = b; the other sources are any blocks.
All inputs are finite; a program needn't handle non-finite values.
Results may differ from a plain program's by a relative error of at most 0.0065.
Values may be sent and summed in bfloat16 or wider, within the bound.
No kernel may reach another device: no remote copies, remote signals or barrier semaphores. Data moves between devices by JAX's collectives and lax.ppermute only.
A program may use at most 64 MiB of HBM per device.

v0:
```python
import jax
import jax.numpy as jnp
from jax import lax
from jax.sharding import PartitionSpec as P

epsilon = 1e-06


def shards(psi_start, left_ops, right_ops, sources):
    blk_dev, width, _ = psi_start.shape
    total_blocks = blk_dev * lax.axis_size("qn")
    count = float(total_blocks * width * width)
    labels = jnp.arange(total_blocks, dtype=jnp.int32)
    weights = jnp.sum((sources[..., None] == labels).astype(jnp.float32), axis=2).astype(
        jnp.bfloat16
    )

    def fold_blocks(piece):
        return jnp.einsum("kbc,cxy->kbxy", weights, piece, preferred_element_type=jnp.float32)

    def project(gathered_sum):
        inputs = gathered_sum.astype(jnp.bfloat16)
        lefted = jnp.einsum("kxz,kbzy->kbxy", left_ops, inputs, preferred_element_type=jnp.float32)
        lefted = lefted.astype(jnp.bfloat16)
        partial_terms = jnp.einsum(
            "kbxy,kzy->bxz", lefted, right_ops, preferred_element_type=jnp.float32
        )
        return lax.psum(partial_terms, "op")

    def totals(values):
        return lax.psum(values, "qn")

    start_sum = lax.psum(jnp.sum(psi_start * psi_start), "qn")
    first = psi_start * lax.rsqrt(start_sum / count + epsilon)
    first_sum = fold_blocks(lax.all_gather(first.astype(jnp.bfloat16), "qn", axis=0, tiled=True))
    sigma_one = project(first_sum)
    energy = totals(jnp.sum(first * sigma_one)) / count
    rest = sigma_one - energy * first
    rest_sum = totals(jnp.sum(rest * rest))
    second = rest * lax.rsqrt(rest_sum / count + epsilon)
    second_sum = fold_blocks(lax.all_gather(second.astype(jnp.bfloat16), "qn", axis=0, tiled=True))
    sigma_two = project(second_sum)
    cross_one, cross_two, diag_sum = totals(
        (jnp.sum(first * sigma_two), jnp.sum(second * sigma_one), jnp.sum(second * sigma_two))
    )
    cross_one = cross_one / count
    cross_two = cross_two / count
    diag_d = diag_sum / count
    coupling = 0.5 * (cross_one + cross_two)
    theta = 0.5 * (energy + diag_d) - jnp.sqrt(0.25 * (energy - diag_d) ** 2 + coupling * coupling)
    weight_one = diag_d - theta
    ritz = weight_one * first - coupling * second
    ritz_residual = weight_one * sigma_one - coupling * sigma_two - theta * ritz
    return (ritz, ritz_residual)


def solution(mesh):
    in_specs = (P("qn", None, None), P("op", None, None), P("op", None, None), P("op", "qn", None))
    out_specs = (P("qn", None, None), P("qn", None, None))
    return jax.shard_map(shards, mesh=mesh, in_specs=in_specs, out_specs=out_specs, check_vma=False)
```

profile of v0, /device:TPU:32, one launch (start us, length us, event | category | flops | bytes accessed | tf_op | source)
XLA Modules:
  0.0 579.8 jit_solution(12428912841847462440)
XLA Ops:
  7.2 0.0 all-gather.3.cloned.1.call-start
  7.2 1.8 multiply_reduce_fusion.5
  9.0 31.1 %psum.56 = f32[]{:T(128)} all-reduce(f32[]{:T(128)} %multiply_reduce_fusion.5), channel_id=1, replica_groups=mesh['op'=16,'qn'=16] {'qn'}, use_global_device_ids=true, to_apply=%region_2.0 | all-reduce | flops 1 | bytes 8 | tf_op jit(solution)/shard_map/psum | solution.py:33
  40.8 1.8 multiply_convert_fusion.1
  42.6 0.0 all-gather.3.cloned.1.call-update
  42.6 0.0 all-reduce.4.cloned.1.call-start
  42.7 0.7 copy.8
  43.4 0.1 convert_reduce_fusion
  43.5 38.9 %all-gather.3.cloned.1.call-done = bf16[32,256,256]{2,1,0:T(8,128)(2,1)} async-done(((bf16[2,256,256]{2,1,0:T(8,128)(2,1)}), bf16[32,256,256]{2,1,0:T(8,128)(2,1)}) %all-gather.3.cloned.1.call-update) | async-done | bytes 4194320 | tf_op jit(solution)/shard_map/all_gather | solution.py:35
  82.4 8.3 %convolution_convert_fusion.1 = bf16[32,2,256,256]{3,0,2,1:T(8,128)(2,1)} fusion(bf16[32,256,256]{2,1,0:T(8,128)(2,1)} %all-gather.3.cloned.1.call-done, bf16[32,2,32]{2,0,1:T(8,128)(2,1)S(1)} %convert_reduce_fusion), kind=kOutput, calls=%fused_computation.11 | convolution fusion | flops 272629760 | bytes 12587008 | tf_op jit(solution)/shard_map/kbc,cxy->kbxy/dot_general | solution.py:19
  90.7 0.0 copy-start
  90.7 14.7 %fusion.28 = f32[2,256,256]{2,1,0:T(8,128)} fusion(bf16[32,256,256]{2,1,0:T(8,128)(2,1)} %param.6, bf16[32,2,256,256]{3,0,2,1:T(8,128)(2,1)} %convolution_convert_fusion.1, bf16[32,256,256]{2,1,0:T(8,128)(2,1)} %param.5), kind=kOutput, calls=%fused_computation.20 | convolution fusion | flops 4299161600 | bytes 17301504 | tf_op jit(solution)/shard_map/kbxy,kzy->bxz/dot_general | solution.py:25
  105.4 0.0 all-reduce.4.cloned.1.call-update
  105.4 0.0 all-gather.5.cloned.1.call-start
  105.4 155.9 %all-reduce.4.cloned.1.call-done = f32[2,256,256]{2,1,0:T(8,128)} async-done(((f32[2,256,256]{2,1,0:T(8,128)}), f32[2,256,256]{2,1,0:T(8,128)}) %all-reduce.4.cloned.1.call-update) | async-done | bytes 524304 | tf_op jit(solution)/shard_map/psum | solution.py:28
  261.3 0.0 copy-done
  261.3 1.8 multiply_reduce_fusion.4
  263.1 27.8 %psum.58 = f32[]{:T(128)} all-reduce(f32[]{:T(128)} %multiply_reduce_fusion.4), channel_id=1, replica_groups=mesh['op'=16,'qn'=16] {'qn'}, use_global_device_ids=true, to_apply=%region_5.0 | all-reduce | flops 1 | bytes 8 | tf_op jit(solution)/shard_map/psum | solution.py:31
  291.6 1.8 multiply_reduce_fusion.3
  293.4 27.8 %psum.59 = f32[]{:T(128)} all-reduce(f32[]{:T(128)} %get-tuple-element.9), channel_id=1, replica_groups=mesh['op'=16,'qn'=16] {'qn'}, use_global_device_ids=true, to_apply=%region_7.0 | all-reduce | flops 1 | bytes 8 | tf_op jit(solution)/shard_map/psum | solution.py:31
  321.8 0.7 multiply_convert_fusion
  322.6 0.0 all-gather.5.cloned.1.call-update
  322.6 0.2 all-reduce.6.cloned.1.call-start
  322.8 35.6 %all-gather.5.cloned.1.call-done = bf16[32,256,256]{2,1,0:T(8,128)(2,1)} async-done(((bf16[2,256,256]{2,1,0:T(8,128)(2,1)}), bf16[32,256,256]{2,1,0:T(8,128)(2,1)}) %all-gather.5.cloned.1.call-update) | async-done | bytes 4194320 | tf_op jit(solution)/shard_map/all_gather | solution.py:41
  358.4 8.4 %convolution_convert_fusion = bf16[32,2,256,256]{3,0,2,1:T(8,128)(2,1)} fusion(bf16[32,256,256]{2,1,0:T(8,128)(2,1)} %all-gather.5.cloned.1.call-done, bf16[32,2,32]{2,0,1:T(8,128)(2,1)S(1)} %convert_reduce_fusion), kind=kOutput, calls=%fused_computation.10 | convolution fusion | flops 272629760 | bytes 12587008 | tf_op jit(solution)/shard_map/kbc,cxy->kbxy/dot_general | solution.py:19
  366.8 0.0 copy-start.1
  366.8 14.7 %fusion.37 = f32[2,256,256]{2,1,0:T(8,128)} fusion(bf16[32,256,256]{2,1,0:T(8,128)(2,1)} %param.6, bf16[32,2,256,256]{3,0,2,1:T(8,128)(2,1)} %convolution_convert_fusion, bf16[32,256,256]{2,1,0:T(8,128)(2,1)} %param.5), kind=kOutput, calls=%fused_computation.21 | convolution fusion | flops 4299161600 | bytes 17301504 | tf_op jit(solution)/shard_map/kbxy,kzy->bxz/dot_general | solution.py:25
  381.5 0.0 all-reduce.6.cloned.1.call-update
  381.5 155.8 %all-reduce.6.cloned.1.call-done = f32[2,256,256]{2,1,0:T(8,128)} async-done(((f32[2,256,256]{2,1,0:T(8,128)}), f32[2,256,256]{2,1,0:T(8,128)}) %all-reduce.6.cloned.1.call-update) | async-done | bytes 524304 | tf_op jit(solution)/shard_map/psum | solution.py:28
  537.3 0.0 copy-done.1
  537.3 1.9 multiply_reduce_fusion.2
  540.6 27.9 %all-reduce = (f32[]{:T(128)}, f32[]{:T(128)}) all-reduce(f32[]{:T(128)S(6)} %div.20, f32[]{:T(128)} %get-tuple-element.2), channel_id=1, replica_groups=mesh['op'=16,'qn'=16] {'qn'}, use_global_device_ids=true, to_apply=%region_12.0 | all-reduce | flops 2 | bytes 16 | tf_op jit(solution)/shard_map/psum | solution.py:31
  571.1 2.2 multiply_subtract_fusion
Async XLA Ops:
  7.2 75.2 %all-gather.3.cloned.1.call-start = ((), (), s32[]{:S(2)}) async-start(), calls=%async_computation | async-start | bytes 4456448 | tf_op jit(solution)/shard_map/all_gather | solution.py:35
  42.6 218.7 %all-reduce.4.cloned.1.call-start = ((), (), s32[]{:S(2)}) async-start(), calls=%async_computation.1 | async-start | bytes 1048576 | tf_op jit(solution)/shard_map/psum | solution.py:28
  90.7 170.6 %copy-start = (f32[2,256,256]{2,1,0:T(8,128)S(1)}, f32[2,256,256]{2,1,0:T(8,128)}, u32[]{:S(2)}) copy-start(f32[2,256,256]{2,1,0:T(8,128)} %param.4) | copy-start | bytes 1572868
  105.4 253.0 %all-gather.5.cloned.1.call-start = ((), (), s32[]{:S(2)}) async-start(), calls=%async_computation.2 | async-start | bytes 4456448 | tf_op jit(solution)/shard_map/all_gather | solution.py:41
  322.6 214.7 %all-reduce.6.cloned.1.call-start = ((), (), s32[]{:S(2)}) async-start(), calls=%async_computation.3 | async-start | bytes 1048576 | tf_op jit(solution)/shard_map/psum | solution.py:28
  366.8 170.5 %copy-start.1 = (f32[2,256,256]{2,1,0:T(8,128)S(1)}, f32[2,256,256]{2,1,0:T(8,128)}, u32[]{:S(2)}) copy-start(f32[2,256,256]{2,1,0:T(8,128)} %all-reduce.4.cloned.1.call-done) | copy-start | bytes 1572868
Sparse Core Ops, SparseCore 0:
  42.7 39.5 all-gather.2
  105.5 155.7 all-reduce.3
  322.7 35.6 all-gather.4
  381.6 155.6 all-reduce.5
where the time goes:
time: 582 us; the launch traced here: 580 us
  waiting for transfers between devices  386 us (66%)
  blocking collectives  115 us (20%)
  matrix products  46 us (8%)
  between operations  19.8 us (3%)
  other arithmetic  12 us (2%)
    psum x2, waiting for transfers between devices, project(): return lax.psum(partial_terms, 'op')  312 us
    psum x3, blocking collectives, totals(): return lax.psum(values, 'qn')  83.5 us
    all_gather x1, waiting for transfers between devices, shards(): lax.all_gather(first.astype(jnp.bfloat16), 'qn', axis=0, tiled=True)  38.9 us
    all_gather x1, waiting for transfers between devices, shards(): lax.all_gather(second.astype(jnp.bfloat16), 'qn', axis=0, tiled=True)  35.6 us
    psum x1, blocking collectives, shards(): start_sum = lax.psum(jnp.sum(psi_start * psi_start), 'qn')  31.1 us
    dot_general x2, matrix products, project(): jnp.einsum('kbxy,kzy->bxz', lefted, right_ops, preferred_element_type=jnp...  29.3 us
    dot_general x2, matrix products, fold_blocks(): jnp.einsum('kbc,cxy->kbxy', weights, piece, preferred_element_type=jnp.fl...  16.7 us
  transfers between devices with their start and end apart: 4, of which 4 were waited for; matrix products, arithmetic and copies ran while one was open for 0% of the time, Pallas kernels for 0%

commit v1 on v0

v1 whole, which is shorter than its diff:
```python
import jax
import jax.numpy as jnp
from jax import lax
from jax.experimental import pallas as pl
from jax.experimental.pallas import tpu as pltpu
from jax.sharding import PartitionSpec as P

epsilon = 1e-06
BF, F32 = jnp.bfloat16, jnp.float32
GROUP = 8
HALF = 128


def ham_kernel(meta, d0, d1, d2, d3, d4, d5a, d5b, d5c, d6, d7, l_ref, ra_ref, rb_ref, mine, other, v, lefted, rights, acc):
    step = pl.program_id(0)

    @pl.when(step == 0)
    def _():
        for slot, piece in enumerate((d0, d1, d2, d3, d4, None, d6, d7)):
            if piece is not None:
                v[4 * slot : 4 * slot + 4] = piece[...]
        v[20:22] = d5a[...]
        v[22:23] = d5b[...]
        v[23:24] = d5c[...]
        acc[...] = jnp.zeros_like(acc)

    for i in range(GROUP):
        rights[:HALF, HALF * i : HALF * (i + 1)] = ra_ref[i]
        rights[HALF:, HALF * i : HALF * (i + 1)] = rb_ref[i]
    for i in range(GROUP):
        sums = []
        for b in range(4):
            at = ((step * GROUP + i) * 4 + b) * 3
            total = v[meta[at]].astype(F32) + v[meta[at + 1]].astype(F32) + v[meta[at + 2]].astype(F32)
            sums.append(total.astype(BF))
        product = jnp.dot(l_ref[i], jnp.concatenate(sums, axis=1), preferred_element_type=F32).astype(BF)
        for b in range(4):
            lefted[256 * b : 256 * (b + 1), HALF * i : HALF * (i + 1)] = product[:, HALF * b : HALF * (b + 1)]
    acc[...] += lax.dot_general(
        lefted[...], rights[...], (((1,), (1,)), ((), ())), preferred_element_type=F32
    )

    @pl.when(step == pl.num_programs(0) - 1)
    def _():
        mine[...] = acc[:, :HALF]
        other[...] = acc[:, HALF:].astype(BF)


def apply_ham(meta, pieces, left_ops, right_ops):
    ops = left_ops.shape[0]
    core = 12 * ops
    full = lambda a: pl.BlockSpec(a.shape, lambda g, m: (0,) * a.ndim)
    return pl.pallas_call(
        ham_kernel,
        grid_spec=pltpu.PrefetchScalarGridSpec(
            num_scalar_prefetch=1,
            grid=(ops // GROUP,),
            in_specs=[full(a) for a in pieces]
            + [
                pl.BlockSpec((GROUP, 256, 256), lambda g, m: (g, 0, 0)),
                pl.BlockSpec((GROUP, HALF, HALF), lambda g, m: (g, m[core], m[core])),
                pl.BlockSpec((GROUP, HALF, HALF), lambda g, m: (g, 1 - m[core], m[core])),
            ],
            out_specs=[pl.BlockSpec((1024, HALF), lambda g, m: (0, 0))] * 2,
            scratch_shapes=[
                pltpu.VMEM((32, 256, HALF), BF),
                pltpu.VMEM((1024, GROUP * HALF), BF),
                pltpu.VMEM((256, GROUP * HALF), BF),
                pltpu.VMEM((1024, 256), F32),
            ],
        ),
        out_shape=[jax.ShapeDtypeStruct((1024, HALF), F32), jax.ShapeDtypeStruct((1024, HALF), BF)],
        compiler_params=pltpu.CompilerParams(vmem_limit_bytes=40 * 1024 * 1024),
    )(meta, *pieces, left_ops, right_ops, right_ops)


def swap(x, bits):
    return lax.ppermute(x, "qn", [(i, i ^ bits) for i in range(16)])


def gather_chips(own):
    x1, y1, y3 = swap(own, 2), swap(own, 4), swap(own, 12)
    x1y1, y2, x1y3 = swap(x1, 4), swap(y1, 12), swap(y3, 2)
    far = swap(y2[:2], 2), swap(x1y3[2:3], 4), swap(x1y1[3:], 12)
    return (own, x1, y1, x1y1, y2) + far + (y3, x1y3)


def sum_over_op(mine, other):
    part = mine + swap(other, 1).astype(F32)
    parts = lax.all_to_all(part.astype(BF).reshape(16, 64, HALF), "op", 0, 0, tiled=True)
    piece = jnp.sum(parts.astype(F32), axis=0).astype(BF)
    whole = lax.all_to_all(jnp.broadcast_to(piece[None], (16, 64, HALF)), "op", 0, 0, tiled=True)
    return whole.reshape(4, 256, HALF)


def shards(psi_start, left_ops, right_ops, sources):
    place = lax.axis_index("qn")
    core = place % 2
    chip = place // 2
    count = 32.0 * 256.0 * 256.0

    def halves(a):
        low, high = a[:, :, :HALF], a[:, :, HALF:]
        return jnp.where(core == 0, low, high), jnp.where(core == 0, high, low)

    def in_order(a, b, axis=0):
        return jnp.where(core == 0, jnp.concatenate([a, b], axis), jnp.concatenate([b, a], axis))

    keep, give = halves(psi_start)
    p = in_order(keep, swap(give, 1))
    src = in_order(sources, swap(sources, 1), 1) ^ (chip * 4)
    meta = jnp.concatenate([src.reshape(-1), core.reshape(1)]).astype(jnp.int32)

    u = sum_over_op(*apply_ham(meta, gather_chips(p.astype(BF)), left_ops, right_ops))
    w = sum_over_op(*apply_ham(meta, gather_chips(u), left_ops, right_ops))
    u, w = u.astype(F32), w.astype(F32)

    dots = jnp.stack([jnp.sum(p * p), jnp.sum(p * u), jnp.sum(u * u), jnp.sum(p * w), jnp.sum(u * w)])
    rows = jnp.broadcast_to(jnp.pad(dots, (0, 123))[None, None], (16, 8, 128))
    totals = jnp.sum(lax.all_to_all(rows, "qn", 0, 0, tiled=True)[:, 0], axis=0) / count
    pp, pu, uu, pw, uw = (totals[i] for i in range(5))

    s = lax.rsqrt(pp + epsilon)
    energy = s * s * pu
    t = lax.rsqrt(s * s * (uu - 2.0 * energy * pu + energy * energy * pp) + epsilon)
    ts = t * s
    diag_d = ts * ts * (uw - energy * (uu + pw) + energy * energy * pu)
    coupling = 0.5 * ts * s * ((pw - energy * pu) + (uu - energy * pu))
    theta = 0.5 * (energy + diag_d) - jnp.sqrt(0.25 * (energy - diag_d) ** 2 + coupling * coupling)
    weight_one = diag_d - theta
    ritz = weight_one * s * p - coupling * ts * (u - energy * p)
    residual = weight_one * s * u - coupling * ts * (w - energy * u) - theta * ritz

    def own_blocks(a):
        low, high = a[:2], a[2:]
        kept = jnp.where(core == 0, low, high)
        got = swap(jnp.where(core == 0, high, low), 1)
        return in_order(kept, got, 2)

    return own_blocks(ritz), own_blocks(residual)


def solution(mesh):
    in_specs = (P("qn", None, None), P("op", None, None), P("op", None, None), P("op", "qn", None))
    out_specs = (P("qn", None, None), P("qn", None, None))
    return jax.shard_map(shards, mesh=mesh, in_specs=in_specs, out_specs=out_specs, check_vma=False)
```

time: 582 us -> 185 us (0.32)
  waiting for transfers between devices: 386 us -> 50.1 us
  blocking collectives: 115 us -> 54.3 us
  matrix products: 46 us -> 0 us
  starting transfers between devices: 0.34 us -> 31.4 us
  Pallas kernels: 0 us -> 18.3 us
  local copies, waits for them, and re-layouts: 0.7 us -> 14.5 us
  between operations: 19.8 us -> 8.53 us
  other arithmetic: 12 us -> 5.88 us
    psum x2 -> x0, waiting for transfers between devices: 312 us -> none  [project(): return lax.psum(partial_terms, 'op')]
    psum x4 -> x0, blocking collectives: 115 us -> none  [the longest x3 83.5 us: totals(): return lax.psum(values, 'qn')]
    all_gather x2 -> x0, waiting for transfers between devices: 74.5 us -> none  [the longest x1 38.9 us: shards(): lax.all_gather(first.astype(jnp.bfloat16), 'qn', axis=0, tiled=True)]
    all_to_all x0 -> x3, blocking collectives: none -> 54.3 us  [the longest x2 38.5 us: sum_over_op(): lax.all_to_all(part.astype(BF).reshape(16, 64, HALF), 'op', 0, 0, tiled=T...]
    dot_general x4 -> x0, matrix products: 46 us -> none  [the longest x2 29.3 us: project(): jnp.einsum('kbxy,kzy->bxz', lefted, right_ops, preferred_element_type=jnp...]
    ppermute x0 -> x24, waiting for transfers between devices: none -> 33.4 us  [swap(): return lax.ppermute(x, 'qn', [(i, i ^ bits) for i in range(16)])]
    ppermute x0 -> x24, starting transfers between devices: none -> 23.3 us  [swap(): return lax.ppermute(x, 'qn', [(i, i ^ bits) for i in range(16)])]
    pallas_call x0 -> x2, Pallas kernels: none -> 18.3 us  [apply_ham(): pl.pallas_call(ham_kernel, grid_spec=pltpu.PrefetchScalarGridSpec(num_sca...]
  transfers between devices with their start and end apart: 4 -> 26, of which waited for: 4 -> 17; matrix products, arithmetic and copies ran while one was open for 0% -> 2% of each run, Pallas kernels for 0% -> 0%
where the time goes in v1:
time: 185 us; the launch traced here: 183 us
  blocking collectives  54.3 us (29%)
  waiting for transfers between devices  50.1 us (27%)
  starting transfers between devices  31.4 us (17%)
  Pallas kernels  18.3 us (10%)
  local copies, waits for them, and re-layouts  14.5 us (8%)
  between operations  8.53 us (5%)
  other arithmetic  5.88 us (3%)
    all_to_all x2, blocking collectives, sum_over_op(): lax.all_to_all(part.astype(BF).reshape(16, 64, HALF), 'op', 0, 0, tiled=T...  38.5 us
    ppermute x24, waiting for transfers between devices, swap(): return lax.ppermute(x, 'qn', [(i, i ^ bits) for i in range(16)])  33.4 us
    ppermute x24, starting transfers between devices, swap(): return lax.ppermute(x, 'qn', [(i, i ^ bits) for i in range(16)])  23.3 us
    pallas_call x2, Pallas kernels, apply_ham(): pl.pallas_call(ham_kernel, grid_spec=pltpu.PrefetchScalarGridSpec(num_sca...  18.3 us
    all_to_all x1, blocking collectives, sum_over_op(): lax.all_to_all(jnp.broadcast_to(piece[None], (16, 64, HALF)), 'op', 0, 0,...  15.8 us
    all_to_all x1, waiting for transfers between devices, sum_over_op(): lax.all_to_all(jnp.broadcast_to(piece[None], (16, 64, HALF)), 'op', 0, 0,...  10.7 us
    unnamed x8, local copies, waits for them, and re-layouts  8.75 us
    all_to_all x1, waiting for transfers between devices, shards(): lax.all_to_all(rows, 'qn', 0, 0, tiled=True)[:, 0]  6.05 us
  transfers between devices with their start and end apart: 26, of which 17 were waited for; matrix products, arithmetic and copies ran while one was open for 2% of the time, Pallas kernels for 0%

profile of v1, /device:TPU:32, one launch (start us, length us, event | category | flops | bytes accessed | tf_op | source)
XLA Modules:
  0.0 183.1 jit_solution(7073706719599618776)
XLA Ops:
  0.6 1.1 slice_select_fusion.4
  1.8 1.5 collective-permute-done
  3.4 1.7 collective-permute-start.3
  5.1 1.5 collective-permute-start.2
  6.6 2.2 %collective-permute-start.7 = (bf16[4,256,128]{2,1,0:T(8,128)(2,1)S(1)}, bf16[4,256,128]{2,1,0:T(8,128)(2,1)S(1)}, u32[]{:S(2)}, u32[]{:S(2)}) collective-permute-start(bf16[4,256,128]{2,1,0:T(8,128)(2,1)S(1)} %get-tuple-element.14.d0), channel_id=1, source_target_pairs={{0,12},{1,13},{2,14},{3,15},{4,8},{5,9},{6,10},{7,11},{8,4},{9,5},... | collective-permute-start | bytes 786440 | tf_op jit(solution)/shard_map/ppermute | solution.py:78
  8.7 3.1 %collective-permute-done.3.d2 = bf16[4,256,128]{2,1,0:T(8,128)(2,1)S(1)} collective-permute-done((bf16[4,256,128]{2,1,0:T(8,128)(2,1)S(1)}, bf16[4,256,128]{2,1,0:T(8,128)(2,1)S(1)}, u32[]{:S(2)}, u32[]{:S(2)}) %collective-permute-start.3) | collective-permute-done | bytes 262176 | tf_op jit(solution)/shard_map/ppermute | solution.py:78
  11.8 3.0 %collective-permute-start.5 = (bf16[4,256,128]{2,1,0:T(8,128)(2,1)S(1)}, bf16[4,256,128]{2,1,0:T(8,128)(2,1)S(1)}, u32[]{:S(2)}, u32[]{:S(2)}) collective-permute-start(bf16[4,256,128]{2,1,0:T(8,128)(2,1)S(1)} %collective-permute-done.3.d2), channel_id=1, source_target_pairs={{0,12},{1,13},{2,14},{3,15},{4,8},{5,9},{6,10},{7,11},{8,4},{9,5},... | collective-permute-start | bytes 786440 | tf_op jit(solution)/shard_map/ppermute | solution.py:78
  15.0 1.0 collective-permute-done.7.d6
  16.5 4.7 %collective-permute-done.5.d4 = bf16[4,256,128]{2,1,0:T(8,128)(2,1)S(1)} collective-permute-done((bf16[4,256,128]{2,1,0:T(8,128)(2,1)S(1)}, bf16[4,256,128]{2,1,0:T(8,128)(2,1)S(1)}, u32[]{:S(2)}, u32[]{:S(2)}) %collective-permute-start.5) | collective-permute-done | bytes 262176 | tf_op jit(solution)/shard_map/ppermute | solution.py:78
  21.2 1.0 collective-permute-start.6
  22.2 0.8 fusion.9
  23.4 3.0 %collective-permute-start.10 = (bf16[1,256,128]{2,1,0:T(8,128)(2,1)S(1)}, bf16[1,256,128]{2,1,0:T(8,128)(2,1)S(1)}, u32[]{:S(2)}, u32[]{:S(2)}) collective-permute-start(bf16[1,256,128]{2,1,0:T(8,128)(2,1)S(1)} %slice.74), channel_id=1, source_target_pairs={{0,12},{1,13},{2,14},{3,15},{4,8},{5,9},{6,10},{7,11},{8,4},{9,5},... | collective-permute-start | bytes 196616 | tf_op jit(solution)/shard_map/ppermute | solution.py:78
  26.5 2.4 %collective-permute-done.10.d5c = bf16[1,256,128]{2,1,0:T(8,128)(2,1)S(1)} collective-permute-done((bf16[1,256,128]{2,1,0:T(8,128)(2,1)S(1)}, bf16[1,256,128]{2,1,0:T(8,128)(2,1)S(1)}, u32[]{:S(2)}, u32[]{:S(2)}) %collective-permute-start.10) | collective-permute-done | bytes 65568 | tf_op jit(solution)/shard_map/ppermute | solution.py:78
  28.9 1.8 %collective-permute-done.9.d5b = bf16[1,256,128]{2,1,0:T(8,128)(2,1)S(1)} collective-permute-done((bf16[1,256,128]{2,1,0:T(8,128)(2,1)S(1)}, bf16[1,256,128]{2,1,0:T(8,128)(2,1)S(1)}, u32[]{:S(2)}, u32[]{:S(2)}) %collective-permute-start.9) | collective-permute-done | bytes 65568 | tf_op jit(solution)/shard_map/ppermute | solution.py:78
  30.8 2.2 %copy-done = bf16[32,256,256]{2,1,0:T(8,128)(2,1)S(1)} copy-done((bf16[32,256,256]{2,1,0:T(8,128)(2,1)S(1)}, bf16[32,256,256]{2,1,0:T(8,128)(2,1)}, u32[]{:S(2)}) %copy-start) | copy-done | bytes 4194328
  33.0 2.2 %copy-done.2 = bf16[32,256,256]{2,1,0:T(8,128)(2,1)S(1)} copy-done((bf16[32,256,256]{2,1,0:T(8,128)(2,1)S(1)}, bf16[32,256,256]{2,1,0:T(8,128)(2,1)}, u32[]{:S(2)}) %copy-start.2) | copy-done | bytes 4194328
  35.2 9.2 %shard_map.59 = (f32[1024,128]{1,0:T(8,128)S(1)}, bf16[1024,128]{1,0:T(8,128)(2,1)S(1)}) custom-call(s32[385]{0:T(512)S(1)} %pad_add_fusion.meta, bf16[4,256,128]{2,1,0:T(8,128)(2,1)S(1)} %get-tuple-element.14.d0, bf16[4,256,128]{2,1,0:T(8,128)(2,1)S(1)} %collective-permute-done.2.d1, bf16[4,256,128]{2,1,0:T(8,128)(2,1)S(1)} %collective-permute-done.3.d2, ...), custom_call_target="tpu_custom_call" | custom-call | tf_op jit(solution)/shard_map/pallas_call | solution.py:53
  44.4 1.5 collective-permute-done.11
  46.0 22.4 %all_to_all.25 = bf16[16,64,128]{2,1,0:T(8,128)(2,1)S(1)} all-to-all(bf16[16,64,128]{2,1,0:T(8,128)(2,1)S(1)} %bitcast.31), channel_id=1, replica_groups=mesh['op'=16,'qn'=16] {'op'}, dimensions={0} | all-to-all | bytes 524288 | tf_op jit(solution)/shard_map/all_to_all | solution.py:90
  68.6 15.8 %all_to_all.26 = bf16[16,64,128]{2,1,0:T(8,128)(2,1)S(1)} all-to-all(bf16[16,64,128]{2,1,0:T(8,128)(2,1)S(1)} %broadcast_in_dim.6), channel_id=1, replica_groups=mesh['op'=16,'qn'=16] {'op'}, dimensions={0} | all-to-all | bytes 524288 | tf_op jit(solution)/shard_map/all_to_all | solution.py:92
  84.4 1.1 collective-permute-start.17
  85.7 5.0 %collective-permute-done.13.d2 = bf16[4,256,128]{2,1,0:T(8,128)(2,1)S(1)} collective-permute-done((bf16[4,256,128]{2,1,0:T(8,128)(2,1)S(1)}, bf16[4,256,128]{2,1,0:T(8,128)(2,1)S(1)}, u32[]{:S(2)}, u32[]{:S(2)}) %collective-permute-start.13) | collective-permute-done | bytes 262176 | tf_op jit(solution)/shard_map/ppermute | solution.py:78
  90.7 1.1 collective-permute-start.15
  91.9 0.8 collective-permute-done.17.d6
  92.9 2.6 %collective-permute-start.14 = (bf16[4,256,128]{2,1,0:T(8,128)(2,1)S(1)}, bf16[4,256,128]{2,1,0:T(8,128)(2,1)S(1)}, u32[]{:S(2)}, u32[]{:S(2)}) collective-permute-start(bf16[4,256,128]{2,1,0:T(8,128)(2,1)S(1)} %collective-permute-done.12.d1), channel_id=1, source_target_pairs={{0,4},{1,5},{2,6},{3,7},{4,0},{5,1},{6,2},{7,3},{8,12},{9,13},{10,... | collective-permute-start | bytes 786440 | tf_op jit(solution)/shard_map/ppermute | solution.py:78
  95.5 2.8 %collective-permute-done.15.d4 = bf16[4,256,128]{2,1,0:T(8,128)(2,1)S(1)} collective-permute-done((bf16[4,256,128]{2,1,0:T(8,128)(2,1)S(1)}, bf16[4,256,128]{2,1,0:T(8,128)(2,1)S(1)}, u32[]{:S(2)}, u32[]{:S(2)}) %collective-permute-start.15) | collective-permute-done | bytes 262176 | tf_op jit(solution)/shard_map/ppermute | solution.py:78
  98.7 1.8 %collective-permute-done.18.d7 = bf16[4,256,128]{2,1,0:T(8,128)(2,1)S(1)} collective-permute-done((bf16[4,256,128]{2,1,0:T(8,128)(2,1)S(1)}, bf16[4,256,128]{2,1,0:T(8,128)(2,1)S(1)}, u32[]{:S(2)}, u32[]{:S(2)}) %collective-permute-start.18) | collective-permute-done | bytes 262176 | tf_op jit(solution)/shard_map/ppermute | solution.py:78
  100.5 2.4 %collective-permute-start.19 = (bf16[1,256,128]{2,1,0:T(8,128)(2,1)S(1)}, bf16[1,256,128]{2,1,0:T(8,128)(2,1)S(1)}, u32[]{:S(2)}, u32[]{:S(2)}) collective-permute-start(bf16[1,256,128]{2,1,0:T(8,128)(2,1)S(1)} %slice.76), channel_id=1, source_target_pairs={{0,4},{1,5},{2,6},{3,7},{4,0},{5,1},{6,2},{7,3},{8,12},{9,13},{10,... | collective-permute-start | bytes 196616 | tf_op jit(solution)/shard_map/ppermute | solution.py:78
  102.9 1.2 collective-permute-start.20
  104.1 1.0 collective-permute-done.19.d5b
  105.1 3.3 %collective-permute-done.20.d5c = bf16[1,256,128]{2,1,0:T(8,128)(2,1)S(1)} collective-permute-done((bf16[1,256,128]{2,1,0:T(8,128)(2,1)S(1)}, bf16[1,256,128]{2,1,0:T(8,128)(2,1)S(1)}, u32[]{:S(2)}, u32[]{:S(2)}) %collective-permute-start.20) | collective-permute-done | bytes 65568 | tf_op jit(solution)/shard_map/ppermute | solution.py:78
  108.5 2.2 %copy-done.1 = bf16[32,256,256]{2,1,0:T(8,128)(2,1)S(1)} copy-done((bf16[32,256,256]{2,1,0:T(8,128)(2,1)S(1)}, bf16[32,256,256]{2,1,0:T(8,128)(2,1)}, u32[]{:S(2)}) %copy-start.1) | copy-done | bytes 4194328
  110.6 2.2 %copy-done.3 = bf16[32,256,256]{2,1,0:T(8,128)(2,1)S(1)} copy-done((bf16[32,256,256]{2,1,0:T(8,128)(2,1)S(1)}, bf16[32,256,256]{2,1,0:T(8,128)(2,1)}, u32[]{:S(2)}) %copy-start.3) | copy-done | bytes 4194328
  112.8 9.2 %shard_map.60 = (f32[1024,128]{1,0:T(8,128)S(1)}, bf16[1024,128]{1,0:T(8,128)(2,1)S(1)}) custom-call(s32[385]{0:T(512)S(1)} %pad_add_fusion.meta, bf16[4,256,128]{2,1,0:T(8,128)(2,1)S(1)} %bitcast.27, bf16[4,256,128]{2,1,0:T(8,128)(2,1)S(1)} %collective-permute-done.12.d1, bf16[4,256,128]{2,1,0:T(8,128)(2,1)S(1)} %collective-permute-done.13.d2, ...), custom_call_target="tpu_custom_call" | custom-call | tf_op jit(solution)/shard_map/pallas_call | solution.py:53
  122.1 1.5 collective-permute-done.21
  123.7 16.1 %all_to_all.27 = bf16[16,64,128]{2,1,0:T(8,128)(2,1)S(1)} all-to-all(bf16[16,64,128]{2,1,0:T(8,128)(2,1)S(1)} %bitcast.32), channel_id=1, replica_groups=mesh['op'=16,'qn'=16] {'op'}, dimensions={0} | all-to-all | bytes 524288 | tf_op jit(solution)/shard_map/all_to_all | solution.py:90
  139.8 0.8 broadcast_in_dim.7
  140.6 4.6 %all-to-all-start.3 = ((bf16[16,64,128]{2,1,0:T(8,128)(2,1)}), bf16[16,64,128]{2,1,0:T(8,128)(2,1)S(1)}, u32[]{:S(2)}, u32[]{:S(2)}) async-start(bf16[16,64,128]{2,1,0:T(8,128)(2,1)} %broadcast_in_dim.7), calls=%async_computation.3 | async-start | bytes 524288 | tf_op jit(solution)/shard_map/all_to_all | solution.py:92
  145.1 0.7 multiply_reduce_fusion.1
  145.9 10.7 %all-to-all-done.3 = bf16[16,64,128]{2,1,0:T(8,128)(2,1)S(1)} async-done(((bf16[16,64,128]{2,1,0:T(8,128)(2,1)}), bf16[16,64,128]{2,1,0:T(8,128)(2,1)S(1)}, u32[]{:S(2)}, u32[]{:S(2)}) %all-to-all-start.3) | async-done | bytes 262176 | tf_op jit(solution)/shard_map/all_to_all | solution.py:92
  156.6 1.0 multiply_reduce_fusion
  157.5 3.3 %stack.23 = f32[5]{0:T(128)S(1)} concatenate(f32[1]{0:T(128)} %bitcast, f32[1]{0:T(128)} %bitcast.4, f32[1]{0:T(128)} %bitcast.5, f32[1]{0:T(128)} %bitcast.8, f32[1]{0:T(128)} %bitcast.9), dimensions={0} | concatenate | bytes 40 | tf_op jit(solution)/shard_map/stack | solution.py:118
  161.5 3.5 %all-to-all-start.4 = ((f32[16,8,128]{2,1,0:T(8,128)}), f32[16,8,128]{2,1,0:T(8,128)S(1)}, u32[]{:S(2)}, u32[]{:S(2)}) async-start(f32[16,8,128]{2,1,0:T(8,128)} %broadcast_in_dim.8), calls=%async_computation.4 | async-start | bytes 131072 | tf_op jit(solution)/shard_map/all_to_all | solution.py:120
  165.0 6.0 %all-to-all-done.4 = f32[16,8,128]{2,1,0:T(8,128)S(1)} async-done(((f32[16,8,128]{2,1,0:T(8,128)}), f32[16,8,128]{2,1,0:T(8,128)S(1)}, u32[]{:S(2)}, u32[]{:S(2)}) %all-to-all-start.4) | async-done | bytes 65568 | tf_op jit(solution)/shard_map/all_to_all | solution.py:120
  171.1 0.7 fusion.11
  180.5 0.9 collective-permute-done.23
  181.4 0.8 maximum_select_fusion.2
  182.2 0.8 maximum_select_fusion.1
  (50 shorter events, 4.2 us)
Async XLA Ops:
  1.7 1.6 collective-permute-start
  3.4 8.4 %collective-permute-start.3 = (bf16[4,256,128]{2,1,0:T(8,128)(2,1)S(1)}, bf16[4,256,128]{2,1,0:T(8,128)(2,1)S(1)}, u32[]{:S(2)}, u32[]{:S(2)}) collective-permute-start(bf16[4,256,128]{2,1,0:T(8,128)(2,1)S(1)} %get-tuple-element.14.d0), channel_id=1, source_target_pairs={{0,4},{1,5},{2,6},{3,7},{4,0},{5,1},{6,2},{7,3},{8,12},{9,13},{10,... | collective-permute-start | bytes 786440 | tf_op jit(solution)/shard_map/ppermute | solution.py:78
  5.1 9.8 %collective-permute-start.2 = (bf16[4,256,128]{2,1,0:T(8,128)(2,1)S(1)}, bf16[4,256,128]{2,1,0:T(8,128)(2,1)S(1)}, u32[]{:S(2)}, u32[]{:S(2)}) collective-permute-start(bf16[4,256,128]{2,1,0:T(8,128)(2,1)S(1)} %get-tuple-element.14.d0), channel_id=1, source_target_pairs={{0,2},{1,3},{2,0},{3,1},{4,6},{5,7},{6,4},{7,5},{8,10},{9,11},{10,... | collective-permute-start | bytes 786440 | tf_op jit(solution)/shard_map/ppermute | solution.py:78
  6.6 9.5 %collective-permute-start.7 = (bf16[4,256,128]{2,1,0:T(8,128)(2,1)S(1)}, bf16[4,256,128]{2,1,0:T(8,128)(2,1)S(1)}, u32[]{:S(2)}, u32[]{:S(2)}) collective-permute-start(bf16[4,256,128]{2,1,0:T(8,128)(2,1)S(1)} %get-tuple-element.14.d0), channel_id=1, source_target_pairs={{0,12},{1,13},{2,14},{3,15},{4,8},{5,9},{6,10},{7,11},{8,4},{9,5},... | collective-permute-start | bytes 786440 | tf_op jit(solution)/shard_map/ppermute | solution.py:78
  11.8 9.3 %collective-permute-start.5 = (bf16[4,256,128]{2,1,0:T(8,128)(2,1)S(1)}, bf16[4,256,128]{2,1,0:T(8,128)(2,1)S(1)}, u32[]{:S(2)}, u32[]{:S(2)}) collective-permute-start(bf16[4,256,128]{2,1,0:T(8,128)(2,1)S(1)} %collective-permute-done.3.d2), channel_id=1, source_target_pairs={{0,12},{1,13},{2,14},{3,15},{4,8},{5,9},{6,10},{7,11},{8,4},{9,5},... | collective-permute-start | bytes 786440 | tf_op jit(solution)/shard_map/ppermute | solution.py:78
  14.9 8.5 %collective-permute-start.4 = (bf16[4,256,128]{2,1,0:T(8,128)(2,1)S(1)}, bf16[4,256,128]{2,1,0:T(8,128)(2,1)S(1)}, u32[]{:S(2)}, u32[]{:S(2)}) collective-permute-start(bf16[4,256,128]{2,1,0:T(8,128)(2,1)S(1)} %collective-permute-done.2.d1), channel_id=1, source_target_pairs={{0,4},{1,5},{2,6},{3,7},{4,0},{5,1},{6,2},{7,3},{8,12},{9,13},{10,... | collective-permute-start | bytes 786440 | tf_op jit(solution)/shard_map/ppermute | solution.py:78
  16.0 10.4 %collective-permute-start.8 = (bf16[4,256,128]{2,1,0:T(8,128)(2,1)S(1)}, bf16[4,256,128]{2,1,0:T(8,128)(2,1)S(1)}, u32[]{:S(2)}, u32[]{:S(2)}) collective-permute-start(bf16[4,256,128]{2,1,0:T(8,128)(2,1)S(1)} %collective-permute-done.7.d6), channel_id=1, source_target_pairs={{0,2},{1,3},{2,0},{3,1},{4,6},{5,7},{6,4},{7,5},{8,10},{9,11},{10,... | collective-permute-start | bytes 786440 | tf_op jit(solution)/shard_map/ppermute | solution.py:78
  16.5 5.7 %collective-permute-start.1 = (s32[32,2,3]{0,1,2:T(2,128)}, s32[32,2,3]{0,1,2:T(2,128)S(1)}, u32[]{:S(2)}, u32[]{:S(2)}) collective-permute-start(s32[32,2,3]{0,1,2:T(2,128)} %param.7), channel_id=1, source_target_pairs={{0,1},{1,0},{2,3},{3,2},{4,5},{5,4},{6,7},{7,6},{8,9},{9,8},{10,11... | collective-permute-start | bytes 2312 | tf_op jit(solution)/shard_map/ppermute | solution.py:78
  21.2 9.6 %collective-permute-start.6 = (bf16[2,256,128]{2,1,0:T(8,128)(2,1)S(1)}, bf16[2,256,128]{2,1,0:T(8,128)(2,1)S(1)}, u32[]{:S(2)}, u32[]{:S(2)}) collective-permute-start(bf16[2,256,128]{2,1,0:T(8,128)(2,1)S(1)} %slice.72), channel_id=1, source_target_pairs={{0,2},{1,3},{2,0},{3,1},{4,6},{5,7},{6,4},{7,5},{8,10},{9,11},{10,... | collective-permute-start | bytes 393224 | tf_op jit(solution)/shard_map/ppermute | solution.py:78
  23.4 5.6 %collective-permute-start.10 = (bf16[1,256,128]{2,1,0:T(8,128)(2,1)S(1)}, bf16[1,256,128]{2,1,0:T(8,128)(2,1)S(1)}, u32[]{:S(2)}, u32[]{:S(2)}) collective-permute-start(bf16[1,256,128]{2,1,0:T(8,128)(2,1)S(1)} %slice.74), channel_id=1, source_target_pairs={{0,12},{1,13},{2,14},{3,15},{4,8},{5,9},{6,10},{7,11},{8,4},{9,5},... | collective-permute-start | bytes 196616 | tf_op jit(solution)/shard_map/ppermute | solution.py:78
  26.4 4.4 %collective-permute-start.9 = (bf16[1,256,128]{2,1,0:T(8,128)(2,1)S(1)}, bf16[1,256,128]{2,1,0:T(8,128)(2,1)S(1)}, u32[]{:S(2)}, u32[]{:S(2)}) collective-permute-start(bf16[1,256,128]{2,1,0:T(8,128)(2,1)S(1)} %slice.73), channel_id=1, source_target_pairs={{0,4},{1,5},{2,6},{3,7},{4,0},{5,1},{6,2},{7,3},{8,12},{9,13},{10,... | collective-permute-start | bytes 196616 | tf_op jit(solution)/shard_map/ppermute | solution.py:78
  30.8 2.2 %copy-start = (bf16[32,256,256]{2,1,0:T(8,128)(2,1)S(1)}, bf16[32,256,256]{2,1,0:T(8,128)(2,1)}, u32[]{:S(2)}) copy-start(bf16[32,256,256]{2,1,0:T(8,128)(2,1)} %rb_ref.3) | copy-start | bytes 12582916
  33.0 2.2 %copy-start.2 = (bf16[32,256,256]{2,1,0:T(8,128)(2,1)S(1)}, bf16[32,256,256]{2,1,0:T(8,128)(2,1)}, u32[]{:S(2)}) copy-start(bf16[32,256,256]{2,1,0:T(8,128)(2,1)} %l_ref.3) | copy-start | bytes 12582916
  44.3 1.6 collective-permute-start.11
  84.4 6.4 %collective-permute-start.13 = (bf16[4,256,128]{2,1,0:T(8,128)(2,1)S(1)}, bf16[4,256,128]{2,1,0:T(8,128)(2,1)S(1)}, u32[]{:S(2)}, u32[]{:S(2)}) collective-permute-start(bf16[4,256,128]{2,1,0:T(8,128)(2,1)S(1)} %bitcast.24), channel_id=1, source_target_pairs={{0,4},{1,5},{2,6},{3,7},{4,0},{5,1},{6,2},{7,3},{8,12},{9,13},{10,... | collective-permute-start | bytes 786440 | tf_op jit(solution)/shard_map/ppermute | solution.py:78
  84.4 8.3 %collective-permute-start.17 = (bf16[4,256,128]{2,1,0:T(8,128)(2,1)S(1)}, bf16[4,256,128]{2,1,0:T(8,128)(2,1)S(1)}, u32[]{:S(2)}, u32[]{:S(2)}) collective-permute-start(bf16[4,256,128]{2,1,0:T(8,128)(2,1)S(1)} %bitcast.25), channel_id=1, source_target_pairs={{0,12},{1,13},{2,14},{3,15},{4,8},{5,9},{6,10},{7,11},{8,4},{9,5},... | collective-permute-start | bytes 786440 | tf_op jit(solution)/shard_map/ppermute | solution.py:78
  85.5 7.4 %collective-permute-start.12 = (bf16[4,256,128]{2,1,0:T(8,128)(2,1)S(1)}, bf16[4,256,128]{2,1,0:T(8,128)(2,1)S(1)}, u32[]{:S(2)}, u32[]{:S(2)}) collective-permute-start(bf16[4,256,128]{2,1,0:T(8,128)(2,1)S(1)} %bitcast.26), channel_id=1, source_target_pairs={{0,2},{1,3},{2,0},{3,1},{4,6},{5,7},{6,4},{7,5},{8,10},{9,11},{10,... | collective-permute-start | bytes 786440 | tf_op jit(solution)/shard_map/ppermute | solution.py:78
  90.7 7.6 %collective-permute-start.15 = (bf16[4,256,128]{2,1,0:T(8,128)(2,1)S(1)}, bf16[4,256,128]{2,1,0:T(8,128)(2,1)S(1)}, u32[]{:S(2)}, u32[]{:S(2)}) collective-permute-start(bf16[4,256,128]{2,1,0:T(8,128)(2,1)S(1)} %collective-permute-done.13.d2), channel_id=1, source_target_pairs={{0,12},{1,13},{2,14},{3,15},{4,8},{5,9},{6,10},{7,11},{8,4},{9,5},... | collective-permute-start | bytes 786440 | tf_op jit(solution)/shard_map/ppermute | solution.py:78
  92.7 7.8 %collective-permute-start.18 = (bf16[4,256,128]{2,1,0:T(8,128)(2,1)S(1)}, bf16[4,256,128]{2,1,0:T(8,128)(2,1)S(1)}, u32[]{:S(2)}, u32[]{:S(2)}) collective-permute-start(bf16[4,256,128]{2,1,0:T(8,128)(2,1)S(1)} %collective-permute-done.17.d6), channel_id=1, source_target_pairs={{0,2},{1,3},{2,0},{3,1},{4,6},{5,7},{6,4},{7,5},{8,10},{9,11},{10,... | collective-permute-start | bytes 786440 | tf_op jit(solution)/shard_map/ppermute | solution.py:78
  92.9 10.0 %collective-permute-start.14 = (bf16[4,256,128]{2,1,0:T(8,128)(2,1)S(1)}, bf16[4,256,128]{2,1,0:T(8,128)(2,1)S(1)}, u32[]{:S(2)}, u32[]{:S(2)}) collective-permute-start(bf16[4,256,128]{2,1,0:T(8,128)(2,1)S(1)} %collective-permute-done.12.d1), channel_id=1, source_target_pairs={{0,4},{1,5},{2,6},{3,7},{4,0},{5,1},{6,2},{7,3},{8,12},{9,13},{10,... | collective-permute-start | bytes 786440 | tf_op jit(solution)/shard_map/ppermute | solution.py:78
  98.3 10.1 %collective-permute-start.16 = (bf16[2,256,128]{2,1,0:T(8,128)(2,1)S(1)}, bf16[2,256,128]{2,1,0:T(8,128)(2,1)S(1)}, u32[]{:S(2)}, u32[]{:S(2)}) collective-permute-start(bf16[2,256,128]{2,1,0:T(8,128)(2,1)S(1)} %slice.75), channel_id=1, source_target_pairs={{0,2},{1,3},{2,0},{3,1},{4,6},{5,7},{6,4},{7,5},{8,10},{9,11},{10,... | collective-permute-start | bytes 393224 | tf_op jit(solution)/shard_map/ppermute | solution.py:78
  100.5 4.6 %collective-permute-start.19 = (bf16[1,256,128]{2,1,0:T(8,128)(2,1)S(1)}, bf16[1,256,128]{2,1,0:T(8,128)(2,1)S(1)}, u32[]{:S(2)}, u32[]{:S(2)}) collective-permute-start(bf16[1,256,128]{2,1,0:T(8,128)(2,1)S(1)} %slice.76), channel_id=1, source_target_pairs={{0,4},{1,5},{2,6},{3,7},{4,0},{5,1},{6,2},{7,3},{8,12},{9,13},{10,... | collective-permute-start | bytes 196616 | tf_op jit(solution)/shard_map/ppermute | solution.py:78
  102.9 5.6 %collective-permute-start.20 = (bf16[1,256,128]{2,1,0:T(8,128)(2,1)S(1)}, bf16[1,256,128]{2,1,0:T(8,128)(2,1)S(1)}, u32[]{:S(2)}, u32[]{:S(2)}) collective-permute-start(bf16[1,256,128]{2,1,0:T(8,128)(2,1)S(1)} %slice.77), channel_id=1, source_target_pairs={{0,12},{1,13},{2,14},{3,15},{4,8},{5,9},{6,10},{7,11},{8,4},{9,5},... | collective-permute-start | bytes 196616 | tf_op jit(solution)/shard_map/ppermute | solution.py:78
  108.5 2.2 %copy-start.1 = (bf16[32,256,256]{2,1,0:T(8,128)(2,1)S(1)}, bf16[32,256,256]{2,1,0:T(8,128)(2,1)}, u32[]{:S(2)}) copy-start(bf16[32,256,256]{2,1,0:T(8,128)(2,1)} %rb_ref.3) | copy-start | bytes 12582916
  110.6 2.2 %copy-start.3 = (bf16[32,256,256]{2,1,0:T(8,128)(2,1)S(1)}, bf16[32,256,256]{2,1,0:T(8,128)(2,1)}, u32[]{:S(2)}) copy-start(bf16[32,256,256]{2,1,0:T(8,128)(2,1)} %l_ref.3) | copy-start | bytes 12582916
  122.0 1.6 collective-permute-start.21
  140.6 16.0 %all-to-all-start.3 = ((bf16[16,64,128]{2,1,0:T(8,128)(2,1)}), bf16[16,64,128]{2,1,0:T(8,128)(2,1)S(1)}, u32[]{:S(2)}, u32[]{:S(2)}) async-start(bf16[16,64,128]{2,1,0:T(8,128)(2,1)} %broadcast_in_dim.7), calls=%async_computation.3 | async-start | bytes 524288 | tf_op jit(solution)/shard_map/all_to_all | solution.py:92
  161.5 9.6 %all-to-all-start.4 = ((f32[16,8,128]{2,1,0:T(8,128)}), f32[16,8,128]{2,1,0:T(8,128)S(1)}, u32[]{:S(2)}, u32[]{:S(2)}) async-start(f32[16,8,128]{2,1,0:T(8,128)} %broadcast_in_dim.8), calls=%async_computation.4 | async-start | bytes 131072 | tf_op jit(solution)/shard_map/all_to_all | solution.py:120
  179.8 1.6 collective-permute-start.23
  180.0 2.3 %collective-permute-start.22 = (f32[2,256,128]{2,1,0:T(8,128)S(1)}, f32[2,256,128]{2,1,0:T(8,128)S(1)}, u32[]{:S(2)}, u32[]{:S(2)}) collective-permute-start(f32[2,256,128]{2,1,0:T(8,128)S(1)} %get-tuple-element.21), channel_id=1, source_target_pairs={{0,1},{1,0},{2,3},{3,2},{4,5},{5,4},{6,7},{7,6},{8,9},{9,8},{10,11... | collective-permute-start | bytes 786440 | tf_op jit(solution)/shard_map/ppermute | solution.py:78

commit v2 on v0

v2 whole, which is shorter than its diff:
```python
import functools

import jax
import jax.numpy as jnp
from jax import lax
from jax.experimental import pallas as pl
from jax.experimental.pallas import tpu as pltpu
from jax.sharding import PartitionSpec as P

epsilon = 1e-06
BF, F32 = jnp.bfloat16, jnp.float32
GROUP = 8
HALF = 128
VMEM = pl.BlockSpec(memory_space=pltpu.VMEM)
SMEM = pl.BlockSpec(memory_space=pltpu.SMEM)
HBM = pl.BlockSpec(memory_space=pl.ANY)
PARAMS = pltpu.CompilerParams(vmem_limit_bytes=40 * 1024 * 1024)


def prepare_kernel(core_ref, r_ref, right, r_half, sems):
    core = core_ref[0]
    ops = r_ref.shape[0]
    mine = pl.ds(pl.multiple_of(core * HALF, HALF), HALF)
    others = pl.ds(pl.multiple_of((1 - core) * HALF, HALF), HALF)
    r_copies = [
        pltpu.make_async_copy(
            r_ref.at[pl.ds(GROUP * i, GROUP), :, mine], r_half.at[pl.ds(GROUP * i, GROUP)], sems.at[i]
        )
        for i in range(ops // GROUP)
    ]
    for copy in r_copies:
        copy.start()
    for i in range(ops):
        if i % GROUP == 0:
            r_copies[i // GROUP].wait()
        right[HALF * i : HALF * (i + 1), :HALF] = r_half[i, mine, :].T
        right[HALF * i : HALF * (i + 1), HALF:] = r_half[i, others, :].T


def prepare(core, right_ops):
    ops = right_ops.shape[0]
    return pl.pallas_call(
        prepare_kernel,
        in_specs=[SMEM, HBM],
        out_specs=VMEM,
        out_shape=jax.ShapeDtypeStruct((ops * HALF, 256), BF),
        scratch_shapes=[pltpu.VMEM((ops, 256, HALF), BF), pltpu.SemaphoreType.DMA((ops // GROUP,))],
        compiler_params=PARAMS,
        cost_estimate=pl.CostEstimate(flops=0, bytes_accessed=8 * 1024 * 1024, transcendentals=0),
    )(core, right_ops)


def ham_kernel(by_block, meta, core_ref, d0, d1, d2, d3, d4, d5a, d5b, d5c, d6, d7, left, right, mine, other, v, lefted, acc):
    for slot, piece in enumerate((d0, d1, d2, d3, d4, None, d6, d7)):
        if piece is not None:
            v[4 * slot : 4 * slot + 4] = piece[...]
    v[20:22] = d5a[...]
    v[22:23] = d5b[...]
    v[23:24] = d5c[...]
    for step in range(left.shape[0] // GROUP):
        for i in range(GROUP):
            k = step * GROUP + i
            sums = []
            for b in range(4):
                at = (k * 4 + b) * 3
                total = v[meta[at]].astype(F32) + v[meta[at + 1]].astype(F32) + v[meta[at + 2]].astype(F32)
                sums.append(total.astype(BF))
            product = jnp.dot(left[k], jnp.concatenate(sums, axis=1), preferred_element_type=F32).astype(BF)
            for b in range(4):
                lefted[256 * b : 256 * (b + 1), HALF * i : HALF * (i + 1)] = product[:, HALF * b : HALF * (b + 1)]
        rows = right[GROUP * HALF * step : GROUP * HALF * (step + 1), :]
        term = jnp.dot(lefted[...], rows, preferred_element_type=F32)
        if step == 0:
            acc[...] = term
        else:
            acc[...] += term
    if by_block:
        core = core_ref[0]
        here = pl.ds(pl.multiple_of(core * HALF, HALF), HALF)
        there = pl.ds(pl.multiple_of((1 - core) * HALF, HALF), HALF)
        mine[:, here] = acc[:512, :HALF]
        mine[:, there] = acc[:512, HALF:]
        other[:, here] = acc[512:, :HALF]
        other[:, there] = acc[512:, HALF:]
    else:
        mine[...] = acc[:, :HALF]
        other[...] = acc[:, HALF:]


def apply_ham(by_block, meta, core, pieces, left, right):
    shape = (512, 256) if by_block else (1024, HALF)
    return pl.pallas_call(
        functools.partial(ham_kernel, by_block),
        in_specs=[SMEM, SMEM] + [VMEM] * (len(pieces) + 2),
        out_specs=[VMEM, VMEM],
        out_shape=[jax.ShapeDtypeStruct(shape, F32)] * 2,
        scratch_shapes=[
            pltpu.VMEM((32, 256, HALF), BF),
            pltpu.VMEM((1024, GROUP * HALF), BF),
            pltpu.VMEM((1024, 256), F32),
        ],
        compiler_params=PARAMS,
    )(meta, core, *pieces, left, right)


def dots_kernel(p, u, out):
    x, y = p[...], u[...].astype(F32)
    lane = lax.broadcasted_iota(jnp.int32, (8, 128), 1)
    rows = jnp.where(lane == 0, jnp.sum(x * x), 0.0)
    rows = jnp.where(lane == 1, jnp.sum(x * y), rows)
    out[...] = jnp.where(lane == 2, jnp.sum(y * y), rows)


def dots(p, u):
    return pl.pallas_call(
        dots_kernel, in_specs=[VMEM, VMEM], out_specs=VMEM, out_shape=jax.ShapeDtypeStruct((8, 128), F32)
    )(p, u)


def pack_kernel(mine, got, p, u, out):
    total = mine[...] + got[...]
    for i in range(16):
        out[i, :32] = total[32 * i : 32 * (i + 1)].astype(BF)
    lane = lax.broadcasted_iota(jnp.int32, (16, 256), 1)
    rows = jnp.zeros((16, 256), F32)
    for at, field in enumerate((p[...], u[...].astype(F32))):
        rest = jnp.full((16, 256), jnp.sum(field.reshape(512, 256) * total))
        for part in range(3):
            term = rest.astype(BF).astype(F32)
            rows = jnp.where(lane == 3 * at + part, term, rows)
            rest = rest - term
    rows = rows.astype(BF)
    for i in range(16):
        out[i, 32:] = rows


def pack(mine, got, p, u):
    return pl.pallas_call(
        pack_kernel, in_specs=[VMEM] * 4, out_specs=VMEM, out_shape=jax.ShapeDtypeStruct((16, 48, 256), BF)
    )(mine, got, p, u)


def unpack_kernel(parts, early, piece, scalars):
    total = parts[0, :32].astype(F32)
    rows = parts[0, 32:].astype(F32)
    for i in range(1, 16):
        total += parts[i, :32].astype(F32)
        rows += parts[i, 32:].astype(F32)
    total = total.astype(BF)
    lane = lax.broadcasted_iota(jnp.int32, (16, 256), 1)
    first_row = lax.broadcasted_iota(jnp.int32, (16, 256), 0) == 0
    pw = jnp.sum(jnp.where(first_row & (lane < 3), rows, 0.0))
    uw = jnp.sum(jnp.where(first_row & (lane >= 3), rows, 0.0))
    lane = lax.broadcasted_iota(jnp.int32, (8, 128), 1)
    out = jnp.where(lane == 3, pw, jnp.where(lane == 4, uw, early[...]))
    for i in range(16):
        piece[i] = total
        scalars[i] = out


def unpack(parts, early):
    return pl.pallas_call(
        unpack_kernel,
        in_specs=[VMEM] * 2,
        out_specs=[VMEM] * 2,
        out_shape=[jax.ShapeDtypeStruct((16, 32, 256), BF), jax.ShapeDtypeStruct((16, 8, 128), F32)],
    )(parts, early)


def finish_kernel(count, scalars, p_ref, u_ref, w_ref, ritz_ref, residual_ref):
    total = scalars[0]
    for i in range(1, 16):
        total += scalars[i]
    lane = lax.broadcasted_iota(jnp.int32, (8, 128), 1)
    row = lax.broadcasted_iota(jnp.int32, (8, 128), 0)
    pp, pu, uu, pw, uw = (
        jnp.full((1, 256), jnp.sum(jnp.where((lane == i) & (row == 0), total, 0.0)) / count) for i in range(5)
    )
    s = lax.rsqrt(pp + epsilon)
    energy = s * s * pu
    t = lax.rsqrt(s * s * (uu - 2.0 * energy * pu + energy * energy * pp) + epsilon)
    ts = t * s
    diag_d = ts * ts * (uw - energy * (uu + pw) + energy * energy * pu)
    coupling = 0.5 * ts * s * ((pw - energy * pu) + (uu - energy * pu))
    gap = energy - diag_d
    theta = 0.5 * (energy + diag_d) - jnp.sqrt(0.25 * gap * gap + coupling * coupling)
    one, two = (diag_d - theta) * s, coupling * ts
    p, u, w = p_ref[0], u_ref[0].astype(F32), w_ref[0].astype(F32)
    ritz = one * p - two * (u - energy * p)
    ritz_ref[0] = ritz
    residual_ref[0] = one * u - two * (w - energy * u) - theta * ritz


def finish(count, scalars, p, u, w):
    block = pl.BlockSpec((1, 256, 256), lambda i: (i, 0, 0))
    return pl.pallas_call(
        functools.partial(finish_kernel, count),
        grid=(p.shape[0],),
        in_specs=[pl.BlockSpec((16, 8, 128), lambda i: (0, 0, 0)), block, block, block],
        out_specs=[block, block],
        out_shape=[jax.ShapeDtypeStruct(p.shape, F32)] * 2,
    )(scalars, p, u, w)


def swap(x, bits):
    return lax.ppermute(x, "qn", [(i, i ^ bits) for i in range(16)])


def gather_chips(own):
    x1, y1, y3 = swap(own, 2), swap(own, 4), swap(own, 12)
    x1y1, y2, x1y3 = swap(x1, 4), swap(y1, 12), swap(y3, 2)
    far = swap(y2[:2], 2), swap(x1y3[2:3], 4), swap(x1y1[3:], 12)
    return (own, x1, y1, x1y1, y2) + far + (y3, x1y3)


def op_exchange(x):
    return lax.all_to_all(x, "op", 0, 0, tiled=True)


def shards(psi_start, left_ops, right_ops, sources):
    place = lax.axis_index("qn")
    core = place % 2
    chip = place // 2
    count = 32.0 * 256.0 * 256.0

    def pick(a, b):
        return jnp.where(core == 0, a, b)

    def in_order(a, b, axis=0):
        return pick(jnp.concatenate([a, b], axis), jnp.concatenate([b, a], axis))

    low, high = psi_start[:, :, :HALF].astype(BF), psi_start[:, :, HALF:].astype(BF)
    own = in_order(pick(low, high), swap(pick(high, low), 1))
    theirs = swap(sources, 1)
    where = chip * 4
    by_chip = (in_order(sources, theirs, 1) ^ where).reshape(-1)
    own_first = (jnp.concatenate([sources, theirs], 1) ^ where).reshape(-1)
    core = core.reshape(1)

    pieces = gather_chips(own)
    right = prepare(core, right_ops)
    mine, other = apply_ham(False, by_chip, core, pieces, left_ops, right)
    parts = op_exchange((mine + swap(other, 1)).astype(BF).reshape(16, 64, HALF))
    piece = jnp.sum(parts.astype(F32), axis=0).astype(BF)
    u_half = op_exchange(jnp.broadcast_to(piece[None], (16, 64, HALF))).reshape(4, 256, HALF)

    pieces = gather_chips(u_half)
    low, high = u_half[:2], u_half[2:]
    core0 = core[0] == 0
    kept, got = jnp.where(core0, low, high), swap(jnp.where(core0, high, low), 1)
    u = jnp.where(core0, jnp.concatenate([kept, got], 2), jnp.concatenate([got, kept], 2))
    early = dots(psi_start, u)
    pieces, u, early = lax.optimization_barrier((pieces, u, early))
    mine, other = apply_ham(True, own_first, core, pieces, left_ops, right)
    piece, scalars = unpack(op_exchange(pack(mine, swap(other, 1), psi_start, u)), early)
    scalars = lax.all_to_all(scalars, "qn", 0, 0, tiled=True)
    w = op_exchange(piece).reshape(2, 256, 256)
    return tuple(finish(count, scalars, psi_start, u, w))


def solution(mesh):
    in_specs = (P("qn", None, None), P("op", None, None), P("op", None, None), P("op", "qn", None))
    out_specs = (P("qn", None, None), P("qn", None, None))
    return jax.shard_map(shards, mesh=mesh, in_specs=in_specs, out_specs=out_specs, check_vma=False)
```

time: 582 us -> 179 us (0.31)
  waiting for transfers between devices: 386 us -> 22.3 us
  matrix products: 46 us -> 0 us
  blocking collectives: 115 us -> 85.4 us
  starting transfers between devices: 0.34 us -> 24.2 us
  Pallas kernels: 0 us -> 23.6 us
  between operations: 19.8 us -> 0.79 us
  local copies, waits for them, and re-layouts: 0.7 us -> 17.2 us
  other arithmetic: 12 us -> 4.43 us
    psum x2 -> x0, waiting for transfers between devices: 312 us -> none  [project(): return lax.psum(partial_terms, 'op')]
    psum x4 -> x0, blocking collectives: 115 us -> none  [the longest x3 83.5 us: totals(): return lax.psum(values, 'qn')]
    all_to_all x0 -> x5, blocking collectives: none -> 85.4 us  [the longest x4 75.1 us: op_exchange(): return lax.all_to_all(x, 'op', 0, 0, tiled=True)]
    all_gather x2 -> x0, waiting for transfers between devices: 74.5 us -> none  [the longest x1 38.9 us: shards(): lax.all_gather(first.astype(jnp.bfloat16), 'qn', axis=0, tiled=True)]
    dot_general x4 -> x0, matrix products: 46 us -> none  [the longest x2 29.3 us: project(): jnp.einsum('kbxy,kzy->bxz', lefted, right_ops, preferred_element_type=jnp...]
    ppermute x0 -> x23, starting transfers between devices: none -> 24.2 us  [swap(): return lax.ppermute(x, 'qn', [(i, i ^ bits) for i in range(16)])]
    pallas_call x0 -> x7, Pallas kernels: none -> 23.6 us  [the longest x2 13.6 us: apply_ham(): pl.pallas_call(functools.partial(ham_kernel, by_block), in_specs=[SMEM, S...]
    ppermute x0 -> x23, waiting for transfers between devices: none -> 22.3 us  [swap(): return lax.ppermute(x, 'qn', [(i, i ^ bits) for i in range(16)])]
  transfers between devices with their start and end apart: 4 -> 23, of which waited for: 4 -> 9; matrix products, arithmetic and copies ran while one was open for 0% -> 6% of each run, Pallas kernels for 0% -> 2%
where the time goes in v2:
time: 179 us; the launch traced here: 178 us
  blocking collectives  85.4 us (48%)
  starting transfers between devices  24.2 us (14%)
  Pallas kernels  23.6 us (13%)
  waiting for transfers between devices  22.3 us (12%)
  local copies, waits for them, and re-layouts  17.2 us (10%)
  other arithmetic  4.43 us (2%)
    all_to_all x4, blocking collectives, op_exchange(): return lax.all_to_all(x, 'op', 0, 0, tiled=True)  75.1 us
    ppermute x23, starting transfers between devices, swap(): return lax.ppermute(x, 'qn', [(i, i ^ bits) for i in range(16)])  24.2 us
    ppermute x23, waiting for transfers between devices, swap(): return lax.ppermute(x, 'qn', [(i, i ^ bits) for i in range(16)])  22.3 us
    pallas_call x2, Pallas kernels, apply_ham(): pl.pallas_call(functools.partial(ham_kernel, by_block), in_specs=[SMEM, S...  13.6 us
    all_to_all x1, blocking collectives, shards(): scalars = lax.all_to_all(scalars, 'qn', 0, 0, tiled=True)  10.3 us
    unnamed x16, local copies, waits for them, and re-layouts  9.1 us
    slice x6, local copies, waits for them, and re-layouts, gather_chips(): far = (swap(y2[:2], 2), swap(x1y3[2:3], 4), swap(x1y1[3:], 12))  3.84 us
  transfers between devices with their start and end apart: 23, of which 9 were waited for; matrix products, arithmetic and copies ran while one was open for 6% of the time, Pallas kernels for 2%

profile of v2, /device:TPU:32, one launch (start us, length us, event | category | flops | bytes accessed | tf_op | source)
XLA Modules:
  0.0 178.0 jit_solution(953211771698773550)
XLA Ops:
  0.7 1.1 convert.5
  1.9 1.3 collective-permute-done.1
  3.2 1.7 collective-permute-start.3
  4.9 2.2 %collective-permute-start.7 = (bf16[4,256,128]{2,1,0:T(8,128)(2,1)S(1)}, bf16[4,256,128]{2,1,0:T(8,128)(2,1)}, u32[]{:S(2)}, u32[]{:S(2)}) collective-permute-start(bf16[4,256,128]{2,1,0:T(8,128)(2,1)S(1)} %maximum_select_fusion.d0), channel_id=1, source_target_pairs={{0,12},{1,13},{2,14},{3,15},{4,8},{5,9},{6,10},{7,11},{8,4},{9,5},... | collective-permute-start | bytes 786440 | tf_op jit(solution)/shard_map/ppermute | solution.py:206
  7.1 1.5 collective-permute-start.2
  8.6 3.1 %collective-permute-done.3.d2 = bf16[4,256,128]{2,1,0:T(8,128)(2,1)S(1)} collective-permute-done((bf16[4,256,128]{2,1,0:T(8,128)(2,1)S(1)}, bf16[4,256,128]{2,1,0:T(8,128)(2,1)S(1)}, u32[]{:S(2)}, u32[]{:S(2)}) %collective-permute-start.3) | collective-permute-done | bytes 262176 | tf_op jit(solution)/shard_map/ppermute | solution.py:206
  11.7 3.0 %collective-permute-start.5 = (bf16[4,256,128]{2,1,0:T(8,128)(2,1)S(1)}, bf16[4,256,128]{2,1,0:T(8,128)(2,1)S(1)}, u32[]{:S(2)}, u32[]{:S(2)}) collective-permute-start(bf16[4,256,128]{2,1,0:T(8,128)(2,1)S(1)} %collective-permute-done.3.d2), channel_id=1, source_target_pairs={{0,12},{1,13},{2,14},{3,15},{4,8},{5,9},{6,10},{7,11},{8,4},{9,5},... | collective-permute-start | bytes 786440 | tf_op jit(solution)/shard_map/ppermute | solution.py:206
  14.7 1.5 collective-permute-start.8
  16.3 4.3 %collective-permute-done.5.d4 = bf16[4,256,128]{2,1,0:T(8,128)(2,1)S(1)} collective-permute-done((bf16[4,256,128]{2,1,0:T(8,128)(2,1)S(1)}, bf16[4,256,128]{2,1,0:T(8,128)(2,1)S(1)}, u32[]{:S(2)}, u32[]{:S(2)}) %collective-permute-start.5) | collective-permute-done | bytes 262176 | tf_op jit(solution)/shard_map/ppermute | solution.py:206
  20.6 0.7 slice.46
  21.2 1.5 collective-permute-start.6
  22.7 2.2 %copy-done.2 = bf16[32,256,256]{2,1,0:T(8,128)(2,1)S(1)} copy-done((bf16[32,256,256]{2,1,0:T(8,128)(2,1)S(1)}, bf16[32,256,256]{2,1,0:T(8,128)(2,1)}, u32[]{:S(2)}) %copy-start.2) | copy-done | bytes 4194328
  24.9 1.2 shard_map.59.right
  26.1 0.6 slice.47
  27.7 2.7 %collective-permute-start.10 = (bf16[1,256,128]{2,1,0:T(8,128)(2,1)}, bf16[1,256,128]{2,1,0:T(8,128)(2,1)}, u32[]{:S(2)}, u32[]{:S(2)}) collective-permute-start(bf16[1,256,128]{2,1,0:T(8,128)(2,1)} %slice.48), channel_id=1, source_target_pairs={{0,12},{1,13},{2,14},{3,15},{4,8},{5,9},{6,10},{7,11},{8,4},{9,5},... | collective-permute-start | bytes 196616 | tf_op jit(solution)/shard_map/ppermute | solution.py:206
  30.9 1.4 copy.7
  32.4 1.1 xor.22.meta
  33.5 2.2 %copy-done = bf16[32,256,256]{2,1,0:T(8,128)(2,1)S(1)} copy-done((bf16[32,256,256]{2,1,0:T(8,128)(2,1)S(1)}, bf16[32,256,256]{2,1,0:T(8,128)(2,1)}, u32[]{:S(2)}) %copy-start) | copy-done | bytes 4194328
  35.7 6.8 %shard_map.60 = (f32[1024,128]{1,0:T(8,128)S(1)}, f32[1024,128]{1,0:T(8,128)S(1)}) custom-call(s32[384]{0:T(512)S(1)} %xor.22.meta, s32[1]{0:T(128)} %bitcast.core_ref, bf16[4,256,128]{2,1,0:T(8,128)(2,1)S(1)} %maximum_select_fusion.d0, bf16[4,256,128]{2,1,0:T(8,128)(2,1)} %collective-permute-done.2.d1, bf16[4,256,128]{2,1,0:T(8,128)(2,1)S(1)} %collective-permute-done.3.d2, ...), custom_call_target="tpu_custom_call" | custom-call | tf_op jit(solution)/shard_map/pallas_call | solution.py:92
  42.8 1.7 collective-permute-done.11
  44.6 22.5 %all_to_all.25 = bf16[16,64,128]{2,1,0:T(8,128)(2,1)S(1)} all-to-all(bf16[16,64,128]{2,1,0:T(8,128)(2,1)S(1)} %bitcast.11), channel_id=1, replica_groups=mesh['op'=16,'qn'=16] {'op'}, dimensions={0} | all-to-all | bytes 524288 | tf_op jit(solution)/shard_map/all_to_all | solution.py:217
  67.2 15.8 %all_to_all.26 = bf16[16,64,128]{2,1,0:T(8,128)(2,1)S(1)} all-to-all(bf16[16,64,128]{2,1,0:T(8,128)(2,1)S(1)} %broadcast_in_dim.2), channel_id=1, replica_groups=mesh['op'=16,'qn'=16] {'op'}, dimensions={0} | all-to-all | bytes 524288 | tf_op jit(solution)/shard_map/all_to_all | solution.py:217
  83.0 2.8 %collective-permute-start.17 = (bf16[4,256,128]{2,1,0:T(8,128)(2,1)S(1)}, bf16[4,256,128]{2,1,0:T(8,128)(2,1)S(1)}, u32[]{:S(2)}, u32[]{:S(2)}) collective-permute-start(bf16[4,256,128]{2,1,0:T(8,128)(2,1)S(1)} %bitcast.6), channel_id=1, source_target_pairs={{0,12},{1,13},{2,14},{3,15},{4,8},{5,9},{6,10},{7,11},{8,4},{9,5},... | collective-permute-start | bytes 786440 | tf_op jit(solution)/shard_map/ppermute | solution.py:206
  86.0 4.5 %collective-permute-done.17.d6 = bf16[4,256,128]{2,1,0:T(8,128)(2,1)S(1)} collective-permute-done((bf16[4,256,128]{2,1,0:T(8,128)(2,1)S(1)}, bf16[4,256,128]{2,1,0:T(8,128)(2,1)S(1)}, u32[]{:S(2)}, u32[]{:S(2)}) %collective-permute-start.17) | collective-permute-done | bytes 262176 | tf_op jit(solution)/shard_map/ppermute | solution.py:206
  90.8 1.4 collective-permute-done.13.d2
  92.2 1.4 collective-permute-start.15
  93.6 1.2 collective-permute-done.12.d1
  94.8 1.4 collective-permute-start.14
  96.2 0.7 broadcast_select_fusion.1
  96.9 2.9 %collective-permute-done.15.d4 = bf16[4,256,128]{2,1,0:T(8,128)(2,1)S(1)} collective-permute-done((bf16[4,256,128]{2,1,0:T(8,128)(2,1)S(1)}, bf16[4,256,128]{2,1,0:T(8,128)(2,1)S(1)}, u32[]{:S(2)}, u32[]{:S(2)}) %collective-permute-start.15) | collective-permute-done | bytes 262176 | tf_op jit(solution)/shard_map/ppermute | solution.py:206
  99.8 0.7 slice.49
  100.8 0.7 copy.6
  101.6 1.1 xor.20.meta
  103.9 2.8 %collective-permute-start.20 = (bf16[1,256,128]{2,1,0:T(8,128)(2,1)}, bf16[1,256,128]{2,1,0:T(8,128)(2,1)}, u32[]{:S(2)}, u32[]{:S(2)}) collective-permute-start(bf16[1,256,128]{2,1,0:T(8,128)(2,1)} %slice.51), channel_id=1, source_target_pairs={{0,12},{1,13},{2,14},{3,15},{4,8},{5,9},{6,10},{7,11},{8,4},{9,5},... | collective-permute-start | bytes 196616 | tf_op jit(solution)/shard_map/ppermute | solution.py:206
  106.7 1.9 %maximum_select_fusion.1.u.u_ref = bf16[2,256,256]{2,1,0:T(8,128)(2,1)} fusion(bf16[2,256,128]{2,1,0:T(8,128)(2,1)} %collective-permute-done.21, bf16[2,256,128]{2,1,0:T(8,128)(2,1)} %bitcast.12, pred[]{:T(512)S(6)} %eq.4), kind=kLoop, calls=%fused_computation.2 | loop fusion | flops 1179648 | bytes 524289 | tf_op jit(solution)/shard_map/jit(_where)/select_n | solution.py:251
  108.6 2.0 %shard_map.61.early = f32[8,128]{1,0:T(8,128)} custom-call(f32[2,256,256]{2,1,0:T(8,128)} %p_ref.1, bf16[2,256,256]{2,1,0:T(8,128)(2,1)} %maximum_select_fusion.1.u.u_ref), custom_call_target="tpu_custom_call" | custom-call | tf_op jit(solution)/shard_map/pallas_call | solution.py:115
  110.6 2.2 %copy-done.1 = bf16[32,256,256]{2,1,0:T(8,128)(2,1)S(1)} copy-done((bf16[32,256,256]{2,1,0:T(8,128)(2,1)S(1)}, bf16[32,256,256]{2,1,0:T(8,128)(2,1)}, u32[]{:S(2)}) %copy-start.1) | copy-done | bytes 4194328
  112.8 0.9 copy-done.5
  113.8 6.8 %shard_map.62 = (f32[512,256]{1,0:T(8,128)S(1)}, f32[512,256]{1,0:T(8,128)S(1)}) custom-call(s32[384]{0:T(512)S(1)} %xor.20.meta, s32[1]{0:T(128)} %bitcast.core_ref, bf16[4,256,128]{2,1,0:T(8,128)(2,1)S(1)} %bitcast.9, bf16[4,256,128]{2,1,0:T(8,128)(2,1)} %collective-permute-done.12.d1, bf16[4,256,128]{2,1,0:T(8,128)(2,1)S(1)} %copy-done.5, ...), custom_call_target="tpu_custom_call" | custom-call | tf_op jit(solution)/shard_map/pallas_call | solution.py:92
  120.6 0.8 copy-done.3
  121.3 1.9 %collective-permute-done.22.got = f32[512,256]{1,0:T(8,128)S(1)} collective-permute-done((f32[512,256]{1,0:T(8,128)S(1)}, f32[512,256]{1,0:T(8,128)S(1)}, u32[]{:S(2)}, u32[]{:S(2)}) %collective-permute-start.22) | collective-permute-done | bytes 524320 | tf_op jit(solution)/shard_map/ppermute | solution.py:206
  123.3 0.8 copy-done.6
  124.0 2.5 %shard_map.63 = bf16[16,48,256]{2,1,0:T(8,128)(2,1)} custom-call(f32[512,256]{1,0:T(8,128)} %copy-done.3, f32[512,256]{1,0:T(8,128)} %copy-done.6, f32[2,256,256]{2,1,0:T(8,128)} %p_ref.1, bf16[2,256,256]{2,1,0:T(8,128)(2,1)} %maximum_select_fusion.1.u.u_ref), custom_call_target="tpu_custom_call" | custom-call | tf_op jit(solution)/shard_map/pallas_call | solution.py:138
  126.5 19.9 %all_to_all.27.parts = bf16[16,48,256]{2,1,0:T(8,128)(2,1)} all-to-all(bf16[16,48,256]{2,1,0:T(8,128)(2,1)} %shard_map.63), channel_id=1, replica_groups=mesh['op'=16,'qn'=16] {'op'}, dimensions={0} | all-to-all | bytes 786432 | tf_op jit(solution)/shard_map/all_to_all | solution.py:217
  146.5 1.8 %shard_map.64 = (bf16[16,32,256]{2,1,0:T(8,128)(2,1)}, f32[16,8,128]{2,1,0:T(8,128)}) custom-call(bf16[16,48,256]{2,1,0:T(8,128)(2,1)} %all_to_all.27.parts, f32[8,128]{1,0:T(8,128)} %shard_map.61.early), custom_call_target="tpu_custom_call" | custom-call | tf_op jit(solution)/shard_map/pallas_call | solution.py:162
  148.2 10.3 %all_to_all.28.scalars = f32[16,8,128]{2,1,0:T(8,128)} all-to-all(f32[16,8,128]{2,1,0:T(8,128)} %get-tuple-element.36), channel_id=1, replica_groups=mesh['op'=16,'qn'=16] {'qn'}, dimensions={0} | all-to-all | bytes 131072 | tf_op jit(solution)/shard_map/all_to_all | solution.py:256
  158.5 16.9 %all_to_all.29 = bf16[16,32,256]{2,1,0:T(8,128)(2,1)} all-to-all(bf16[16,32,256]{2,1,0:T(8,128)(2,1)} %get-tuple-element.37), channel_id=1, replica_groups=mesh['op'=16,'qn'=16] {'op'}, dimensions={0} | all-to-all | bytes 524288 | tf_op jit(solution)/shard_map/all_to_all | solution.py:217
  175.5 2.5 %shard_map.65 = (f32[2,256,256]{2,1,0:T(8,128)}, f32[2,256,256]{2,1,0:T(8,128)}) custom-call(f32[16,8,128]{2,1,0:T(8,128)} %all_to_all.28.scalars, f32[2,256,256]{2,1,0:T(8,128)} %p_ref.1, bf16[2,256,256]{2,1,0:T(8,128)(2,1)} %maximum_select_fusion.1.u.u_ref, bf16[2,256,256]{2,1,0:T(8,128)(2,1)} %bitcast.10), custom_call_target="tpu_custom_call" | custom-call | tf_op jit(solution)/shard_map/pallas_call | solution.py:196
  (45 shorter events, 4.5 us)
Async XLA Ops:
  0.6 29.7 %copy-start.7 = (s32[32,2,3]{0,1,2:T(2,128)S(1)}, s32[32,2,3]{0,1,2:T(2,128)}, u32[]{:S(2)}) copy-start(s32[32,2,3]{0,1,2:T(2,128)} %param.7) | copy-start | bytes 2308
  1.8 1.4 collective-permute-start.1
  3.2 8.4 %collective-permute-start.3 = (bf16[4,256,128]{2,1,0:T(8,128)(2,1)S(1)}, bf16[4,256,128]{2,1,0:T(8,128)(2,1)S(1)}, u32[]{:S(2)}, u32[]{:S(2)}) collective-permute-start(bf16[4,256,128]{2,1,0:T(8,128)(2,1)S(1)} %maximum_select_fusion.d0), channel_id=1, source_target_pairs={{0,4},{1,5},{2,6},{3,7},{4,0},{5,1},{6,2},{7,3},{8,12},{9,13},{10,... | collective-permute-start | bytes 786440 | tf_op jit(solution)/shard_map/ppermute | solution.py:206
  4.9 9.8 %collective-permute-start.7 = (bf16[4,256,128]{2,1,0:T(8,128)(2,1)S(1)}, bf16[4,256,128]{2,1,0:T(8,128)(2,1)}, u32[]{:S(2)}, u32[]{:S(2)}) collective-permute-start(bf16[4,256,128]{2,1,0:T(8,128)(2,1)S(1)} %maximum_select_fusion.d0), channel_id=1, source_target_pairs={{0,12},{1,13},{2,14},{3,15},{4,8},{5,9},{6,10},{7,11},{8,4},{9,5},... | collective-permute-start | bytes 786440 | tf_op jit(solution)/shard_map/ppermute | solution.py:206
  7.1 9.1 %collective-permute-start.2 = (bf16[4,256,128]{2,1,0:T(8,128)(2,1)S(1)}, bf16[4,256,128]{2,1,0:T(8,128)(2,1)}, u32[]{:S(2)}, u32[]{:S(2)}) collective-permute-start(bf16[4,256,128]{2,1,0:T(8,128)(2,1)S(1)} %maximum_select_fusion.d0), channel_id=1, source_target_pairs={{0,2},{1,3},{2,0},{3,1},{4,6},{5,7},{6,4},{7,5},{8,10},{9,11},{10,... | collective-permute-start | bytes 786440 | tf_op jit(solution)/shard_map/ppermute | solution.py:206
  11.7 8.9 %collective-permute-start.5 = (bf16[4,256,128]{2,1,0:T(8,128)(2,1)S(1)}, bf16[4,256,128]{2,1,0:T(8,128)(2,1)S(1)}, u32[]{:S(2)}, u32[]{:S(2)}) collective-permute-start(bf16[4,256,128]{2,1,0:T(8,128)(2,1)S(1)} %collective-permute-done.3.d2), channel_id=1, source_target_pairs={{0,12},{1,13},{2,14},{3,15},{4,8},{5,9},{6,10},{7,11},{8,4},{9,5},... | collective-permute-start | bytes 786440 | tf_op jit(solution)/shard_map/ppermute | solution.py:206
  14.7 11.4 %collective-permute-start.8 = (bf16[4,256,128]{2,1,0:T(8,128)(2,1)}, bf16[4,256,128]{2,1,0:T(8,128)(2,1)S(1)}, u32[]{:S(2)}, u32[]{:S(2)}) collective-permute-start(bf16[4,256,128]{2,1,0:T(8,128)(2,1)} %collective-permute-done.7.d6), channel_id=1, source_target_pairs={{0,2},{1,3},{2,0},{3,1},{4,6},{5,7},{6,4},{7,5},{8,10},{9,11},{10,... | collective-permute-start | bytes 786440 | tf_op jit(solution)/shard_map/ppermute | solution.py:206
  16.2 10.9 %collective-permute-start.4 = (bf16[4,256,128]{2,1,0:T(8,128)(2,1)}, bf16[4,256,128]{2,1,0:T(8,128)(2,1)S(1)}, u32[]{:S(2)}, u32[]{:S(2)}) collective-permute-start(bf16[4,256,128]{2,1,0:T(8,128)(2,1)} %collective-permute-done.2.d1), channel_id=1, source_target_pairs={{0,4},{1,5},{2,6},{3,7},{4,0},{5,1},{6,2},{7,3},{8,12},{9,13},{10,... | collective-permute-start | bytes 786440 | tf_op jit(solution)/shard_map/ppermute | solution.py:206
  21.2 12.2 %collective-permute-start.6 = (bf16[2,256,128]{2,1,0:T(8,128)(2,1)}, bf16[2,256,128]{2,1,0:T(8,128)(2,1)S(1)}, u32[]{:S(2)}, u32[]{:S(2)}) collective-permute-start(bf16[2,256,128]{2,1,0:T(8,128)(2,1)} %slice.46), channel_id=1, source_target_pairs={{0,2},{1,3},{2,0},{3,1},{4,6},{5,7},{6,4},{7,5},{8,10},{9,11},{10,... | collective-permute-start | bytes 393224 | tf_op jit(solution)/shard_map/ppermute | solution.py:206
  22.7 7.6 %collective-permute-start = (s32[32,2,3]{0,1,2:T(2,128)}, s32[32,2,3]{0,1,2:T(2,128)S(1)}, u32[]{:S(2)}, u32[]{:S(2)}) collective-permute-start(s32[32,2,3]{0,1,2:T(2,128)} %param.7), channel_id=1, source_target_pairs={{0,1},{1,0},{2,3},{3,2},{4,5},{5,4},{6,7},{7,6},{8,9},{9,8},{10,11... | collective-permute-start | bytes 2312 | tf_op jit(solution)/shard_map/ppermute | solution.py:206
  22.7 2.2 %copy-start.2 = (bf16[32,256,256]{2,1,0:T(8,128)(2,1)S(1)}, bf16[32,256,256]{2,1,0:T(8,128)(2,1)}, u32[]{:S(2)}) copy-start(bf16[32,256,256]{2,1,0:T(8,128)(2,1)} %r_ref.1) | copy-start | bytes 12582916
  26.8 6.7 %collective-permute-start.9 = (bf16[1,256,128]{2,1,0:T(8,128)(2,1)}, bf16[1,256,128]{2,1,0:T(8,128)(2,1)}, u32[]{:S(2)}, u32[]{:S(2)}) collective-permute-start(bf16[1,256,128]{2,1,0:T(8,128)(2,1)} %slice.47), channel_id=1, source_target_pairs={{0,4},{1,5},{2,6},{3,7},{4,0},{5,1},{6,2},{7,3},{8,12},{9,13},{10,... | collective-permute-start | bytes 196616 | tf_op jit(solution)/shard_map/ppermute | solution.py:206
  27.7 5.8 %collective-permute-start.10 = (bf16[1,256,128]{2,1,0:T(8,128)(2,1)}, bf16[1,256,128]{2,1,0:T(8,128)(2,1)}, u32[]{:S(2)}, u32[]{:S(2)}) collective-permute-start(bf16[1,256,128]{2,1,0:T(8,128)(2,1)} %slice.48), channel_id=1, source_target_pairs={{0,12},{1,13},{2,14},{3,15},{4,8},{5,9},{6,10},{7,11},{8,4},{9,5},... | collective-permute-start | bytes 196616 | tf_op jit(solution)/shard_map/ppermute | solution.py:206
  33.5 2.2 %copy-start = (bf16[32,256,256]{2,1,0:T(8,128)(2,1)S(1)}, bf16[32,256,256]{2,1,0:T(8,128)(2,1)}, u32[]{:S(2)}) copy-start(bf16[32,256,256]{2,1,0:T(8,128)(2,1)} %left.3) | copy-start | bytes 12582916
  42.5 2.0 %collective-permute-start.11 = (f32[1024,128]{1,0:T(8,128)S(1)}, f32[1024,128]{1,0:T(8,128)S(1)}, u32[]{:S(2)}, u32[]{:S(2)}) collective-permute-start(f32[1024,128]{1,0:T(8,128)S(1)} %get-tuple-element.21), channel_id=1, source_target_pairs={{0,1},{1,0},{2,3},{3,2},{4,5},{5,4},{6,7},{7,6},{8,9},{9,8},{10,11... | collective-permute-start | bytes 1572872 | tf_op jit(solution)/shard_map/ppermute | solution.py:206
  83.0 7.6 %collective-permute-start.17 = (bf16[4,256,128]{2,1,0:T(8,128)(2,1)S(1)}, bf16[4,256,128]{2,1,0:T(8,128)(2,1)S(1)}, u32[]{:S(2)}, u32[]{:S(2)}) collective-permute-start(bf16[4,256,128]{2,1,0:T(8,128)(2,1)S(1)} %bitcast.6), channel_id=1, source_target_pairs={{0,12},{1,13},{2,14},{3,15},{4,8},{5,9},{6,10},{7,11},{8,4},{9,5},... | collective-permute-start | bytes 786440 | tf_op jit(solution)/shard_map/ppermute | solution.py:206
  85.8 6.4 %collective-permute-start.13 = (bf16[4,256,128]{2,1,0:T(8,128)(2,1)S(1)}, bf16[4,256,128]{2,1,0:T(8,128)(2,1)S(1)}, u32[]{:S(2)}, u32[]{:S(2)}) collective-permute-start(bf16[4,256,128]{2,1,0:T(8,128)(2,1)S(1)} %bitcast.7), channel_id=1, source_target_pairs={{0,4},{1,5},{2,6},{3,7},{4,0},{5,1},{6,2},{7,3},{8,12},{9,13},{10,... | collective-permute-start | bytes 786440 | tf_op jit(solution)/shard_map/ppermute | solution.py:206
  85.8 9.0 %collective-permute-start.12 = (bf16[4,256,128]{2,1,0:T(8,128)(2,1)S(1)}, bf16[4,256,128]{2,1,0:T(8,128)(2,1)}, u32[]{:S(2)}, u32[]{:S(2)}) collective-permute-start(bf16[4,256,128]{2,1,0:T(8,128)(2,1)S(1)} %bitcast.8), channel_id=1, source_target_pairs={{0,2},{1,3},{2,0},{3,1},{4,6},{5,7},{6,4},{7,5},{8,10},{9,11},{10,... | collective-permute-start | bytes 786440 | tf_op jit(solution)/shard_map/ppermute | solution.py:206
  90.6 12.1 %collective-permute-start.18 = (bf16[4,256,128]{2,1,0:T(8,128)(2,1)S(1)}, bf16[4,256,128]{2,1,0:T(8,128)(2,1)S(1)}, u32[]{:S(2)}, u32[]{:S(2)}) collective-permute-start(bf16[4,256,128]{2,1,0:T(8,128)(2,1)S(1)} %collective-permute-done.17.d6), channel_id=1, source_target_pairs={{0,2},{1,3},{2,0},{3,1},{4,6},{5,7},{6,4},{7,5},{8,10},{9,11},{10,... | collective-permute-start | bytes 786440 | tf_op jit(solution)/shard_map/ppermute | solution.py:206
  92.2 7.6 %copy-start.4 = (bf16[4,256,128]{2,1,0:T(8,128)(2,1)}, bf16[4,256,128]{2,1,0:T(8,128)(2,1)S(1)}, u32[]{:S(2)}) copy-start(bf16[4,256,128]{2,1,0:T(8,128)(2,1)S(1)} %collective-permute-done.13.d2) | copy-start | bytes 786436
  92.2 7.6 %collective-permute-start.15 = (bf16[4,256,128]{2,1,0:T(8,128)(2,1)S(1)}, bf16[4,256,128]{2,1,0:T(8,128)(2,1)S(1)}, u32[]{:S(2)}, u32[]{:S(2)}) collective-permute-start(bf16[4,256,128]{2,1,0:T(8,128)(2,1)S(1)} %collective-permute-done.13.d2), channel_id=1, source_target_pairs={{0,12},{1,13},{2,14},{3,15},{4,8},{5,9},{6,10},{7,11},{8,4},{9,5},... | collective-permute-start | bytes 786440 | tf_op jit(solution)/shard_map/ppermute | solution.py:206
  94.8 8.5 %collective-permute-start.14 = (bf16[4,256,128]{2,1,0:T(8,128)(2,1)}, bf16[4,256,128]{2,1,0:T(8,128)(2,1)S(1)}, u32[]{:S(2)}, u32[]{:S(2)}) collective-permute-start(bf16[4,256,128]{2,1,0:T(8,128)(2,1)} %collective-permute-done.12.d1), channel_id=1, source_target_pairs={{0,4},{1,5},{2,6},{3,7},{4,0},{5,1},{6,2},{7,3},{8,12},{9,13},{10,... | collective-permute-start | bytes 786440 | tf_op jit(solution)/shard_map/ppermute | solution.py:206
  96.9 9.9 %collective-permute-start.21 = (bf16[2,256,128]{2,1,0:T(8,128)(2,1)}, bf16[2,256,128]{2,1,0:T(8,128)(2,1)}, u32[]{:S(2)}, u32[]{:S(2)}) collective-permute-start(bf16[2,256,128]{2,1,0:T(8,128)(2,1)} %bitcast.4), channel_id=1, source_target_pairs={{0,1},{1,0},{2,3},{3,2},{4,5},{5,4},{6,7},{7,6},{8,9},{9,8},{10,11... | collective-permute-start | bytes 393224 | tf_op jit(solution)/shard_map/ppermute | solution.py:206
  100.4 10.2 %collective-permute-start.16 = (bf16[2,256,128]{2,1,0:T(8,128)(2,1)}, bf16[2,256,128]{2,1,0:T(8,128)(2,1)S(1)}, u32[]{:S(2)}, u32[]{:S(2)}) collective-permute-start(bf16[2,256,128]{2,1,0:T(8,128)(2,1)} %slice.49), channel_id=1, source_target_pairs={{0,2},{1,3},{2,0},{3,1},{4,6},{5,7},{6,4},{7,5},{8,10},{9,11},{10,... | collective-permute-start | bytes 393224 | tf_op jit(solution)/shard_map/ppermute | solution.py:206
  103.3 7.3 %collective-permute-start.19 = (bf16[1,256,128]{2,1,0:T(8,128)(2,1)}, bf16[1,256,128]{2,1,0:T(8,128)(2,1)}, u32[]{:S(2)}, u32[]{:S(2)}) collective-permute-start(bf16[1,256,128]{2,1,0:T(8,128)(2,1)} %slice.50), channel_id=1, source_target_pairs={{0,4},{1,5},{2,6},{3,7},{4,0},{5,1},{6,2},{7,3},{8,12},{9,13},{10,... | collective-permute-start | bytes 196616 | tf_op jit(solution)/shard_map/ppermute | solution.py:206
  103.9 6.7 %collective-permute-start.20 = (bf16[1,256,128]{2,1,0:T(8,128)(2,1)}, bf16[1,256,128]{2,1,0:T(8,128)(2,1)}, u32[]{:S(2)}, u32[]{:S(2)}) collective-permute-start(bf16[1,256,128]{2,1,0:T(8,128)(2,1)} %slice.51), channel_id=1, source_target_pairs={{0,12},{1,13},{2,14},{3,15},{4,8},{5,9},{6,10},{7,11},{8,4},{9,5},... | collective-permute-start | bytes 196616 | tf_op jit(solution)/shard_map/ppermute | solution.py:206
  110.6 2.2 %copy-start.1 = (bf16[32,256,256]{2,1,0:T(8,128)(2,1)S(1)}, bf16[32,256,256]{2,1,0:T(8,128)(2,1)}, u32[]{:S(2)}) copy-start(bf16[32,256,256]{2,1,0:T(8,128)(2,1)} %left.3) | copy-start | bytes 12582916
  112.8 0.9 copy-start.5
  120.5 0.8 copy-start.3
  121.3 1.9 %collective-permute-start.22 = (f32[512,256]{1,0:T(8,128)S(1)}, f32[512,256]{1,0:T(8,128)S(1)}, u32[]{:S(2)}, u32[]{:S(2)}) collective-permute-start(f32[512,256]{1,0:T(8,128)S(1)} %get-tuple-element.33), channel_id=1, source_target_pairs={{0,1},{1,0},{2,3},{3,2},{4,5},{5,4},{6,7},{7,6},{8,9},{9,8},{10,11... | collective-permute-start | bytes 1572872 | tf_op jit(solution)/shard_map/ppermute | solution.py:206
  123.2 0.8 copy-start.6

commit v3 on v2

--- a/solution.py
+++ b/solution.py
@@ -14,7 +14,8 @@
 VMEM = pl.BlockSpec(memory_space=pltpu.VMEM)
 SMEM = pl.BlockSpec(memory_space=pltpu.SMEM)
 HBM = pl.BlockSpec(memory_space=pl.ANY)
-PARAMS = pltpu.CompilerParams(vmem_limit_bytes=40 * 1024 * 1024)
+def limit(mib):
+    return pltpu.CompilerParams(vmem_limit_bytes=mib * 1024 * 1024)
 
 
 def prepare_kernel(core_ref, r_ref, right, r_half, sems):
@@ -45,7 +46,7 @@
         out_specs=VMEM,
         out_shape=jax.ShapeDtypeStruct((ops * HALF, 256), BF),
         scratch_shapes=[pltpu.VMEM((ops, 256, HALF), BF), pltpu.SemaphoreType.DMA((ops // GROUP,))],
-        compiler_params=PARAMS,
+        compiler_params=limit(6),
         cost_estimate=pl.CostEstimate(flops=0, bytes_accessed=8 * 1024 * 1024, transcendentals=0),
     )(core, right_ops)
 
@@ -62,8 +63,7 @@
             k = step * GROUP + i
             sums = []
             for b in range(4):
-                at = (k * 4 + b) * 3
-                total = v[meta[at]].astype(F32) + v[meta[at + 1]].astype(F32) + v[meta[at + 2]].astype(F32)
+                total = v[meta[0, b, k]].astype(F32) + v[meta[1, b, k]].astype(F32) + v[meta[2, b, k]].astype(F32)
                 sums.append(total.astype(BF))
             product = jnp.dot(left[k], jnp.concatenate(sums, axis=1), preferred_element_type=F32).astype(BF)
             for b in range(4):
@@ -99,7 +99,7 @@
             pltpu.VMEM((1024, GROUP * HALF), BF),
             pltpu.VMEM((1024, 256), F32),
         ],
-        compiler_params=PARAMS,
+        compiler_params=limit(14),
     )(meta, core, *pieces, left, right)
 
 
@@ -113,69 +113,79 @@
 
 def dots(p, u):
     return pl.pallas_call(
-        dots_kernel, in_specs=[VMEM, VMEM], out_specs=VMEM, out_shape=jax.ShapeDtypeStruct((8, 128), F32)
+        dots_kernel,
+        in_specs=[VMEM, VMEM],
+        out_specs=VMEM,
+        out_shape=jax.ShapeDtypeStruct((8, 128), F32),
+        compiler_params=limit(4),
     )(p, u)
 
 
-def pack_kernel(mine, got, p, u, out):
+def pack_kernel(mine, got, p, u, early, out, stats):
     total = mine[...] + got[...]
-    for i in range(16):
-        out[i, :32] = total[32 * i : 32 * (i + 1)].astype(BF)
-    lane = lax.broadcasted_iota(jnp.int32, (16, 256), 1)
+    out[...] = total.astype(BF).reshape(16, 32, 256)
+    pw = jnp.sum(p[...].reshape(512, 256) * total)
+    uw = jnp.sum(u[...].reshape(512, 256).astype(F32) * total)
+    lane = lax.broadcasted_iota(jnp.int32, (8, 128), 1)
+    stats[...] = jnp.where(lane == 3, pw, jnp.where(lane == 4, uw, early[...]))
+
+
+def pack(mine, got, p, u, early):
+    return pl.pallas_call(
+        pack_kernel,
+        in_specs=[VMEM] * 5,
+        out_specs=[VMEM] * 2,
+        out_shape=[jax.ShapeDtypeStruct((16, 32, 256), BF), jax.ShapeDtypeStruct((8, 128), F32)],
+        compiler_params=limit(4),
+    )(mine, got, p, u, early)
+
+
+def relay_kernel(parts, stats, out):
+    total = parts[0].astype(F32)
+    for i in range(1, 16):
+        total += parts[i].astype(F32)
+    total = total.astype(BF)
+    lane = lax.broadcasted_iota(jnp.int32, (8, 128), 1)
+    first_row = lax.broadcasted_iota(jnp.int32, (8, 128), 0) == 0
+    wide = lax.broadcasted_iota(jnp.int32, (16, 256), 1)
     rows = jnp.zeros((16, 256), F32)
-    for at, field in enumerate((p[...], u[...].astype(F32))):
-        rest = jnp.full((16, 256), jnp.sum(field.reshape(512, 256) * total))
+    for at in range(2):
+        rest = jnp.full((16, 256), jnp.sum(jnp.where(first_row & (lane == 3 + at), stats[...], 0.0)))
         for part in range(3):
             term = rest.astype(BF).astype(F32)
-            rows = jnp.where(lane == 3 * at + part, term, rows)
+            rows = jnp.where(wide == 3 * at + part, term, rows)
             rest = rest - term
     rows = rows.astype(BF)
     for i in range(16):
+        out[i, :32] = total
         out[i, 32:] = rows
 
 
-def pack(mine, got, p, u):
-    return pl.pallas_call(
-        pack_kernel, in_specs=[VMEM] * 4, out_specs=VMEM, out_shape=jax.ShapeDtypeStruct((16, 48, 256), BF)
-    )(mine, got, p, u)
-
-
-def unpack_kernel(parts, early, piece, scalars):
-    total = parts[0, :32].astype(F32)
-    rows = parts[0, 32:].astype(F32)
+def relay(parts, stats):
+    return pl.pallas_call(
+        relay_kernel,
+        in_specs=[VMEM] * 2,
+        out_specs=VMEM,
+        out_shape=jax.ShapeDtypeStruct((16, 48, 256), BF),
+        compiler_params=limit(4),
+    )(parts, stats)
+
+
+def finish_kernel(count, stats, whole, p_ref, u_ref, ritz_ref, residual_ref):
+    rows = whole[0, 32:].astype(F32)
     for i in range(1, 16):
-        total += parts[i, :32].astype(F32)
-        rows += parts[i, 32:].astype(F32)
-    total = total.astype(BF)
-    lane = lax.broadcasted_iota(jnp.int32, (16, 256), 1)
-    first_row = lax.broadcasted_iota(jnp.int32, (16, 256), 0) == 0
-    pw = jnp.sum(jnp.where(first_row & (lane < 3), rows, 0.0))
-    uw = jnp.sum(jnp.where(first_row & (lane >= 3), rows, 0.0))
-    lane = lax.broadcasted_iota(jnp.int32, (8, 128), 1)
-    out = jnp.where(lane == 3, pw, jnp.where(lane == 4, uw, early[...]))
-    for i in range(16):
-        piece[i] = total
-        scalars[i] = out
-
-
-def unpack(parts, early):
-    return pl.pallas_call(
-        unpack_kernel,
-        in_specs=[VMEM] * 2,
-        out_specs=[VMEM] * 2,
-        out_shape=[jax.ShapeDtypeStruct((16, 32, 256), BF), jax.ShapeDtypeStruct((16, 8, 128), F32)],
-    )(parts, early)
-
-
-def finish_kernel(count, scalars, p_ref, u_ref, w_ref, ritz_ref, residual_ref):
-    total = scalars[0]
-    for i in range(1, 16):
-        total += scalars[i]
+        rows += whole[i, 32:].astype(F32)
     lane = lax.broadcasted_iota(jnp.int32, (8, 128), 1)
     row = lax.broadcasted_iota(jnp.int32, (8, 128), 0)
-    pp, pu, uu, pw, uw = (
-        jnp.full((1, 256), jnp.sum(jnp.where((lane == i) & (row == 0), total, 0.0)) / count) for i in range(5)
-    )
+    wide = lax.broadcasted_iota(jnp.int32, (16, 256), 1)
+    tall = lax.broadcasted_iota(jnp.int32, (16, 256), 0)
+
+    def scalar(total):
+        return jnp.full((1, 256), total / count)
+
+    pp, pu, uu = (scalar(jnp.sum(jnp.where((lane == i) & (row == 0), stats[...], 0.0))) for i in range(3))
+    pw = scalar(jnp.sum(jnp.where((wide < 3) & (tall == 0), rows, 0.0)))
+    uw = scalar(jnp.sum(jnp.where((wide >= 3) & (wide < 6) & (tall == 0), rows, 0.0)))
     s = lax.rsqrt(pp + epsilon)
     energy = s * s * pu
     t = lax.rsqrt(s * s * (uu - 2.0 * energy * pu + energy * energy * pp) + epsilon)
@@ -185,21 +195,24 @@
     gap = energy - diag_d
     theta = 0.5 * (energy + diag_d) - jnp.sqrt(0.25 * gap * gap + coupling * coupling)
     one, two = (diag_d - theta) * s, coupling * ts
-    p, u, w = p_ref[0], u_ref[0].astype(F32), w_ref[0].astype(F32)
+    block = pl.program_id(0)
+    p, u = p_ref[0], u_ref[0].astype(F32)
+    w = whole[pl.ds(8 * block, 8), :32, :].reshape(256, 256).astype(F32)
     ritz = one * p - two * (u - energy * p)
     ritz_ref[0] = ritz
     residual_ref[0] = one * u - two * (w - energy * u) - theta * ritz
 
 
-def finish(count, scalars, p, u, w):
+def finish(count, stats, whole, p, u):
     block = pl.BlockSpec((1, 256, 256), lambda i: (i, 0, 0))
     return pl.pallas_call(
         functools.partial(finish_kernel, count),
         grid=(p.shape[0],),
-        in_specs=[pl.BlockSpec((16, 8, 128), lambda i: (0, 0, 0)), block, block, block],
+        in_specs=[VMEM, VMEM, block, block],
         out_specs=[block, block],
         out_shape=[jax.ShapeDtypeStruct(p.shape, F32)] * 2,
-    )(scalars, p, u, w)
+        compiler_params=limit(6),
+    )(stats, whole, p, u)
 
 
 def swap(x, bits):
@@ -231,10 +244,9 @@
 
     low, high = psi_start[:, :, :HALF].astype(BF), psi_start[:, :, HALF:].astype(BF)
     own = in_order(pick(low, high), swap(pick(high, low), 1))
+    sources = jnp.transpose(sources, (2, 1, 0)) ^ (chip * 4)
     theirs = swap(sources, 1)
-    where = chip * 4
-    by_chip = (in_order(sources, theirs, 1) ^ where).reshape(-1)
-    own_first = (jnp.concatenate([sources, theirs], 1) ^ where).reshape(-1)
+    by_chip, own_first = in_order(sources, theirs, 1), jnp.concatenate([sources, theirs], 1)
     core = core.reshape(1)
 
     pieces = gather_chips(own)
@@ -252,10 +264,11 @@
     early = dots(psi_start, u)
     pieces, u, early = lax.optimization_barrier((pieces, u, early))
     mine, other = apply_ham(True, own_first, core, pieces, left_ops, right)
-    piece, scalars = unpack(op_exchange(pack(mine, swap(other, 1), psi_start, u)), early)
-    scalars = lax.all_to_all(scalars, "qn", 0, 0, tiled=True)
-    w = op_exchange(piece).reshape(2, 256, 256)
-    return tuple(finish(count, scalars, psi_start, u, w))
+    packed, stats = pack(mine, swap(other, 1), psi_start, u, early)
+    parts = op_exchange(packed)
+    for bits in (1, 2, 4, 8):
+        stats = stats + swap(stats, bits)
+    return tuple(finish(count, stats, op_exchange(relay(parts, stats)), psi_start, u))
 
 
 def solution(mesh):

time: 179 us -> 158 us (0.88)
  blocking collectives: 85.4 us -> 59.2 us
  waiting for transfers between devices: 22.3 us -> 40.6 us
  local copies, waits for them, and re-layouts: 17.2 us -> 4.47 us
  starting transfers between devices: 24.2 us -> 32.3 us
  Pallas kernels: 23.6 us -> 17.5 us
  other arithmetic: 4.43 us -> 2.07 us
    ppermute x23 -> x27, waiting for transfers between devices: 22.3 us -> 40.6 us  [swap(): return lax.ppermute(x, 'qn', [(i, i ^ bits) for i in range(16)])]
    all_to_all x4 -> x3, blocking collectives: 75.1 us -> 59.2 us  [op_exchange(): return lax.all_to_all(x, 'op', 0, 0, tiled=True)]
    all_to_all x1 -> x0, blocking collectives: 10.3 us -> none  [shards(): scalars = lax.all_to_all(scalars, 'qn', 0, 0, tiled=True)]
    all_to_all x0 -> x1, starting transfers between devices: none -> 5.17 us  [op_exchange(): return lax.all_to_all(x, 'op', 0, 0, tiled=True)]
    unnamed x16 -> x8, local copies, waits for them, and re-layouts: 9.1 us -> 4.39 us
    xor x4 -> x0, local copies, waits for them, and re-layouts: 4.26 us -> none  [the longest x2 2.47 us: shards(): by_chip = (in_order(sources, theirs, 1) ^ where).reshape(-1)]
    slice x6, local copies, waits for them, and re-layouts: 3.84 us -> 0.04 us  [gather_chips(): far = (swap(y2[:2], 2), swap(x1y3[2:3], 4), swap(x1y1[3:], 12))]
    pallas_call x2, Pallas kernels: 4.28 us -> 1.07 us  [the longest x1 0.93 us: pack(): pl.pallas_call(pack_kernel, in_specs=[VMEM] * 5, out_specs=[VMEM] * 2, ou...]
  transfers between devices with their start and end apart: 23 -> 28, of which waited for: 9 -> 18; matrix products, arithmetic and copies ran while one was open for 6% -> 1% of each run, Pallas kernels for 2% -> 1%
where the time goes in v3:
time: 158 us; the launch traced here: 157 us
  blocking collectives  59.2 us (37%)
  waiting for transfers between devices  40.6 us (26%)
  starting transfers between devices  32.3 us (20%)
  Pallas kernels  17.5 us (11%)
  local copies, waits for them, and re-layouts  4.47 us (3%)
  other arithmetic  2.07 us (1%)
    all_to_all x3, blocking collectives, op_exchange(): return lax.all_to_all(x, 'op', 0, 0, tiled=True)  59.2 us
    ppermute x27, waiting for transfers between devices, swap(): return lax.ppermute(x, 'qn', [(i, i ^ bits) for i in range(16)])  40.6 us
    ppermute x27, starting transfers between devices, swap(): return lax.ppermute(x, 'qn', [(i, i ^ bits) for i in range(16)])  27.2 us
    pallas_call x2, Pallas kernels, apply_ham(): pl.pallas_call(functools.partial(ham_kernel, by_block), in_specs=[SMEM, S...  13.6 us
    all_to_all x1, starting transfers between devices, op_exchange(): return lax.all_to_all(x, 'op', 0, 0, tiled=True)  5.17 us
    unnamed x8, local copies, waits for them, and re-layouts  4.39 us
  transfers between devices with their start and end apart: 28, of which 18 were waited for; matrix products, arithmetic and copies ran while one was open for 1% of the time, Pallas kernels for 1%

profile of v3, /device:TPU:32, one launch (start us, length us, event | category | flops | bytes accessed | tf_op | source)
XLA Modules:
  0.0 157.1 jit_solution(14135281464186515338)
XLA Ops:
  0.6 1.1 convert.5
  1.9 1.3 collective-permute-done.1
  3.2 1.7 %collective-permute-start.3 = (bf16[4,256,128]{2,1,0:T(8,128)(2,1)S(1)}, bf16[4,256,128]{2,1,0:T(8,128)(2,1)S(1)}, u32[]{:S(2)}, u32[]{:S(2)}) collective-permute-start(bf16[4,256,128]{2,1,0:T(8,128)(2,1)S(1)} %maximum_select_fusion.d0), channel_id=1, source_target_pairs={{0,4},{1,5},{2,6},{3,7},{4,0},{5,1},{6,2},{7,3},{8,12},{9,13},{10,... | collective-permute-start | bytes 786440 | tf_op jit(solution)/shard_map/ppermute | solution.py:219
  4.9 2.2 %collective-permute-start.7 = (bf16[4,256,128]{2,1,0:T(8,128)(2,1)S(1)}, bf16[4,256,128]{2,1,0:T(8,128)(2,1)}, u32[]{:S(2)}, u32[]{:S(2)}) collective-permute-start(bf16[4,256,128]{2,1,0:T(8,128)(2,1)S(1)} %maximum_select_fusion.d0), channel_id=1, source_target_pairs={{0,12},{1,13},{2,14},{3,15},{4,8},{5,9},{6,10},{7,11},{8,4},{9,5},... | collective-permute-start | bytes 786440 | tf_op jit(solution)/shard_map/ppermute | solution.py:219
  7.1 1.5 collective-permute-start.2
  8.6 3.1 %collective-permute-done.3.d2 = bf16[4,256,128]{2,1,0:T(8,128)(2,1)S(1)} collective-permute-done((bf16[4,256,128]{2,1,0:T(8,128)(2,1)S(1)}, bf16[4,256,128]{2,1,0:T(8,128)(2,1)S(1)}, u32[]{:S(2)}, u32[]{:S(2)}) %collective-permute-start.3) | collective-permute-done | bytes 262176 | tf_op jit(solution)/shard_map/ppermute | solution.py:219
  11.7 3.0 %collective-permute-start.5 = (bf16[4,256,128]{2,1,0:T(8,128)(2,1)S(1)}, bf16[4,256,128]{2,1,0:T(8,128)(2,1)S(1)}, u32[]{:S(2)}, u32[]{:S(2)}) collective-permute-start(bf16[4,256,128]{2,1,0:T(8,128)(2,1)S(1)} %collective-permute-done.3.d2), channel_id=1, source_target_pairs={{0,12},{1,13},{2,14},{3,15},{4,8},{5,9},{6,10},{7,11},{8,4},{9,5},... | collective-permute-start | bytes 786440 | tf_op jit(solution)/shard_map/ppermute | solution.py:219
  14.7 1.5 collective-permute-start.8
  16.3 4.3 %collective-permute-done.5.d4 = bf16[4,256,128]{2,1,0:T(8,128)(2,1)S(1)} collective-permute-done((bf16[4,256,128]{2,1,0:T(8,128)(2,1)S(1)}, bf16[4,256,128]{2,1,0:T(8,128)(2,1)S(1)}, u32[]{:S(2)}, u32[]{:S(2)}) %collective-permute-start.5) | collective-permute-done | bytes 262176 | tf_op jit(solution)/shard_map/ppermute | solution.py:219
  20.6 1.6 %collective-permute-start.6 = (bf16[2,256,128]{2,1,0:T(8,128)(2,1)S(1)}, bf16[2,256,128]{2,1,0:T(8,128)(2,1)S(1)}, u32[]{:S(2)}, u32[]{:S(2)}) collective-permute-start(bf16[2,256,128]{2,1,0:T(8,128)(2,1)S(1)} %slice.46), channel_id=1, source_target_pairs={{0,2},{1,3},{2,0},{3,1},{4,6},{5,7},{6,4},{7,5},{8,10},{9,11},{10,... | collective-permute-start | bytes 393224 | tf_op jit(solution)/shard_map/ppermute | solution.py:219
  22.2 0.7 xor_bitcast_fusion
  22.9 2.2 %copy-done.3 = bf16[32,256,256]{2,1,0:T(8,128)(2,1)S(1)} copy-done((bf16[32,256,256]{2,1,0:T(8,128)(2,1)S(1)}, bf16[32,256,256]{2,1,0:T(8,128)(2,1)}, u32[]{:S(2)}) %copy-start.3) | copy-done | bytes 4194328
  25.0 1.2 shard_map.59.right
  26.2 0.4 collective-permute-start.9
  26.6 2.9 %collective-permute-start.10 = (bf16[1,256,128]{2,1,0:T(8,128)(2,1)S(1)}, bf16[1,256,128]{2,1,0:T(8,128)(2,1)S(1)}, u32[]{:S(2)}, u32[]{:S(2)}) collective-permute-start(bf16[1,256,128]{2,1,0:T(8,128)(2,1)S(1)} %slice.48), channel_id=1, source_target_pairs={{0,12},{1,13},{2,14},{3,15},{4,8},{5,9},{6,10},{7,11},{8,4},{9,5},... | collective-permute-start | bytes 196616 | tf_op jit(solution)/shard_map/ppermute | solution.py:219
  29.6 1.2 collective-permute-done.9.d5b
  30.8 1.6 collective-permute-done.10.d5c
  32.4 7.0 %shard_map.60 = (f32[1024,128]{1,0:T(8,128)S(1)}, f32[1024,128]{1,0:T(8,128)S(1)}) custom-call(s32[3,4,32]{2,1,0:T(4,128)S(1)} %get-tuple-element.42.meta, s32[1]{0:T(128)} %bitcast.1.core_ref, bf16[4,256,128]{2,1,0:T(8,128)(2,1)S(1)} %maximum_select_fusion.d0, bf16[4,256,128]{2,1,0:T(8,128)(2,1)} %collective-permute-done.2.d1, ...), custom_call_target="tpu_custom_call" | custom-call | tf_op jit(solution)/shard_map/pallas_call | solution.py:92
  39.5 1.9 %collective-permute-done.11 = f32[1024,128]{1,0:T(8,128)S(1)} collective-permute-done((f32[1024,128]{1,0:T(8,128)S(1)}, f32[1024,128]{1,0:T(8,128)S(1)}, u32[]{:S(2)}, u32[]{:S(2)}) %collective-permute-start.11) | collective-permute-done | bytes 524320 | tf_op jit(solution)/shard_map/ppermute | solution.py:219
  41.4 22.4 %all_to_all.20 = bf16[16,64,128]{2,1,0:T(8,128)(2,1)S(1)} all-to-all(bf16[16,64,128]{2,1,0:T(8,128)(2,1)S(1)} %bitcast.11), channel_id=1, replica_groups=mesh['op'=16,'qn'=16] {'op'}, dimensions={0} | all-to-all | bytes 524288 | tf_op jit(solution)/shard_map/all_to_all | solution.py:230
  64.0 15.8 %all_to_all.21 = bf16[16,64,128]{2,1,0:T(8,128)(2,1)S(1)} all-to-all(bf16[16,64,128]{2,1,0:T(8,128)(2,1)S(1)} %broadcast_in_dim.2), channel_id=1, replica_groups=mesh['op'=16,'qn'=16] {'op'}, dimensions={0} | all-to-all | bytes 524288 | tf_op jit(solution)/shard_map/all_to_all | solution.py:230
  79.8 2.9 %collective-permute-start.17 = (bf16[4,256,128]{2,1,0:T(8,128)(2,1)S(1)}, bf16[4,256,128]{2,1,0:T(8,128)(2,1)S(1)}, u32[]{:S(2)}, u32[]{:S(2)}) collective-permute-start(bf16[4,256,128]{2,1,0:T(8,128)(2,1)S(1)} %bitcast.7), channel_id=1, source_target_pairs={{0,12},{1,13},{2,14},{3,15},{4,8},{5,9},{6,10},{7,11},{8,4},{9,5},... | collective-permute-start | bytes 786440 | tf_op jit(solution)/shard_map/ppermute | solution.py:219
  82.9 4.4 %collective-permute-done.17.d6 = bf16[4,256,128]{2,1,0:T(8,128)(2,1)S(1)} collective-permute-done((bf16[4,256,128]{2,1,0:T(8,128)(2,1)S(1)}, bf16[4,256,128]{2,1,0:T(8,128)(2,1)S(1)}, u32[]{:S(2)}, u32[]{:S(2)}) %collective-permute-start.17) | collective-permute-done | bytes 262176 | tf_op jit(solution)/shard_map/ppermute | solution.py:219
  87.6 1.5 collective-permute-done.13.d2
  89.1 1.4 collective-permute-start.15
  90.5 1.1 collective-permute-done.12.d1
  91.6 1.4 collective-permute-start.14
  93.1 3.6 %collective-permute-done.15.d4 = bf16[4,256,128]{2,1,0:T(8,128)(2,1)S(1)} collective-permute-done((bf16[4,256,128]{2,1,0:T(8,128)(2,1)S(1)}, bf16[4,256,128]{2,1,0:T(8,128)(2,1)S(1)}, u32[]{:S(2)}, u32[]{:S(2)}) %collective-permute-start.15) | collective-permute-done | bytes 262176 | tf_op jit(solution)/shard_map/ppermute | solution.py:219
  96.7 0.4 collective-permute-start.16
  97.2 1.5 collective-permute-done.14.d3
  98.7 1.8 %collective-permute-start.20 = (bf16[1,256,128]{2,1,0:T(8,128)(2,1)S(1)}, bf16[1,256,128]{2,1,0:T(8,128)(2,1)S(1)}, u32[]{:S(2)}, u32[]{:S(2)}) collective-permute-start(bf16[1,256,128]{2,1,0:T(8,128)(2,1)S(1)} %slice.51), channel_id=1, source_target_pairs={{0,12},{1,13},{2,14},{3,15},{4,8},{5,9},{6,10},{7,11},{8,4},{9,5},... | collective-permute-start | bytes 196616 | tf_op jit(solution)/shard_map/ppermute | solution.py:219
  100.5 0.3 shard_map.61.early
  100.9 0.6 collective-permute-done.19.d5b
  101.4 2.7 %collective-permute-done.20.d5c = bf16[1,256,128]{2,1,0:T(8,128)(2,1)S(1)} collective-permute-done((bf16[1,256,128]{2,1,0:T(8,128)(2,1)S(1)}, bf16[1,256,128]{2,1,0:T(8,128)(2,1)S(1)}, u32[]{:S(2)}, u32[]{:S(2)}) %collective-permute-start.20) | collective-permute-done | bytes 65568 | tf_op jit(solution)/shard_map/ppermute | solution.py:219
  104.1 2.2 %copy-done.1 = bf16[32,256,256]{2,1,0:T(8,128)(2,1)S(1)} copy-done((bf16[32,256,256]{2,1,0:T(8,128)(2,1)S(1)}, bf16[32,256,256]{2,1,0:T(8,128)(2,1)}, u32[]{:S(2)}) %copy-start.1) | copy-done | bytes 4194328
  106.3 6.6 %shard_map.62 = (f32[512,256]{1,0:T(8,128)S(1)}, f32[512,256]{1,0:T(8,128)S(1)}) custom-call(s32[3,4,32]{2,1,0:T(4,128)S(1)} %get-tuple-element.43.meta, s32[1]{0:T(128)} %bitcast.1.core_ref, bf16[4,256,128]{2,1,0:T(8,128)(2,1)S(1)} %bitcast.10, bf16[4,256,128]{2,1,0:T(8,128)(2,1)S(1)} %collective-permute-done.12.d1, ...), custom_call_target="tpu_custom_call" | custom-call | tf_op jit(solution)/shard_map/pallas_call | solution.py:92
  113.0 1.9 %collective-permute-done.22.got = f32[512,256]{1,0:T(8,128)S(1)} collective-permute-done((f32[512,256]{1,0:T(8,128)S(1)}, f32[512,256]{1,0:T(8,128)S(1)}, u32[]{:S(2)}, u32[]{:S(2)}) %collective-permute-start.22) | collective-permute-done | bytes 524320 | tf_op jit(solution)/shard_map/ppermute | solution.py:219
  114.9 0.9 shard_map.63
  115.9 5.2 %all-to-all-start.2 = ((bf16[16,32,256]{2,1,0:T(8,128)(2,1)}), bf16[16,32,256]{2,1,0:T(8,128)(2,1)S(1)}, u32[]{:S(2)}, u32[]{:S(2)}) async-start(bf16[16,32,256]{2,1,0:T(8,128)(2,1)} %get-tuple-element.37), calls=%async_computation.2 | async-start | bytes 524288 | tf_op jit(solution)/shard_map/all_to_all | solution.py:230
  121.0 1.2 collective-permute-done.23
  122.2 0.6 collective-permute-start.24
  122.8 3.1 %collective-permute-done.24 = f32[8,128]{1,0:T(8,128)S(1)} collective-permute-done((f32[8,128]{1,0:T(8,128)S(1)}, f32[8,128]{1,0:T(8,128)S(1)}, u32[]{:S(2)}, u32[]{:S(2)}) %collective-permute-start.24) | collective-permute-done | bytes 4128 | tf_op jit(solution)/shard_map/ppermute | solution.py:219
  125.9 0.4 collective-permute-start.25
  126.2 3.2 %collective-permute-done.25 = f32[8,128]{1,0:T(8,128)S(1)} collective-permute-done((f32[8,128]{1,0:T(8,128)S(1)}, f32[8,128]{1,0:T(8,128)S(1)}, u32[]{:S(2)}, u32[]{:S(2)}) %collective-permute-start.25) | collective-permute-done | bytes 4128 | tf_op jit(solution)/shard_map/ppermute | solution.py:219
  129.5 2.5 %collective-permute-start.26 = (f32[8,128]{1,0:T(8,128)S(1)}, f32[8,128]{1,0:T(8,128)S(1)}, u32[]{:S(2)}, u32[]{:S(2)}) collective-permute-start(f32[8,128]{1,0:T(8,128)S(1)} %add.24), channel_id=1, source_target_pairs={{0,8},{1,9},{2,10},{3,11},{4,12},{5,13},{6,14},{7,15},{8,0},{9,1},... | collective-permute-start | bytes 12296 | tf_op jit(solution)/shard_map/ppermute | solution.py:219
  131.9 2.7 %collective-permute-done.26 = f32[8,128]{1,0:T(8,128)S(1)} collective-permute-done((f32[8,128]{1,0:T(8,128)S(1)}, f32[8,128]{1,0:T(8,128)S(1)}, u32[]{:S(2)}, u32[]{:S(2)}) %collective-permute-start.26) | collective-permute-done | bytes 4128 | tf_op jit(solution)/shard_map/ppermute | solution.py:219
  134.7 21.0 %all_to_all.22.whole = bf16[16,48,256]{2,1,0:T(8,128)(2,1)S(1)} all-to-all(bf16[16,48,256]{2,1,0:T(8,128)(2,1)S(1)} %shard_map.64), channel_id=1, replica_groups=mesh['op'=16,'qn'=16] {'op'}, dimensions={0} | all-to-all | bytes 786432 | tf_op jit(solution)/shard_map/all_to_all | solution.py:230
  155.7 1.4 shard_map.65
  (46 shorter events, 1.6 us)
Async XLA Ops:
  1.7 1.4 collective-permute-start.1
  3.2 8.4 %collective-permute-start.3 = (bf16[4,256,128]{2,1,0:T(8,128)(2,1)S(1)}, bf16[4,256,128]{2,1,0:T(8,128)(2,1)S(1)}, u32[]{:S(2)}, u32[]{:S(2)}) collective-permute-start(bf16[4,256,128]{2,1,0:T(8,128)(2,1)S(1)} %maximum_select_fusion.d0), channel_id=1, source_target_pairs={{0,4},{1,5},{2,6},{3,7},{4,0},{5,1},{6,2},{7,3},{8,12},{9,13},{10,... | collective-permute-start | bytes 786440 | tf_op jit(solution)/shard_map/ppermute | solution.py:219
  4.9 9.8 %collective-permute-start.7 = (bf16[4,256,128]{2,1,0:T(8,128)(2,1)S(1)}, bf16[4,256,128]{2,1,0:T(8,128)(2,1)}, u32[]{:S(2)}, u32[]{:S(2)}) collective-permute-start(bf16[4,256,128]{2,1,0:T(8,128)(2,1)S(1)} %maximum_select_fusion.d0), channel_id=1, source_target_pairs={{0,12},{1,13},{2,14},{3,15},{4,8},{5,9},{6,10},{7,11},{8,4},{9,5},... | collective-permute-start | bytes 786440 | tf_op jit(solution)/shard_map/ppermute | solution.py:219
  7.1 9.1 %collective-permute-start.2 = (bf16[4,256,128]{2,1,0:T(8,128)(2,1)S(1)}, bf16[4,256,128]{2,1,0:T(8,128)(2,1)}, u32[]{:S(2)}, u32[]{:S(2)}) collective-permute-start(bf16[4,256,128]{2,1,0:T(8,128)(2,1)S(1)} %maximum_select_fusion.d0), channel_id=1, source_target_pairs={{0,2},{1,3},{2,0},{3,1},{4,6},{5,7},{6,4},{7,5},{8,10},{9,11},{10,... | collective-permute-start | bytes 786440 | tf_op jit(solution)/shard_map/ppermute | solution.py:219
  11.7 8.9 %collective-permute-start.5 = (bf16[4,256,128]{2,1,0:T(8,128)(2,1)S(1)}, bf16[4,256,128]{2,1,0:T(8,128)(2,1)S(1)}, u32[]{:S(2)}, u32[]{:S(2)}) collective-permute-start(bf16[4,256,128]{2,1,0:T(8,128)(2,1)S(1)} %collective-permute-done.3.d2), channel_id=1, source_target_pairs={{0,12},{1,13},{2,14},{3,15},{4,8},{5,9},{6,10},{7,11},{8,4},{9,5},... | collective-permute-start | bytes 786440 | tf_op jit(solution)/shard_map/ppermute | solution.py:219
  14.7 11.5 %collective-permute-start.8 = (bf16[4,256,128]{2,1,0:T(8,128)(2,1)}, bf16[4,256,128]{2,1,0:T(8,128)(2,1)S(1)}, u32[]{:S(2)}, u32[]{:S(2)}) collective-permute-start(bf16[4,256,128]{2,1,0:T(8,128)(2,1)} %collective-permute-done.7.d6), channel_id=1, source_target_pairs={{0,2},{1,3},{2,0},{3,1},{4,6},{5,7},{6,4},{7,5},{8,10},{9,11},{10,... | collective-permute-start | bytes 786440 | tf_op jit(solution)/shard_map/ppermute | solution.py:219
  16.2 10.5 %collective-permute-start.4 = (bf16[4,256,128]{2,1,0:T(8,128)(2,1)}, bf16[4,256,128]{2,1,0:T(8,128)(2,1)S(1)}, u32[]{:S(2)}, u32[]{:S(2)}) collective-permute-start(bf16[4,256,128]{2,1,0:T(8,128)(2,1)} %collective-permute-done.2.d1), channel_id=1, source_target_pairs={{0,4},{1,5},{2,6},{3,7},{4,0},{5,1},{6,2},{7,3},{8,12},{9,13},{10,... | collective-permute-start | bytes 786440 | tf_op jit(solution)/shard_map/ppermute | solution.py:219
  16.3 16.1 %copy-start = (bf16[32,256,256]{2,1,0:T(8,128)(2,1)S(1)}, bf16[32,256,256]{2,1,0:T(8,128)(2,1)}, u32[]{:S(2)}) copy-start(bf16[32,256,256]{2,1,0:T(8,128)(2,1)} %left.3) | copy-start | bytes 12582916
  20.6 11.8 %collective-permute-start.6 = (bf16[2,256,128]{2,1,0:T(8,128)(2,1)S(1)}, bf16[2,256,128]{2,1,0:T(8,128)(2,1)S(1)}, u32[]{:S(2)}, u32[]{:S(2)}) collective-permute-start(bf16[2,256,128]{2,1,0:T(8,128)(2,1)S(1)} %slice.46), channel_id=1, source_target_pairs={{0,2},{1,3},{2,0},{3,1},{4,6},{5,7},{6,4},{7,5},{8,10},{9,11},{10,... | collective-permute-start | bytes 393224 | tf_op jit(solution)/shard_map/ppermute | solution.py:219
  22.8 6.7 %collective-permute-start = (s32[3,2,32]{2,1,0:T(2,128)S(1)}, s32[3,2,32]{2,1,0:T(2,128)S(1)}, u32[]{:S(2)}, u32[]{:S(2)}) collective-permute-start(s32[3,2,32]{2,1,0:T(2,128)S(1)} %xor_bitcast_fusion), channel_id=1, source_target_pairs={{0,1},{1,0},{2,3},{3,2},{4,5},{5,4},{6,7},{7,6},{8,9},{9,8},{10,11... | collective-permute-start | bytes 2312 | tf_op jit(solution)/shard_map/ppermute | solution.py:219
  22.9 2.2 %copy-start.3 = (bf16[32,256,256]{2,1,0:T(8,128)(2,1)S(1)}, bf16[32,256,256]{2,1,0:T(8,128)(2,1)}, u32[]{:S(2)}) copy-start(bf16[32,256,256]{2,1,0:T(8,128)(2,1)} %r_ref.1) | copy-start | bytes 12582916
  26.2 4.6 %collective-permute-start.9 = (bf16[1,256,128]{2,1,0:T(8,128)(2,1)S(1)}, bf16[1,256,128]{2,1,0:T(8,128)(2,1)S(1)}, u32[]{:S(2)}, u32[]{:S(2)}) collective-permute-start(bf16[1,256,128]{2,1,0:T(8,128)(2,1)S(1)} %slice.47), channel_id=1, source_target_pairs={{0,4},{1,5},{2,6},{3,7},{4,0},{5,1},{6,2},{7,3},{8,12},{9,13},{10,... | collective-permute-start | bytes 196616 | tf_op jit(solution)/shard_map/ppermute | solution.py:219
  26.6 5.7 %collective-permute-start.10 = (bf16[1,256,128]{2,1,0:T(8,128)(2,1)S(1)}, bf16[1,256,128]{2,1,0:T(8,128)(2,1)S(1)}, u32[]{:S(2)}, u32[]{:S(2)}) collective-permute-start(bf16[1,256,128]{2,1,0:T(8,128)(2,1)S(1)} %slice.48), channel_id=1, source_target_pairs={{0,12},{1,13},{2,14},{3,15},{4,8},{5,9},{6,10},{7,11},{8,4},{9,5},... | collective-permute-start | bytes 196616 | tf_op jit(solution)/shard_map/ppermute | solution.py:219
  39.4 61.2 %copy-start.2 = (f32[2,256,256]{2,1,0:T(8,128)S(1)}, f32[2,256,256]{2,1,0:T(8,128)}, u32[]{:S(2)}) copy-start(f32[2,256,256]{2,1,0:T(8,128)} %p_ref.1) | copy-start | bytes 1572868
  39.4 2.0 %collective-permute-start.11 = (f32[1024,128]{1,0:T(8,128)S(1)}, f32[1024,128]{1,0:T(8,128)S(1)}, u32[]{:S(2)}, u32[]{:S(2)}) collective-permute-start(f32[1024,128]{1,0:T(8,128)S(1)} %get-tuple-element.21), channel_id=1, source_target_pairs={{0,1},{1,0},{2,3},{3,2},{4,5},{5,4},{6,7},{7,6},{8,9},{9,8},{10,11... | collective-permute-start | bytes 1572872 | tf_op jit(solution)/shard_map/ppermute | solution.py:219
  79.8 7.6 %collective-permute-start.17 = (bf16[4,256,128]{2,1,0:T(8,128)(2,1)S(1)}, bf16[4,256,128]{2,1,0:T(8,128)(2,1)S(1)}, u32[]{:S(2)}, u32[]{:S(2)}) collective-permute-start(bf16[4,256,128]{2,1,0:T(8,128)(2,1)S(1)} %bitcast.7), channel_id=1, source_target_pairs={{0,12},{1,13},{2,14},{3,15},{4,8},{5,9},{6,10},{7,11},{8,4},{9,5},... | collective-permute-start | bytes 786440 | tf_op jit(solution)/shard_map/ppermute | solution.py:219
  82.7 6.4 %collective-permute-start.13 = (bf16[4,256,128]{2,1,0:T(8,128)(2,1)S(1)}, bf16[4,256,128]{2,1,0:T(8,128)(2,1)S(1)}, u32[]{:S(2)}, u32[]{:S(2)}) collective-permute-start(bf16[4,256,128]{2,1,0:T(8,128)(2,1)S(1)} %bitcast.8), channel_id=1, source_target_pairs={{0,4},{1,5},{2,6},{3,7},{4,0},{5,1},{6,2},{7,3},{8,12},{9,13},{10,... | collective-permute-start | bytes 786440 | tf_op jit(solution)/shard_map/ppermute | solution.py:219
  82.7 8.9 %collective-permute-start.12 = (bf16[4,256,128]{2,1,0:T(8,128)(2,1)S(1)}, bf16[4,256,128]{2,1,0:T(8,128)(2,1)S(1)}, u32[]{:S(2)}, u32[]{:S(2)}) collective-permute-start(bf16[4,256,128]{2,1,0:T(8,128)(2,1)S(1)} %bitcast.9), channel_id=1, source_target_pairs={{0,2},{1,3},{2,0},{3,1},{4,6},{5,7},{6,4},{7,5},{8,10},{9,11},{10,... | collective-permute-start | bytes 786440 | tf_op jit(solution)/shard_map/ppermute | solution.py:219
  87.4 9.7 %collective-permute-start.18 = (bf16[4,256,128]{2,1,0:T(8,128)(2,1)S(1)}, bf16[4,256,128]{2,1,0:T(8,128)(2,1)S(1)}, u32[]{:S(2)}, u32[]{:S(2)}) collective-permute-start(bf16[4,256,128]{2,1,0:T(8,128)(2,1)S(1)} %collective-permute-done.17.d6), channel_id=1, source_target_pairs={{0,2},{1,3},{2,0},{3,1},{4,6},{5,7},{6,4},{7,5},{8,10},{9,11},{10,... | collective-permute-start | bytes 786440 | tf_op jit(solution)/shard_map/ppermute | solution.py:219
  89.1 7.6 %collective-permute-start.15 = (bf16[4,256,128]{2,1,0:T(8,128)(2,1)S(1)}, bf16[4,256,128]{2,1,0:T(8,128)(2,1)S(1)}, u32[]{:S(2)}, u32[]{:S(2)}) collective-permute-start(bf16[4,256,128]{2,1,0:T(8,128)(2,1)S(1)} %collective-permute-done.13.d2), channel_id=1, source_target_pairs={{0,12},{1,13},{2,14},{3,15},{4,8},{5,9},{6,10},{7,11},{8,4},{9,5},... | collective-permute-start | bytes 786440 | tf_op jit(solution)/shard_map/ppermute | solution.py:219
  91.6 7.1 %collective-permute-start.14 = (bf16[4,256,128]{2,1,0:T(8,128)(2,1)S(1)}, bf16[4,256,128]{2,1,0:T(8,128)(2,1)S(1)}, u32[]{:S(2)}, u32[]{:S(2)}) collective-permute-start(bf16[4,256,128]{2,1,0:T(8,128)(2,1)S(1)} %collective-permute-done.12.d1), channel_id=1, source_target_pairs={{0,4},{1,5},{2,6},{3,7},{4,0},{5,1},{6,2},{7,3},{8,12},{9,13},{10,... | collective-permute-start | bytes 786440 | tf_op jit(solution)/shard_map/ppermute | solution.py:219
  93.0 7.5 %collective-permute-start.21 = (bf16[2,256,128]{2,1,0:T(8,128)(2,1)S(1)}, bf16[2,256,128]{2,1,0:T(8,128)(2,1)S(1)}, u32[]{:S(2)}, u32[]{:S(2)}) collective-permute-start(bf16[2,256,128]{2,1,0:T(8,128)(2,1)S(1)} %bitcast.13), channel_id=1, source_target_pairs={{0,1},{1,0},{2,3},{3,2},{4,5},{5,4},{6,7},{7,6},{8,9},{9,8},{10,11... | collective-permute-start | bytes 393224 | tf_op jit(solution)/shard_map/ppermute | solution.py:219
  96.7 7.5 %collective-permute-start.16 = (bf16[2,256,128]{2,1,0:T(8,128)(2,1)S(1)}, bf16[2,256,128]{2,1,0:T(8,128)(2,1)S(1)}, u32[]{:S(2)}, u32[]{:S(2)}) collective-permute-start(bf16[2,256,128]{2,1,0:T(8,128)(2,1)S(1)} %slice.49), channel_id=1, source_target_pairs={{0,2},{1,3},{2,0},{3,1},{4,6},{5,7},{6,4},{7,5},{8,10},{9,11},{10,... | collective-permute-start | bytes 393224 | tf_op jit(solution)/shard_map/ppermute | solution.py:219
  97.1 4.4 %collective-permute-start.19 = (bf16[1,256,128]{2,1,0:T(8,128)(2,1)S(1)}, bf16[1,256,128]{2,1,0:T(8,128)(2,1)S(1)}, u32[]{:S(2)}, u32[]{:S(2)}) collective-permute-start(bf16[1,256,128]{2,1,0:T(8,128)(2,1)S(1)} %slice.50), channel_id=1, source_target_pairs={{0,4},{1,5},{2,6},{3,7},{4,0},{5,1},{6,2},{7,3},{8,12},{9,13},{10,... | collective-permute-start | bytes 196616 | tf_op jit(solution)/shard_map/ppermute | solution.py:219
  98.7 5.5 %collective-permute-start.20 = (bf16[1,256,128]{2,1,0:T(8,128)(2,1)S(1)}, bf16[1,256,128]{2,1,0:T(8,128)(2,1)S(1)}, u32[]{:S(2)}, u32[]{:S(2)}) collective-permute-start(bf16[1,256,128]{2,1,0:T(8,128)(2,1)S(1)} %slice.51), channel_id=1, source_target_pairs={{0,12},{1,13},{2,14},{3,15},{4,8},{5,9},{6,10},{7,11},{8,4},{9,5},... | collective-permute-start | bytes 196616 | tf_op jit(solution)/shard_map/ppermute | solution.py:219
  104.1 2.2 %copy-start.1 = (bf16[32,256,256]{2,1,0:T(8,128)(2,1)S(1)}, bf16[32,256,256]{2,1,0:T(8,128)(2,1)}, u32[]{:S(2)}) copy-start(bf16[32,256,256]{2,1,0:T(8,128)(2,1)} %left.3) | copy-start | bytes 12582916
  112.9 2.0 %collective-permute-start.22 = (f32[512,256]{1,0:T(8,128)S(1)}, f32[512,256]{1,0:T(8,128)S(1)}, u32[]{:S(2)}, u32[]{:S(2)}) collective-permute-start(f32[512,256]{1,0:T(8,128)S(1)} %get-tuple-element.33), channel_id=1, source_target_pairs={{0,1},{1,0},{2,3},{3,2},{4,5},{5,4},{6,7},{7,6},{8,9},{9,8},{10,11... | collective-permute-start | bytes 1572872 | tf_op jit(solution)/shard_map/ppermute | solution.py:219
  115.9 18.7 %all-to-all-start.2 = ((bf16[16,32,256]{2,1,0:T(8,128)(2,1)}), bf16[16,32,256]{2,1,0:T(8,128)(2,1)S(1)}, u32[]{:S(2)}, u32[]{:S(2)}) async-start(bf16[16,32,256]{2,1,0:T(8,128)(2,1)} %get-tuple-element.37), calls=%async_computation.2 | async-start | bytes 524288 | tf_op jit(solution)/shard_map/all_to_all | solution.py:230
  121.0 1.2 collective-permute-start.23
  122.2 3.6 %collective-permute-start.24 = (f32[8,128]{1,0:T(8,128)S(1)}, f32[8,128]{1,0:T(8,128)S(1)}, u32[]{:S(2)}, u32[]{:S(2)}) collective-permute-start(f32[8,128]{1,0:T(8,128)S(1)} %add.22), channel_id=1, source_target_pairs={{0,2},{1,3},{2,0},{3,1},{4,6},{5,7},{6,4},{7,5},{8,10},{9,11},{10,... | collective-permute-start | bytes 12296 | tf_op jit(solution)/shard_map/ppermute | solution.py:219
  125.9 3.6 %collective-permute-start.25 = (f32[8,128]{1,0:T(8,128)S(1)}, f32[8,128]{1,0:T(8,128)S(1)}, u32[]{:S(2)}, u32[]{:S(2)}) collective-permute-start(f32[8,128]{1,0:T(8,128)S(1)} %add.23), channel_id=1, source_target_pairs={{0,4},{1,5},{2,6},{3,7},{4,0},{5,1},{6,2},{7,3},{8,12},{9,13},{10,... | collective-permute-start | bytes 12296 | tf_op jit(solution)/shard_map/ppermute | solution.py:219
  129.5 5.1 %collective-permute-start.26 = (f32[8,128]{1,0:T(8,128)S(1)}, f32[8,128]{1,0:T(8,128)S(1)}, u32[]{:S(2)}, u32[]{:S(2)}) collective-permute-start(f32[8,128]{1,0:T(8,128)S(1)} %add.24), channel_id=1, source_target_pairs={{0,8},{1,9},{2,10},{3,11},{4,12},{5,13},{6,14},{7,15},{8,0},{9,1},... | collective-permute-start | bytes 12296 | tf_op jit(solution)/shard_map/ppermute | solution.py:219

commit v4 on v3

--- a/solution.py
+++ b/solution.py
@@ -13,7 +13,7 @@
 HALF = 128
 VMEM = pl.BlockSpec(memory_space=pltpu.VMEM)
 SMEM = pl.BlockSpec(memory_space=pltpu.SMEM)
-HBM = pl.BlockSpec(memory_space=pl.ANY)
+HBM = pl.BlockSpec(memory_space=pltpu.HBM)
 def limit(mib):
     return pltpu.CompilerParams(vmem_limit_bytes=mib * 1024 * 1024)
 
@@ -46,18 +46,17 @@
         out_specs=VMEM,
         out_shape=jax.ShapeDtypeStruct((ops * HALF, 256), BF),
         scratch_shapes=[pltpu.VMEM((ops, 256, HALF), BF), pltpu.SemaphoreType.DMA((ops // GROUP,))],
-        compiler_params=limit(6),
+        compiler_params=limit(3),
         cost_estimate=pl.CostEstimate(flops=0, bytes_accessed=8 * 1024 * 1024, transcendentals=0),
     )(core, right_ops)
 
 
-def ham_kernel(by_block, meta, core_ref, d0, d1, d2, d3, d4, d5a, d5b, d5c, d6, d7, left, right, mine, other, v, lefted, acc):
-    for slot, piece in enumerate((d0, d1, d2, d3, d4, None, d6, d7)):
-        if piece is not None:
-            v[4 * slot : 4 * slot + 4] = piece[...]
-    v[20:22] = d5a[...]
-    v[22:23] = d5b[...]
-    v[23:24] = d5c[...]
+def ham_kernel(by_block, meta, core_ref, *refs):
+    pieces, (left, right, mine, other, v, lefted, acc) = refs[:9], refs[9:]
+    at = 0
+    for piece in pieces:
+        v[at : at + piece.shape[0]] = piece[...]
+        at += piece.shape[0]
     for step in range(left.shape[0] // GROUP):
         for i in range(GROUP):
             k = step * GROUP + i
@@ -76,56 +75,59 @@
             acc[...] += term
     if by_block:
         core = core_ref[0]
-        here = pl.ds(pl.multiple_of(core * HALF, HALF), HALF)
-        there = pl.ds(pl.multiple_of((1 - core) * HALF, HALF), HALF)
-        mine[:, here] = acc[:512, :HALF]
-        mine[:, there] = acc[:512, HALF:]
-        other[:, here] = acc[512:, :HALF]
-        other[:, there] = acc[512:, HALF:]
+        mine[core] = acc[:512, :HALF]
+        mine[1 - core] = acc[:512, HALF:]
+        other[core] = acc[512:, :HALF]
+        other[1 - core] = acc[512:, HALF:]
     else:
         mine[...] = acc[:, :HALF]
         other[...] = acc[:, HALF:]
 
 
 def apply_ham(by_block, meta, core, pieces, left, right):
-    shape = (512, 256) if by_block else (1024, HALF)
+    shape = (2, 512, HALF) if by_block else (1024, HALF)
     return pl.pallas_call(
         functools.partial(ham_kernel, by_block),
         in_specs=[SMEM, SMEM] + [VMEM] * (len(pieces) + 2),
-        out_specs=[VMEM, VMEM],
+        out_specs=[VMEM] * 2,
         out_shape=[jax.ShapeDtypeStruct(shape, F32)] * 2,
         scratch_shapes=[
             pltpu.VMEM((32, 256, HALF), BF),
             pltpu.VMEM((1024, GROUP * HALF), BF),
             pltpu.VMEM((1024, 256), F32),
         ],
-        compiler_params=limit(14),
+        compiler_params=limit(8),
     )(meta, core, *pieces, left, right)
 
 
-def dots_kernel(p, u, out):
+def between_kernel(p, u, left, out, left_out):
     x, y = p[...], u[...].astype(F32)
     lane = lax.broadcasted_iota(jnp.int32, (8, 128), 1)
     rows = jnp.where(lane == 0, jnp.sum(x * x), 0.0)
     rows = jnp.where(lane == 1, jnp.sum(x * y), rows)
     out[...] = jnp.where(lane == 2, jnp.sum(y * y), rows)
-
-
-def dots(p, u):
-    return pl.pallas_call(
-        dots_kernel,
-        in_specs=[VMEM, VMEM],
-        out_specs=VMEM,
-        out_shape=jax.ShapeDtypeStruct((8, 128), F32),
-        compiler_params=limit(4),
-    )(p, u)
+    for k in range(left.shape[0]):
+        left_out[k] = left[k]
+
+
+def between(p, u, left):
+    return pl.pallas_call(
+        between_kernel,
+        in_specs=[VMEM] * 3,
+        out_specs=[VMEM] * 2,
+        out_shape=[jax.ShapeDtypeStruct((8, 128), F32), jax.ShapeDtypeStruct(left.shape, BF)],
+        compiler_params=limit(2),
+    )(p, u, left)
 
 
 def pack_kernel(mine, got, p, u, early, out, stats):
     total = mine[...] + got[...]
-    out[...] = total.astype(BF).reshape(16, 32, 256)
-    pw = jnp.sum(p[...].reshape(512, 256) * total)
-    uw = jnp.sum(u[...].reshape(512, 256).astype(F32) * total)
+    out[...] = total.astype(BF).reshape(16, 64, HALF)
+    pw = uw = 0.0
+    for i in range(2):
+        cols = slice(HALF * i, HALF * (i + 1))
+        pw += jnp.sum(p[:, :, cols].reshape(512, HALF) * total[i])
+        uw += jnp.sum(u[:, :, cols].reshape(512, HALF).astype(F32) * total[i])
     lane = lax.broadcasted_iota(jnp.int32, (8, 128), 1)
     stats[...] = jnp.where(lane == 3, pw, jnp.where(lane == 4, uw, early[...]))
 
@@ -135,8 +137,8 @@
         pack_kernel,
         in_specs=[VMEM] * 5,
         out_specs=[VMEM] * 2,
-        out_shape=[jax.ShapeDtypeStruct((16, 32, 256), BF), jax.ShapeDtypeStruct((8, 128), F32)],
-        compiler_params=limit(4),
+        out_shape=[jax.ShapeDtypeStruct((16, 64, HALF), BF), jax.ShapeDtypeStruct((8, 128), F32)],
+        compiler_params=limit(2),
     )(mine, got, p, u, early)
 
 
@@ -147,18 +149,18 @@
     total = total.astype(BF)
     lane = lax.broadcasted_iota(jnp.int32, (8, 128), 1)
     first_row = lax.broadcasted_iota(jnp.int32, (8, 128), 0) == 0
-    wide = lax.broadcasted_iota(jnp.int32, (16, 256), 1)
-    rows = jnp.zeros((16, 256), F32)
+    wide = lax.broadcasted_iota(jnp.int32, (16, HALF), 1)
+    rows = jnp.zeros((16, HALF), F32)
     for at in range(2):
-        rest = jnp.full((16, 256), jnp.sum(jnp.where(first_row & (lane == 3 + at), stats[...], 0.0)))
+        rest = jnp.full((16, HALF), jnp.sum(jnp.where(first_row & (lane == 3 + at), stats[...], 0.0)))
         for part in range(3):
             term = rest.astype(BF).astype(F32)
             rows = jnp.where(wide == 3 * at + part, term, rows)
             rest = rest - term
     rows = rows.astype(BF)
     for i in range(16):
-        out[i, :32] = total
-        out[i, 32:] = rows
+        out[i, :64] = total
+        out[i, 64:] = rows
 
 
 def relay(parts, stats):
@@ -166,19 +168,19 @@
         relay_kernel,
         in_specs=[VMEM] * 2,
         out_specs=VMEM,
-        out_shape=jax.ShapeDtypeStruct((16, 48, 256), BF),
-        compiler_params=limit(4),
+        out_shape=jax.ShapeDtypeStruct((16, 80, HALF), BF),
+        compiler_params=limit(2),
     )(parts, stats)
 
 
 def finish_kernel(count, stats, whole, p_ref, u_ref, ritz_ref, residual_ref):
-    rows = whole[0, 32:].astype(F32)
+    rows = whole[0, 64:].astype(F32)
     for i in range(1, 16):
-        rows += whole[i, 32:].astype(F32)
+        rows += whole[i, 64:].astype(F32)
     lane = lax.broadcasted_iota(jnp.int32, (8, 128), 1)
     row = lax.broadcasted_iota(jnp.int32, (8, 128), 0)
-    wide = lax.broadcasted_iota(jnp.int32, (16, 256), 1)
-    tall = lax.broadcasted_iota(jnp.int32, (16, 256), 0)
+    wide = lax.broadcasted_iota(jnp.int32, (16, HALF), 1)
+    tall = lax.broadcasted_iota(jnp.int32, (16, HALF), 0)
 
     def scalar(total):
         return jnp.full((1, 256), total / count)
@@ -197,7 +199,8 @@
     one, two = (diag_d - theta) * s, coupling * ts
     block = pl.program_id(0)
     p, u = p_ref[0], u_ref[0].astype(F32)
-    w = whole[pl.ds(8 * block, 8), :32, :].reshape(256, 256).astype(F32)
+    w = [whole[pl.ds(8 * half + 4 * block, 4), :64, :].reshape(256, HALF) for half in range(2)]
+    w = jnp.concatenate(w, axis=1).astype(F32)
     ritz = one * p - two * (u - energy * p)
     ritz_ref[0] = ritz
     residual_ref[0] = one * u - two * (w - energy * u) - theta * ritz
@@ -211,7 +214,7 @@
         in_specs=[VMEM, VMEM, block, block],
         out_specs=[block, block],
         out_shape=[jax.ShapeDtypeStruct(p.shape, F32)] * 2,
-        compiler_params=limit(6),
+        compiler_params=limit(4),
     )(stats, whole, p, u)
 
 
@@ -219,11 +222,15 @@
     return lax.ppermute(x, "qn", [(i, i ^ bits) for i in range(16)])
 
 
+def swap_other_x(x):
+    return lax.ppermute(x, ("op", "qn"), [(i, i ^ (8 * 16 + 2)) for i in range(256)])
+
+
 def gather_chips(own):
-    x1, y1, y3 = swap(own, 2), swap(own, 4), swap(own, 12)
-    x1y1, y2, x1y3 = swap(x1, 4), swap(y1, 12), swap(y3, 2)
-    far = swap(y2[:2], 2), swap(x1y3[2:3], 4), swap(x1y1[3:], 12)
-    return (own, x1, y1, x1y1, y2) + far + (y3, x1y3)
+    x1, y1, y3, y2 = swap(own, 2), swap(own, 4), swap(own, 12), swap(own, 8)
+    x1y1, x1y3 = swap(y1, 2), swap_other_x(y3)
+    x1y2 = swap(y2[:2], 2), swap_other_x(y2[2:])
+    return own, x1, y1, x1y1, y2, *x1y2, y3, x1y3
 
 
 def op_exchange(x):
@@ -261,13 +268,14 @@
     core0 = core[0] == 0
     kept, got = jnp.where(core0, low, high), swap(jnp.where(core0, high, low), 1)
     u = jnp.where(core0, jnp.concatenate([kept, got], 2), jnp.concatenate([got, kept], 2))
-    early = dots(psi_start, u)
-    pieces, u, early = lax.optimization_barrier((pieces, u, early))
-    mine, other = apply_ham(True, own_first, core, pieces, left_ops, right)
+    early, left = between(psi_start, u, left_ops)
+    pieces, u, early, left = lax.optimization_barrier((pieces, u, early, left))
+    mine, other = apply_ham(True, own_first, core, pieces, left, right)
     packed, stats = pack(mine, swap(other, 1), psi_start, u, early)
     parts = op_exchange(packed)
-    for bits in (1, 2, 4, 8):
+    for bits in (1, 2):
         stats = stats + swap(stats, bits)
+    stats = (stats + swap(stats, 8)) + (swap(stats, 4) + swap(stats, 12))
     return tuple(finish(count, stats, op_exchange(relay(parts, stats)), psi_start, u))
 
 

time: 158 us -> 145 us (0.918)
  waiting for transfers between devices: 40.6 us -> 28.2 us
  starting transfers between devices: 32.3 us -> 34.1 us
  blocking collectives: 59.2 us -> 57.6 us
    ppermute x27 -> x22, waiting for transfers between devices: 40.6 us -> 27.1 us  [swap(): return lax.ppermute(x, 'qn', [(i, i ^ bits) for i in range(16)])]
    ppermute x0 -> x4, starting transfers between devices: none -> 8.59 us  [swap_other_x(): lax.ppermute(x, ('op', 'qn'), [(i, i ^ 8 * 16 + 2) for i in range(256)])]
    ppermute x27 -> x22, starting transfers between devices: 27.2 us -> 20.4 us  [swap(): return lax.ppermute(x, 'qn', [(i, i ^ bits) for i in range(16)])]
    all_to_all x3, blocking collectives: 59.2 us -> 57.6 us  [op_exchange(): return lax.all_to_all(x, 'op', 0, 0, tiled=True)]
  transfers between devices with their start and end apart: 28 -> 27, of which waited for: 18 -> 16; matrix products, arithmetic and copies ran while one was open for 1% -> 1% of each run, Pallas kernels for 1% -> 1%
where the time goes in v4:
time: 145 us
  blocking collectives  57.6 us (40%)
  starting transfers between devices  34.1 us (24%)
  waiting for transfers between devices  28.2 us (19%)
  Pallas kernels  17.2 us (12%)
  local copies, waits for them, and re-layouts  4.46 us (3%)
  other arithmetic  2.21 us (2%)
    all_to_all x3, blocking collectives, op_exchange(): return lax.all_to_all(x, 'op', 0, 0, tiled=True)  57.6 us
    ppermute x22, waiting for transfers between devices, swap(): return lax.ppermute(x, 'qn', [(i, i ^ bits) for i in range(16)])  27.1 us
    ppermute x22, starting transfers between devices, swap(): return lax.ppermute(x, 'qn', [(i, i ^ bits) for i in range(16)])  20.4 us
    pallas_call x2, Pallas kernels, apply_ham(): pl.pallas_call(functools.partial(ham_kernel, by_block), in_specs=[SMEM, S...  13.2 us
    ppermute x4, starting transfers between devices, swap_other_x(): lax.ppermute(x, ('op', 'qn'), [(i, i ^ 8 * 16 + 2) for i in range(256)])  8.59 us
    all_to_all x1, starting transfers between devices, op_exchange(): return lax.all_to_all(x, 'op', 0, 0, tiled=True)  5.15 us
    unnamed x8, local copies, waits for them, and re-layouts  4.38 us
  transfers between devices with their start and end apart: 27, of which 16 were waited for; matrix products, arithmetic and copies ran while one was open for 1% of the time, Pallas kernels for 1%

profile of v4, /device:TPU:32, one launch (start us, length us, event | category | flops | bytes accessed | tf_op | source)
XLA Modules:
  0.0 144.7 jit_solution(13896701989663988743)
XLA Ops:
  0.6 1.1 convert.5
  1.9 1.3 collective-permute-done.1
  3.2 3.1 %collective-permute-start.8 = (bf16[4,256,128]{2,1,0:T(8,128)(2,1)S(1)}, bf16[4,256,128]{2,1,0:T(8,128)(2,1)S(1)}, u32[]{:S(2)}, u32[]{:S(2)}) collective-permute-start(bf16[4,256,128]{2,1,0:T(8,128)(2,1)S(1)} %maximum_select_fusion.refs_0_), channel_id=1, source_target_pairs={{0,12},{1,13},{2,14},{3,15},{4,8},{5,9},{6,10},{7,11},{8,4},{9,5},... | collective-permute-start | bytes 786440 | tf_op jit(solution)/shard_map/ppermute | solution.py:222
  6.3 0.1 collective-permute-start.3
  6.5 1.5 %collective-permute-start.5 = (bf16[4,256,128]{2,1,0:T(8,128)(2,1)S(1)}, bf16[4,256,128]{2,1,0:T(8,128)(2,1)S(1)}, u32[]{:S(2)}, u32[]{:S(2)}) collective-permute-start(bf16[4,256,128]{2,1,0:T(8,128)(2,1)S(1)} %maximum_select_fusion.refs_0_), channel_id=1, source_target_pairs={{0,8},{1,9},{2,10},{3,11},{4,12},{5,13},{6,14},{7,15},{8,0},{9,1},... | collective-permute-start | bytes 786440 | tf_op jit(solution)/shard_map/ppermute | solution.py:222
  8.0 0.8 xor_bitcast_fusion
  8.8 1.5 %collective-permute-start.2 = (bf16[4,256,128]{2,1,0:T(8,128)(2,1)S(1)}, bf16[4,256,128]{2,1,0:T(8,128)(2,1)S(1)}, u32[]{:S(2)}, u32[]{:S(2)}) collective-permute-start(bf16[4,256,128]{2,1,0:T(8,128)(2,1)S(1)} %maximum_select_fusion.refs_0_), channel_id=1, source_target_pairs={{0,2},{1,3},{2,0},{3,1},{4,6},{5,7},{6,4},{7,5},{8,10},{9,11},{10,... | collective-permute-start | bytes 786440 | tf_op jit(solution)/shard_map/ppermute | solution.py:222
  10.3 2.6 %collective-permute-done.8.refs_7_ = bf16[4,256,128]{2,1,0:T(8,128)(2,1)S(1)} collective-permute-done((bf16[4,256,128]{2,1,0:T(8,128)(2,1)S(1)}, bf16[4,256,128]{2,1,0:T(8,128)(2,1)S(1)}, u32[]{:S(2)}, u32[]{:S(2)}) %collective-permute-start.8) | collective-permute-done | bytes 262176 | tf_op jit(solution)/shard_map/ppermute | solution.py:222
  12.9 2.8 %collective-permute-start.9 = (bf16[4,256,128]{2,1,0:T(8,128)(2,1)S(1)}, bf16[4,256,128]{2,1,0:T(8,128)(2,1)S(1)}, u32[]{:S(2)}, u32[]{:S(2)}) collective-permute-start(bf16[4,256,128]{2,1,0:T(8,128)(2,1)S(1)} %collective-permute-done.8.refs_7_), channel_id=1, source_target_pairs={{0,130},{1,131},{2,128},{3,129},{4,134},{5,135},{6,132},{7,133},{8... | collective-permute-start | bytes 786440 | tf_op jit(solution)/shard_map/ppermute | solution.py:226
  15.7 1.3 collective-permute-start.4
  17.0 2.8 %collective-permute-done.5.refs_4_ = bf16[4,256,128]{2,1,0:T(8,128)(2,1)S(1)} collective-permute-done((bf16[4,256,128]{2,1,0:T(8,128)(2,1)S(1)}, bf16[4,256,128]{2,1,0:T(8,128)(2,1)S(1)}, u32[]{:S(2)}, u32[]{:S(2)}) %collective-permute-start.5) | collective-permute-done | bytes 262176 | tf_op jit(solution)/shard_map/ppermute | solution.py:222
  19.9 2.8 %collective-permute-start.7 = (bf16[2,256,128]{2,1,0:T(8,128)(2,1)S(1)}, bf16[2,256,128]{2,1,0:T(8,128)(2,1)S(1)}, u32[]{:S(2)}, u32[]{:S(2)}) collective-permute-start(bf16[2,256,128]{2,1,0:T(8,128)(2,1)S(1)} %get-tuple-element.46), channel_id=1, source_target_pairs={{0,130},{1,131},{2,128},{3,129},{4,134},{5,135},{6,132},{7,133},{8... | collective-permute-start | bytes 393224 | tf_op jit(solution)/shard_map/ppermute | solution.py:226
  22.7 0.2 collective-permute-start.6
  22.9 2.2 %copy-done.3 = bf16[32,256,256]{2,1,0:T(8,128)(2,1)S(1)} copy-done((bf16[32,256,256]{2,1,0:T(8,128)(2,1)S(1)}, bf16[32,256,256]{2,1,0:T(8,128)(2,1)}, u32[]{:S(2)}) %copy-start.3) | copy-done | bytes 4194328
  25.1 1.2 shard_map.59.refs_10_
  26.3 1.3 collective-permute-done.6.refs_5_
  27.7 6.6 %shard_map.60 = (f32[1024,128]{1,0:T(8,128)S(1)}, f32[1024,128]{1,0:T(8,128)S(1)}) custom-call(s32[3,4,32]{2,1,0:T(4,128)S(1)} %get-tuple-element.50.meta, s32[1]{0:T(128)} %bitcast.1.core_ref, bf16[4,256,128]{2,1,0:T(8,128)(2,1)S(1)} %maximum_select_fusion.refs_0_, bf16[4,256,128]{2,1,0:T(8,128)(2,1)S(1)} %collective-permute-done.2.refs_1_, ...), custom_call_target="tpu_custom_call" | custom-call | tf_op jit(solution)/shard_map/pallas_call | solution.py:89
  34.4 1.9 %collective-permute-done.10 = f32[1024,128]{1,0:T(8,128)S(1)} collective-permute-done((f32[1024,128]{1,0:T(8,128)S(1)}, f32[1024,128]{1,0:T(8,128)S(1)}, u32[]{:S(2)}, u32[]{:S(2)}) %collective-permute-start.10) | collective-permute-done | bytes 524320 | tf_op jit(solution)/shard_map/ppermute | solution.py:222
  36.3 21.0 %all_to_all.20 = bf16[16,64,128]{2,1,0:T(8,128)(2,1)S(1)} all-to-all(bf16[16,64,128]{2,1,0:T(8,128)(2,1)S(1)} %bitcast.12), channel_id=1, replica_groups=mesh['op'=16,'qn'=16] {'op'}, dimensions={0} | all-to-all | bytes 524288 | tf_op jit(solution)/shard_map/all_to_all | solution.py:237
  57.5 15.8 %all_to_all.21 = bf16[16,64,128]{2,1,0:T(8,128)(2,1)S(1)} all-to-all(bf16[16,64,128]{2,1,0:T(8,128)(2,1)S(1)} %broadcast_in_dim.2), channel_id=1, replica_groups=mesh['op'=16,'qn'=16] {'op'}, dimensions={0} | all-to-all | bytes 524288 | tf_op jit(solution)/shard_map/all_to_all | solution.py:237
  73.3 3.0 %collective-permute-start.17 = (bf16[4,256,128]{2,1,0:T(8,128)(2,1)S(1)}, bf16[4,256,128]{2,1,0:T(8,128)(2,1)S(1)}, u32[]{:S(2)}, u32[]{:S(2)}) collective-permute-start(bf16[4,256,128]{2,1,0:T(8,128)(2,1)S(1)} %bitcast.7), channel_id=1, source_target_pairs={{0,12},{1,13},{2,14},{3,15},{4,8},{5,9},{6,10},{7,11},{8,4},{9,5},... | collective-permute-start | bytes 786440 | tf_op jit(solution)/shard_map/ppermute | solution.py:222
  76.3 1.7 %collective-permute-start.14 = (bf16[4,256,128]{2,1,0:T(8,128)(2,1)S(1)}, bf16[4,256,128]{2,1,0:T(8,128)(2,1)S(1)}, u32[]{:S(2)}, u32[]{:S(2)}) collective-permute-start(bf16[4,256,128]{2,1,0:T(8,128)(2,1)S(1)} %bitcast.9), channel_id=1, source_target_pairs={{0,8},{1,9},{2,10},{3,11},{4,12},{5,13},{6,14},{7,15},{8,0},{9,1},... | collective-permute-start | bytes 786440 | tf_op jit(solution)/shard_map/ppermute | solution.py:222
  78.0 0.7 collective-permute-start.11
  78.8 4.7 %collective-permute-done.17.refs_7_ = bf16[4,256,128]{2,1,0:T(8,128)(2,1)S(1)} collective-permute-done((bf16[4,256,128]{2,1,0:T(8,128)(2,1)S(1)}, bf16[4,256,128]{2,1,0:T(8,128)(2,1)S(1)}, u32[]{:S(2)}, u32[]{:S(2)}) %collective-permute-start.17) | collective-permute-done | bytes 262176 | tf_op jit(solution)/shard_map/ppermute | solution.py:222
  83.5 0.4 collective-permute-start.18
  83.9 0.9 collective-permute-done.12.refs_2_
  84.8 0.6 collective-permute-start.13
  85.4 1.9 %collective-permute-done.14.refs_4_ = bf16[4,256,128]{2,1,0:T(8,128)(2,1)S(1)} collective-permute-done((bf16[4,256,128]{2,1,0:T(8,128)(2,1)S(1)}, bf16[4,256,128]{2,1,0:T(8,128)(2,1)S(1)}, u32[]{:S(2)}, u32[]{:S(2)}) %collective-permute-start.14) | collective-permute-done | bytes 262176 | tf_op jit(solution)/shard_map/ppermute | solution.py:222
  87.4 2.6 %collective-permute-start.16 = (bf16[2,256,128]{2,1,0:T(8,128)(2,1)S(1)}, bf16[2,256,128]{2,1,0:T(8,128)(2,1)S(1)}, u32[]{:S(2)}, u32[]{:S(2)}) collective-permute-start(bf16[2,256,128]{2,1,0:T(8,128)(2,1)S(1)} %get-tuple-element.44), channel_id=1, source_target_pairs={{0,130},{1,131},{2,128},{3,129},{4,134},{5,135},{6,132},{7,133},{8... | collective-permute-start | bytes 393224 | tf_op jit(solution)/shard_map/ppermute | solution.py:226
  89.9 0.1 collective-permute-start.15
  90.2 2.2 %copy-done.1 = bf16[32,256,256]{2,1,0:T(8,128)(2,1)S(1)} copy-done((bf16[32,256,256]{2,1,0:T(8,128)(2,1)S(1)}, bf16[32,256,256]{2,1,0:T(8,128)(2,1)}, u32[]{:S(2)}) %copy-start.1) | copy-done | bytes 4194328
  92.4 0.5 shard_map.61
  92.8 1.0 collective-permute-done.16.refs_6_
  93.9 1.0 collective-permute-done.15.refs_5_
  94.9 6.6 %shard_map.62 = (f32[2,512,128]{2,1,0:T(8,128)S(1)}, f32[2,512,128]{2,1,0:T(8,128)S(1)}) custom-call(s32[3,4,32]{2,1,0:T(4,128)S(1)} %get-tuple-element.51.meta, s32[1]{0:T(128)} %bitcast.1.core_ref, bf16[4,256,128]{2,1,0:T(8,128)(2,1)S(1)} %bitcast.11, bf16[4,256,128]{2,1,0:T(8,128)(2,1)S(1)} %collective-permute-done.11.refs_1_, ...), custom_call_target="tpu_custom_call" | custom-call | tf_op jit(solution)/shard_map/pallas_call | solution.py:89
  101.6 1.9 %collective-permute-done.20.got = f32[2,512,128]{2,1,0:T(8,128)S(1)} collective-permute-done((f32[2,512,128]{2,1,0:T(8,128)S(1)}, f32[2,512,128]{2,1,0:T(8,128)S(1)}, u32[]{:S(2)}, u32[]{:S(2)}) %collective-permute-start.20) | collective-permute-done | bytes 524320 | tf_op jit(solution)/shard_map/ppermute | solution.py:222
  103.5 0.9 shard_map.63
  104.4 5.2 %all-to-all-start.2 = ((bf16[16,64,128]{2,1,0:T(8,128)(2,1)}), bf16[16,64,128]{2,1,0:T(8,128)(2,1)S(1)}, u32[]{:S(2)}, u32[]{:S(2)}) async-start(bf16[16,64,128]{2,1,0:T(8,128)(2,1)} %get-tuple-element.41), calls=%async_computation.2 | async-start | bytes 524288 | tf_op jit(solution)/shard_map/all_to_all | solution.py:237
  109.6 1.2 collective-permute-done.21
  110.7 1.4 collective-permute-start.22
  112.1 2.3 %collective-permute-done.22 = f32[8,128]{1,0:T(8,128)S(1)} collective-permute-done((f32[8,128]{1,0:T(8,128)S(1)}, f32[8,128]{1,0:T(8,128)S(1)}, u32[]{:S(2)}, u32[]{:S(2)}) %collective-permute-start.22) | collective-permute-done | bytes 4128 | tf_op jit(solution)/shard_map/ppermute | solution.py:222
  114.4 2.9 %collective-permute-start.25 = (f32[8,128]{1,0:T(8,128)S(1)}, f32[8,128]{1,0:T(8,128)S(1)}, u32[]{:S(2)}, u32[]{:S(2)}) collective-permute-start(f32[8,128]{1,0:T(8,128)S(1)} %add.26), channel_id=1, source_target_pairs={{0,12},{1,13},{2,14},{3,15},{4,8},{5,9},{6,10},{7,11},{8,4},{9,5},... | collective-permute-start | bytes 12296 | tf_op jit(solution)/shard_map/ppermute | solution.py:222
  117.3 1.8 %collective-permute-start.23 = (f32[8,128]{1,0:T(8,128)S(1)}, f32[8,128]{1,0:T(8,128)S(1)}, u32[]{:S(2)}, u32[]{:S(2)}) collective-permute-start(f32[8,128]{1,0:T(8,128)S(1)} %add.26), channel_id=1, source_target_pairs={{0,8},{1,9},{2,10},{3,11},{4,12},{5,13},{6,14},{7,15},{8,0},{9,1},... | collective-permute-start | bytes 12296 | tf_op jit(solution)/shard_map/ppermute | solution.py:222
  119.2 1.7 %collective-permute-done.24 = f32[8,128]{1,0:T(8,128)S(1)} collective-permute-done((f32[8,128]{1,0:T(8,128)S(1)}, f32[8,128]{1,0:T(8,128)S(1)}, u32[]{:S(2)}, u32[]{:S(2)}) %collective-permute-start.24) | collective-permute-done | bytes 4128 | tf_op jit(solution)/shard_map/ppermute | solution.py:222
  120.9 1.5 %collective-permute-done.23 = f32[8,128]{1,0:T(8,128)S(1)} collective-permute-done((f32[8,128]{1,0:T(8,128)S(1)}, f32[8,128]{1,0:T(8,128)S(1)}, u32[]{:S(2)}, u32[]{:S(2)}) %collective-permute-start.23) | collective-permute-done | bytes 4128 | tf_op jit(solution)/shard_map/ppermute | solution.py:222
  122.4 0.1 shard_map.64
  122.5 20.8 %all_to_all.22.whole = bf16[16,80,128]{2,1,0:T(8,128)(2,1)S(1)} all-to-all(bf16[16,80,128]{2,1,0:T(8,128)(2,1)S(1)} %shard_map.64), channel_id=1, replica_groups=mesh['op'=16,'qn'=16] {'op'}, dimensions={0} | all-to-all | bytes 655360 | tf_op jit(solution)/shard_map/all_to_all | solution.py:237
  143.3 1.4 shard_map.65
  (39 shorter events, 0.9 us)
Async XLA Ops:
  1.7 1.4 collective-permute-start.1
  3.2 9.7 %collective-permute-start.8 = (bf16[4,256,128]{2,1,0:T(8,128)(2,1)S(1)}, bf16[4,256,128]{2,1,0:T(8,128)(2,1)S(1)}, u32[]{:S(2)}, u32[]{:S(2)}) collective-permute-start(bf16[4,256,128]{2,1,0:T(8,128)(2,1)S(1)} %maximum_select_fusion.refs_0_), channel_id=1, source_target_pairs={{0,12},{1,13},{2,14},{3,15},{4,8},{5,9},{6,10},{7,11},{8,4},{9,5},... | collective-permute-start | bytes 786440 | tf_op jit(solution)/shard_map/ppermute | solution.py:222
  6.3 9.4 %collective-permute-start.3 = (bf16[4,256,128]{2,1,0:T(8,128)(2,1)S(1)}, bf16[4,256,128]{2,1,0:T(8,128)(2,1)S(1)}, u32[]{:S(2)}, u32[]{:S(2)}) collective-permute-start(bf16[4,256,128]{2,1,0:T(8,128)(2,1)S(1)} %maximum_select_fusion.refs_0_), channel_id=1, source_target_pairs={{0,4},{1,5},{2,6},{3,7},{4,0},{5,1},{6,2},{7,3},{8,12},{9,13},{10,... | collective-permute-start | bytes 786440 | tf_op jit(solution)/shard_map/ppermute | solution.py:222
  6.5 13.4 %collective-permute-start.5 = (bf16[4,256,128]{2,1,0:T(8,128)(2,1)S(1)}, bf16[4,256,128]{2,1,0:T(8,128)(2,1)S(1)}, u32[]{:S(2)}, u32[]{:S(2)}) collective-permute-start(bf16[4,256,128]{2,1,0:T(8,128)(2,1)S(1)} %maximum_select_fusion.refs_0_), channel_id=1, source_target_pairs={{0,8},{1,9},{2,10},{3,11},{4,12},{5,13},{6,14},{7,15},{8,0},{9,1},... | collective-permute-start | bytes 786440 | tf_op jit(solution)/shard_map/ppermute | solution.py:222
  8.0 19.7 %copy-start = (bf16[32,256,256]{2,1,0:T(8,128)(2,1)S(1)}, bf16[32,256,256]{2,1,0:T(8,128)(2,1)}, u32[]{:S(2)}) copy-start(bf16[32,256,256]{2,1,0:T(8,128)(2,1)} %left.1) | copy-start | bytes 12582916
  8.8 13.9 %collective-permute-start = (s32[3,2,32]{2,1,0:T(2,128)S(1)}, s32[3,2,32]{2,1,0:T(2,128)S(1)}, u32[]{:S(2)}, u32[]{:S(2)}) collective-permute-start(s32[3,2,32]{2,1,0:T(2,128)S(1)} %xor_bitcast_fusion), channel_id=1, source_target_pairs={{0,1},{1,0},{2,3},{3,2},{4,5},{5,4},{6,7},{7,6},{8,9},{9,8},{10,11... | collective-permute-start | bytes 2312 | tf_op jit(solution)/shard_map/ppermute | solution.py:222
  8.8 17.5 %collective-permute-start.2 = (bf16[4,256,128]{2,1,0:T(8,128)(2,1)S(1)}, bf16[4,256,128]{2,1,0:T(8,128)(2,1)S(1)}, u32[]{:S(2)}, u32[]{:S(2)}) collective-permute-start(bf16[4,256,128]{2,1,0:T(8,128)(2,1)S(1)} %maximum_select_fusion.refs_0_), channel_id=1, source_target_pairs={{0,2},{1,3},{2,0},{3,1},{4,6},{5,7},{6,4},{7,5},{8,10},{9,11},{10,... | collective-permute-start | bytes 786440 | tf_op jit(solution)/shard_map/ppermute | solution.py:222
  12.9 14.7 %collective-permute-start.9 = (bf16[4,256,128]{2,1,0:T(8,128)(2,1)S(1)}, bf16[4,256,128]{2,1,0:T(8,128)(2,1)S(1)}, u32[]{:S(2)}, u32[]{:S(2)}) collective-permute-start(bf16[4,256,128]{2,1,0:T(8,128)(2,1)S(1)} %collective-permute-done.8.refs_7_), channel_id=1, source_target_pairs={{0,130},{1,131},{2,128},{3,129},{4,134},{5,135},{6,132},{7,133},{8... | collective-permute-start | bytes 786440 | tf_op jit(solution)/shard_map/ppermute | solution.py:226
  15.7 12.0 %collective-permute-start.4 = (bf16[4,256,128]{2,1,0:T(8,128)(2,1)S(1)}, bf16[4,256,128]{2,1,0:T(8,128)(2,1)S(1)}, u32[]{:S(2)}, u32[]{:S(2)}) collective-permute-start(bf16[4,256,128]{2,1,0:T(8,128)(2,1)S(1)} %collective-permute-done.3.refs_2_), channel_id=1, source_target_pairs={{0,2},{1,3},{2,0},{3,1},{4,6},{5,7},{6,4},{7,5},{8,10},{9,11},{10,... | collective-permute-start | bytes 786440 | tf_op jit(solution)/shard_map/ppermute | solution.py:222
  19.9 6.5 %collective-permute-start.7 = (bf16[2,256,128]{2,1,0:T(8,128)(2,1)S(1)}, bf16[2,256,128]{2,1,0:T(8,128)(2,1)S(1)}, u32[]{:S(2)}, u32[]{:S(2)}) collective-permute-start(bf16[2,256,128]{2,1,0:T(8,128)(2,1)S(1)} %get-tuple-element.46), channel_id=1, source_target_pairs={{0,130},{1,131},{2,128},{3,129},{4,134},{5,135},{6,132},{7,133},{8... | collective-permute-start | bytes 393224 | tf_op jit(solution)/shard_map/ppermute | solution.py:226
  22.7 5.0 %collective-permute-start.6 = (bf16[2,256,128]{2,1,0:T(8,128)(2,1)S(1)}, bf16[2,256,128]{2,1,0:T(8,128)(2,1)S(1)}, u32[]{:S(2)}, u32[]{:S(2)}) collective-permute-start(bf16[2,256,128]{2,1,0:T(8,128)(2,1)S(1)} %get-tuple-element.47), channel_id=1, source_target_pairs={{0,2},{1,3},{2,0},{3,1},{4,6},{5,7},{6,4},{7,5},{8,10},{9,11},{10,... | collective-permute-start | bytes 393224 | tf_op jit(solution)/shard_map/ppermute | solution.py:222
  22.9 2.2 %copy-start.3 = (bf16[32,256,256]{2,1,0:T(8,128)(2,1)S(1)}, bf16[32,256,256]{2,1,0:T(8,128)(2,1)}, u32[]{:S(2)}) copy-start(bf16[32,256,256]{2,1,0:T(8,128)(2,1)} %r_ref.1) | copy-start | bytes 12582916
  34.3 55.9 %copy-start.2 = (f32[2,256,256]{2,1,0:T(8,128)S(1)}, f32[2,256,256]{2,1,0:T(8,128)}, u32[]{:S(2)}) copy-start(f32[2,256,256]{2,1,0:T(8,128)} %p_ref.1) | copy-start | bytes 1572868
  34.3 2.0 %collective-permute-start.10 = (f32[1024,128]{1,0:T(8,128)S(1)}, f32[1024,128]{1,0:T(8,128)S(1)}, u32[]{:S(2)}, u32[]{:S(2)}) collective-permute-start(f32[1024,128]{1,0:T(8,128)S(1)} %get-tuple-element.23), channel_id=1, source_target_pairs={{0,1},{1,0},{2,3},{3,2},{4,5},{5,4},{6,7},{7,6},{8,9},{9,8},{10,11... | collective-permute-start | bytes 1572872 | tf_op jit(solution)/shard_map/ppermute | solution.py:222
  73.3 10.2 %collective-permute-start.17 = (bf16[4,256,128]{2,1,0:T(8,128)(2,1)S(1)}, bf16[4,256,128]{2,1,0:T(8,128)(2,1)S(1)}, u32[]{:S(2)}, u32[]{:S(2)}) collective-permute-start(bf16[4,256,128]{2,1,0:T(8,128)(2,1)S(1)} %bitcast.7), channel_id=1, source_target_pairs={{0,12},{1,13},{2,14},{3,15},{4,8},{5,9},{6,10},{7,11},{8,4},{9,5},... | collective-permute-start | bytes 786440 | tf_op jit(solution)/shard_map/ppermute | solution.py:222
  76.3 8.5 %collective-permute-start.12 = (bf16[4,256,128]{2,1,0:T(8,128)(2,1)S(1)}, bf16[4,256,128]{2,1,0:T(8,128)(2,1)S(1)}, u32[]{:S(2)}, u32[]{:S(2)}) collective-permute-start(bf16[4,256,128]{2,1,0:T(8,128)(2,1)S(1)} %bitcast.8), channel_id=1, source_target_pairs={{0,4},{1,5},{2,6},{3,7},{4,0},{5,1},{6,2},{7,3},{8,12},{9,13},{10,... | collective-permute-start | bytes 786440 | tf_op jit(solution)/shard_map/ppermute | solution.py:222
  76.3 11.0 %collective-permute-start.14 = (bf16[4,256,128]{2,1,0:T(8,128)(2,1)S(1)}, bf16[4,256,128]{2,1,0:T(8,128)(2,1)S(1)}, u32[]{:S(2)}, u32[]{:S(2)}) collective-permute-start(bf16[4,256,128]{2,1,0:T(8,128)(2,1)S(1)} %bitcast.9), channel_id=1, source_target_pairs={{0,8},{1,9},{2,10},{3,11},{4,12},{5,13},{6,14},{7,15},{8,0},{9,1},... | collective-permute-start | bytes 786440 | tf_op jit(solution)/shard_map/ppermute | solution.py:222
  78.0 14.9 %collective-permute-start.11 = (bf16[4,256,128]{2,1,0:T(8,128)(2,1)S(1)}, bf16[4,256,128]{2,1,0:T(8,128)(2,1)S(1)}, u32[]{:S(2)}, u32[]{:S(2)}) collective-permute-start(bf16[4,256,128]{2,1,0:T(8,128)(2,1)S(1)} %bitcast.10), channel_id=1, source_target_pairs={{0,2},{1,3},{2,0},{3,1},{4,6},{5,7},{6,4},{7,5},{8,10},{9,11},{10,... | collective-permute-start | bytes 786440 | tf_op jit(solution)/shard_map/ppermute | solution.py:222
  78.7 11.2 %collective-permute-start.19 = (bf16[2,256,128]{2,1,0:T(8,128)(2,1)S(1)}, bf16[2,256,128]{2,1,0:T(8,128)(2,1)S(1)}, u32[]{:S(2)}, u32[]{:S(2)}) collective-permute-start(bf16[2,256,128]{2,1,0:T(8,128)(2,1)S(1)} %bitcast.14), channel_id=1, source_target_pairs={{0,1},{1,0},{2,3},{3,2},{4,5},{5,4},{6,7},{7,6},{8,9},{9,8},{10,11... | collective-permute-start | bytes 393224 | tf_op jit(solution)/shard_map/ppermute | solution.py:222
  83.5 11.4 %collective-permute-start.18 = (bf16[4,256,128]{2,1,0:T(8,128)(2,1)S(1)}, bf16[4,256,128]{2,1,0:T(8,128)(2,1)S(1)}, u32[]{:S(2)}, u32[]{:S(2)}) collective-permute-start(bf16[4,256,128]{2,1,0:T(8,128)(2,1)S(1)} %collective-permute-done.17.refs_7_), channel_id=1, source_target_pairs={{0,130},{1,131},{2,128},{3,129},{4,134},{5,135},{6,132},{7,133},{8... | collective-permute-start | bytes 786440 | tf_op jit(solution)/shard_map/ppermute | solution.py:226
  84.8 10.1 %collective-permute-start.13 = (bf16[4,256,128]{2,1,0:T(8,128)(2,1)S(1)}, bf16[4,256,128]{2,1,0:T(8,128)(2,1)S(1)}, u32[]{:S(2)}, u32[]{:S(2)}) collective-permute-start(bf16[4,256,128]{2,1,0:T(8,128)(2,1)S(1)} %collective-permute-done.12.refs_2_), channel_id=1, source_target_pairs={{0,2},{1,3},{2,0},{3,1},{4,6},{5,7},{6,4},{7,5},{8,10},{9,11},{10,... | collective-permute-start | bytes 786440 | tf_op jit(solution)/shard_map/ppermute | solution.py:222
  87.4 6.5 %collective-permute-start.16 = (bf16[2,256,128]{2,1,0:T(8,128)(2,1)S(1)}, bf16[2,256,128]{2,1,0:T(8,128)(2,1)S(1)}, u32[]{:S(2)}, u32[]{:S(2)}) collective-permute-start(bf16[2,256,128]{2,1,0:T(8,128)(2,1)S(1)} %get-tuple-element.44), channel_id=1, source_target_pairs={{0,130},{1,131},{2,128},{3,129},{4,134},{5,135},{6,132},{7,133},{8... | collective-permute-start | bytes 393224 | tf_op jit(solution)/shard_map/ppermute | solution.py:226
  89.9 5.0 %collective-permute-start.15 = (bf16[2,256,128]{2,1,0:T(8,128)(2,1)S(1)}, bf16[2,256,128]{2,1,0:T(8,128)(2,1)S(1)}, u32[]{:S(2)}, u32[]{:S(2)}) collective-permute-start(bf16[2,256,128]{2,1,0:T(8,128)(2,1)S(1)} %get-tuple-element.45), channel_id=1, source_target_pairs={{0,2},{1,3},{2,0},{3,1},{4,6},{5,7},{6,4},{7,5},{8,10},{9,11},{10,... | collective-permute-start | bytes 393224 | tf_op jit(solution)/shard_map/ppermute | solution.py:222
  90.2 2.2 %copy-start.1 = (bf16[32,256,256]{2,1,0:T(8,128)(2,1)S(1)}, bf16[32,256,256]{2,1,0:T(8,128)(2,1)}, u32[]{:S(2)}) copy-start(bf16[32,256,256]{2,1,0:T(8,128)(2,1)} %left.1) | copy-start | bytes 12582916
  101.5 2.0 %collective-permute-start.20 = (f32[2,512,128]{2,1,0:T(8,128)S(1)}, f32[2,512,128]{2,1,0:T(8,128)S(1)}, u32[]{:S(2)}, u32[]{:S(2)}) collective-permute-start(f32[2,512,128]{2,1,0:T(8,128)S(1)} %get-tuple-element.37), channel_id=1, source_target_pairs={{0,1},{1,0},{2,3},{3,2},{4,5},{5,4},{6,7},{7,6},{8,9},{9,8},{10,11... | collective-permute-start | bytes 1572872 | tf_op jit(solution)/shard_map/ppermute | solution.py:222
  104.4 18.0 %all-to-all-start.2 = ((bf16[16,64,128]{2,1,0:T(8,128)(2,1)}), bf16[16,64,128]{2,1,0:T(8,128)(2,1)S(1)}, u32[]{:S(2)}, u32[]{:S(2)}) async-start(bf16[16,64,128]{2,1,0:T(8,128)(2,1)} %get-tuple-element.41), calls=%async_computation.2 | async-start | bytes 524288 | tf_op jit(solution)/shard_map/all_to_all | solution.py:237
  109.6 1.2 collective-permute-start.21
  110.7 3.6 %collective-permute-start.22 = (f32[8,128]{1,0:T(8,128)S(1)}, f32[8,128]{1,0:T(8,128)S(1)}, u32[]{:S(2)}, u32[]{:S(2)}) collective-permute-start(f32[8,128]{1,0:T(8,128)S(1)} %add.25), channel_id=1, source_target_pairs={{0,2},{1,3},{2,0},{3,1},{4,6},{5,7},{6,4},{7,5},{8,10},{9,11},{10,... | collective-permute-start | bytes 12296 | tf_op jit(solution)/shard_map/ppermute | solution.py:222
  114.4 4.8 %collective-permute-start.25 = (f32[8,128]{1,0:T(8,128)S(1)}, f32[8,128]{1,0:T(8,128)S(1)}, u32[]{:S(2)}, u32[]{:S(2)}) collective-permute-start(f32[8,128]{1,0:T(8,128)S(1)} %add.26), channel_id=1, source_target_pairs={{0,12},{1,13},{2,14},{3,15},{4,8},{5,9},{6,10},{7,11},{8,4},{9,5},... | collective-permute-start | bytes 12296 | tf_op jit(solution)/shard_map/ppermute | solution.py:222
  117.3 3.6 %collective-permute-start.24 = (f32[8,128]{1,0:T(8,128)S(1)}, f32[8,128]{1,0:T(8,128)S(1)}, u32[]{:S(2)}, u32[]{:S(2)}) collective-permute-start(f32[8,128]{1,0:T(8,128)S(1)} %add.26), channel_id=1, source_target_pairs={{0,4},{1,5},{2,6},{3,7},{4,0},{5,1},{6,2},{7,3},{8,12},{9,13},{10,... | collective-permute-start | bytes 12296 | tf_op jit(solution)/shard_map/ppermute | solution.py:222
  117.3 5.1 %collective-permute-start.23 = (f32[8,128]{1,0:T(8,128)S(1)}, f32[8,128]{1,0:T(8,128)S(1)}, u32[]{:S(2)}, u32[]{:S(2)}) collective-permute-start(f32[8,128]{1,0:T(8,128)S(1)} %add.26), channel_id=1, source_target_pairs={{0,8},{1,9},{2,10},{3,11},{4,12},{5,13},{6,14},{7,15},{8,0},{9,1},... | collective-permute-start | bytes 12296 | tf_op jit(solution)/shard_map/ppermute | solution.py:222

commit v5 on v4

--- a/solution.py
+++ b/solution.py
@@ -9,7 +9,7 @@
 
 epsilon = 1e-06
 BF, F32 = jnp.bfloat16, jnp.float32
-GROUP = 8
+GROUP = 4
 HALF = 128
 VMEM = pl.BlockSpec(memory_space=pltpu.VMEM)
 SMEM = pl.BlockSpec(memory_space=pltpu.SMEM)
@@ -122,7 +122,7 @@
 
 def pack_kernel(mine, got, p, u, early, out, stats):
     total = mine[...] + got[...]
-    out[...] = total.astype(BF).reshape(16, 64, HALF)
+    out[...] = total.reshape(16, 64, HALF)
     pw = uw = 0.0
     for i in range(2):
         cols = slice(HALF * i, HALF * (i + 1))
@@ -137,15 +137,15 @@
         pack_kernel,
         in_specs=[VMEM] * 5,
         out_specs=[VMEM] * 2,
-        out_shape=[jax.ShapeDtypeStruct((16, 64, HALF), BF), jax.ShapeDtypeStruct((8, 128), F32)],
+        out_shape=[jax.ShapeDtypeStruct((16, 64, HALF), F32), jax.ShapeDtypeStruct((8, 128), F32)],
         compiler_params=limit(2),
     )(mine, got, p, u, early)
 
 
 def relay_kernel(parts, stats, out):
-    total = parts[0].astype(F32)
+    total = parts[0]
     for i in range(1, 16):
-        total += parts[i].astype(F32)
+        total += parts[i]
     total = total.astype(BF)
     lane = lax.broadcasted_iota(jnp.int32, (8, 128), 1)
     first_row = lax.broadcasted_iota(jnp.int32, (8, 128), 0) == 0
@@ -273,8 +273,7 @@
     mine, other = apply_ham(True, own_first, core, pieces, left, right)
     packed, stats = pack(mine, swap(other, 1), psi_start, u, early)
     parts = op_exchange(packed)
-    for bits in (1, 2):
-        stats = stats + swap(stats, bits)
+    stats = (stats + swap(stats, 1)) + (swap(stats, 2) + swap(stats, 3))
     stats = (stats + swap(stats, 8)) + (swap(stats, 4) + swap(stats, 12))
     return tuple(finish(count, stats, op_exchange(relay(parts, stats)), psi_start, u))
 

time: 145 us -> 146 us (level)
  waiting for transfers between devices: 28.2 us -> 31 us
  blocking collectives: 57.6 us -> 55 us
    all_to_all x1, waiting for transfers between devices: 0.01 us -> 4.12 us  [op_exchange(): return lax.all_to_all(x, 'op', 0, 0, tiled=True)]
    all_to_all x3, blocking collectives: 57.6 us -> 55 us  [op_exchange(): return lax.all_to_all(x, 'op', 0, 0, tiled=True)]
    ppermute x22 -> x23, waiting for transfers between devices: 27.1 us -> 25.8 us  [swap(): return lax.ppermute(x, 'qn', [(i, i ^ bits) for i in range(16)])]
    ppermute x22 -> x23, starting transfers between devices: 20.4 us -> 21 us  [swap(): return lax.ppermute(x, 'qn', [(i, i ^ bits) for i in range(16)])]
  transfers between devices with their start and end apart: 27 -> 28, of which waited for: 16 -> 17; matrix products, arithmetic and copies ran while one was open for 1% -> 1% of each run, Pallas kernels for 1% -> 1%
where the time goes in v5:
time: 146 us; the launch traced here: 145 us
  blocking collectives  55 us (38%)
  starting transfers between devices  34.7 us (24%)
  waiting for transfers between devices  31 us (21%)
  Pallas kernels  17 us (12%)
  local copies, waits for them, and re-layouts  4.46 us (3%)
  other arithmetic  2.21 us (2%)
    all_to_all x3, blocking collectives, op_exchange(): return lax.all_to_all(x, 'op', 0, 0, tiled=True)  55 us
    ppermute x23, waiting for transfers between devices, swap(): return lax.ppermute(x, 'qn', [(i, i ^ bits) for i in range(16)])  25.8 us
    ppermute x23, starting transfers between devices, swap(): return lax.ppermute(x, 'qn', [(i, i ^ bits) for i in range(16)])  21 us
    pallas_call x2, Pallas kernels, apply_ham(): pl.pallas_call(functools.partial(ham_kernel, by_block), in_specs=[SMEM, S...  12.7 us
    ppermute x4, starting transfers between devices, swap_other_x(): lax.ppermute(x, ('op', 'qn'), [(i, i ^ 8 * 16 + 2) for i in range(256)])  8.59 us
    all_to_all x1, starting transfers between devices, op_exchange(): return lax.all_to_all(x, 'op', 0, 0, tiled=True)  5.15 us
    unnamed x8, local copies, waits for them, and re-layouts  4.38 us
    all_to_all x1, waiting for transfers between devices, op_exchange(): return lax.all_to_all(x, 'op', 0, 0, tiled=True)  4.12 us
  transfers between devices with their start and end apart: 28, of which 17 were waited for; matrix products, arithmetic and copies ran while one was open for 1% of the time, Pallas kernels for 1%

profile of v5, /device:TPU:32, one launch (start us, length us, event | category | flops | bytes accessed | tf_op | source)
XLA Modules:
  0.0 145.2 jit_solution(9650874286826598764)
XLA Ops:
  0.6 1.1 convert.5
  1.9 1.3 collective-permute-done.1
  3.2 3.1 %collective-permute-start.8 = (bf16[4,256,128]{2,1,0:T(8,128)(2,1)S(1)}, bf16[4,256,128]{2,1,0:T(8,128)(2,1)S(1)}, u32[]{:S(2)}, u32[]{:S(2)}) collective-permute-start(bf16[4,256,128]{2,1,0:T(8,128)(2,1)S(1)} %maximum_select_fusion.refs_0_), channel_id=1, source_target_pairs={{0,12},{1,13},{2,14},{3,15},{4,8},{5,9},{6,10},{7,11},{8,4},{9,5},... | collective-permute-start | bytes 786440 | tf_op jit(solution)/shard_map/ppermute | solution.py:222
  6.5 1.5 %collective-permute-start.5 = (bf16[4,256,128]{2,1,0:T(8,128)(2,1)S(1)}, bf16[4,256,128]{2,1,0:T(8,128)(2,1)S(1)}, u32[]{:S(2)}, u32[]{:S(2)}) collective-permute-start(bf16[4,256,128]{2,1,0:T(8,128)(2,1)S(1)} %maximum_select_fusion.refs_0_), channel_id=1, source_target_pairs={{0,8},{1,9},{2,10},{3,11},{4,12},{5,13},{6,14},{7,15},{8,0},{9,1},... | collective-permute-start | bytes 786440 | tf_op jit(solution)/shard_map/ppermute | solution.py:222
  8.0 0.8 xor_bitcast_fusion
  8.8 1.5 %collective-permute-start.2 = (bf16[4,256,128]{2,1,0:T(8,128)(2,1)S(1)}, bf16[4,256,128]{2,1,0:T(8,128)(2,1)S(1)}, u32[]{:S(2)}, u32[]{:S(2)}) collective-permute-start(bf16[4,256,128]{2,1,0:T(8,128)(2,1)S(1)} %maximum_select_fusion.refs_0_), channel_id=1, source_target_pairs={{0,2},{1,3},{2,0},{3,1},{4,6},{5,7},{6,4},{7,5},{8,10},{9,11},{10,... | collective-permute-start | bytes 786440 | tf_op jit(solution)/shard_map/ppermute | solution.py:222
  10.3 2.6 %collective-permute-done.8.refs_7_ = bf16[4,256,128]{2,1,0:T(8,128)(2,1)S(1)} collective-permute-done((bf16[4,256,128]{2,1,0:T(8,128)(2,1)S(1)}, bf16[4,256,128]{2,1,0:T(8,128)(2,1)S(1)}, u32[]{:S(2)}, u32[]{:S(2)}) %collective-permute-start.8) | collective-permute-done | bytes 262176 | tf_op jit(solution)/shard_map/ppermute | solution.py:222
  12.9 2.8 %collective-permute-start.9 = (bf16[4,256,128]{2,1,0:T(8,128)(2,1)S(1)}, bf16[4,256,128]{2,1,0:T(8,128)(2,1)S(1)}, u32[]{:S(2)}, u32[]{:S(2)}) collective-permute-start(bf16[4,256,128]{2,1,0:T(8,128)(2,1)S(1)} %collective-permute-done.8.refs_7_), channel_id=1, source_target_pairs={{0,130},{1,131},{2,128},{3,129},{4,134},{5,135},{6,132},{7,133},{8... | collective-permute-start | bytes 786440 | tf_op jit(solution)/shard_map/ppermute | solution.py:226
  15.7 1.3 collective-permute-start.4
  17.0 2.8 %collective-permute-done.5.refs_4_ = bf16[4,256,128]{2,1,0:T(8,128)(2,1)S(1)} collective-permute-done((bf16[4,256,128]{2,1,0:T(8,128)(2,1)S(1)}, bf16[4,256,128]{2,1,0:T(8,128)(2,1)S(1)}, u32[]{:S(2)}, u32[]{:S(2)}) %collective-permute-start.5) | collective-permute-done | bytes 262176 | tf_op jit(solution)/shard_map/ppermute | solution.py:222
  19.9 2.8 %collective-permute-start.7 = (bf16[2,256,128]{2,1,0:T(8,128)(2,1)S(1)}, bf16[2,256,128]{2,1,0:T(8,128)(2,1)S(1)}, u32[]{:S(2)}, u32[]{:S(2)}) collective-permute-start(bf16[2,256,128]{2,1,0:T(8,128)(2,1)S(1)} %get-tuple-element.46), channel_id=1, source_target_pairs={{0,130},{1,131},{2,128},{3,129},{4,134},{5,135},{6,132},{7,133},{8... | collective-permute-start | bytes 393224 | tf_op jit(solution)/shard_map/ppermute | solution.py:226
  22.7 0.2 collective-permute-start.6
  22.9 2.2 %copy-done.3 = bf16[32,256,256]{2,1,0:T(8,128)(2,1)S(1)} copy-done((bf16[32,256,256]{2,1,0:T(8,128)(2,1)S(1)}, bf16[32,256,256]{2,1,0:T(8,128)(2,1)}, u32[]{:S(2)}) %copy-start.3) | copy-done | bytes 4194328
  25.1 1.4 shard_map.59.refs_10_
  26.6 1.1 collective-permute-done.6.refs_5_
  27.7 6.3 %shard_map.60 = (f32[1024,128]{1,0:T(8,128)S(1)}, f32[1024,128]{1,0:T(8,128)S(1)}) custom-call(s32[3,4,32]{2,1,0:T(4,128)S(1)} %get-tuple-element.50.meta, s32[1]{0:T(128)} %bitcast.1.core_ref, bf16[4,256,128]{2,1,0:T(8,128)(2,1)S(1)} %maximum_select_fusion.refs_0_, bf16[4,256,128]{2,1,0:T(8,128)(2,1)S(1)} %collective-permute-done.2.refs_1_, ...), custom_call_target="tpu_custom_call" | custom-call | tf_op jit(solution)/shard_map/pallas_call | solution.py:89
  34.1 1.9 %collective-permute-done.10 = f32[1024,128]{1,0:T(8,128)S(1)} collective-permute-done((f32[1024,128]{1,0:T(8,128)S(1)}, f32[1024,128]{1,0:T(8,128)S(1)}, u32[]{:S(2)}, u32[]{:S(2)}) %collective-permute-start.10) | collective-permute-done | bytes 524320 | tf_op jit(solution)/shard_map/ppermute | solution.py:222
  36.1 21.0 %all_to_all.20 = bf16[16,64,128]{2,1,0:T(8,128)(2,1)S(1)} all-to-all(bf16[16,64,128]{2,1,0:T(8,128)(2,1)S(1)} %bitcast.12), channel_id=1, replica_groups=mesh['op'=16,'qn'=16] {'op'}, dimensions={0} | all-to-all | bytes 524288 | tf_op jit(solution)/shard_map/all_to_all | solution.py:237
  57.2 15.8 %all_to_all.21 = bf16[16,64,128]{2,1,0:T(8,128)(2,1)S(1)} all-to-all(bf16[16,64,128]{2,1,0:T(8,128)(2,1)S(1)} %broadcast_in_dim.2), channel_id=1, replica_groups=mesh['op'=16,'qn'=16] {'op'}, dimensions={0} | all-to-all | bytes 524288 | tf_op jit(solution)/shard_map/all_to_all | solution.py:237
  73.0 3.0 %collective-permute-start.17 = (bf16[4,256,128]{2,1,0:T(8,128)(2,1)S(1)}, bf16[4,256,128]{2,1,0:T(8,128)(2,1)S(1)}, u32[]{:S(2)}, u32[]{:S(2)}) collective-permute-start(bf16[4,256,128]{2,1,0:T(8,128)(2,1)S(1)} %bitcast.7), channel_id=1, source_target_pairs={{0,12},{1,13},{2,14},{3,15},{4,8},{5,9},{6,10},{7,11},{8,4},{9,5},... | collective-permute-start | bytes 786440 | tf_op jit(solution)/shard_map/ppermute | solution.py:222
  76.0 1.7 %collective-permute-start.14 = (bf16[4,256,128]{2,1,0:T(8,128)(2,1)S(1)}, bf16[4,256,128]{2,1,0:T(8,128)(2,1)S(1)}, u32[]{:S(2)}, u32[]{:S(2)}) collective-permute-start(bf16[4,256,128]{2,1,0:T(8,128)(2,1)S(1)} %bitcast.9), channel_id=1, source_target_pairs={{0,8},{1,9},{2,10},{3,11},{4,12},{5,13},{6,14},{7,15},{8,0},{9,1},... | collective-permute-start | bytes 786440 | tf_op jit(solution)/shard_map/ppermute | solution.py:222
  77.7 0.7 collective-permute-start.11
  78.6 4.7 %collective-permute-done.17.refs_7_ = bf16[4,256,128]{2,1,0:T(8,128)(2,1)S(1)} collective-permute-done((bf16[4,256,128]{2,1,0:T(8,128)(2,1)S(1)}, bf16[4,256,128]{2,1,0:T(8,128)(2,1)S(1)}, u32[]{:S(2)}, u32[]{:S(2)}) %collective-permute-start.17) | collective-permute-done | bytes 262176 | tf_op jit(solution)/shard_map/ppermute | solution.py:222
  83.3 0.4 collective-permute-start.18
  83.7 0.9 collective-permute-done.12.refs_2_
  84.5 0.6 collective-permute-start.13
  85.1 1.9 %collective-permute-done.14.refs_4_ = bf16[4,256,128]{2,1,0:T(8,128)(2,1)S(1)} collective-permute-done((bf16[4,256,128]{2,1,0:T(8,128)(2,1)S(1)}, bf16[4,256,128]{2,1,0:T(8,128)(2,1)S(1)}, u32[]{:S(2)}, u32[]{:S(2)}) %collective-permute-start.14) | collective-permute-done | bytes 262176 | tf_op jit(solution)/shard_map/ppermute | solution.py:222
  87.1 2.6 %collective-permute-start.16 = (bf16[2,256,128]{2,1,0:T(8,128)(2,1)S(1)}, bf16[2,256,128]{2,1,0:T(8,128)(2,1)S(1)}, u32[]{:S(2)}, u32[]{:S(2)}) collective-permute-start(bf16[2,256,128]{2,1,0:T(8,128)(2,1)S(1)} %get-tuple-element.44), channel_id=1, source_target_pairs={{0,130},{1,131},{2,128},{3,129},{4,134},{5,135},{6,132},{7,133},{8... | collective-permute-start | bytes 393224 | tf_op jit(solution)/shard_map/ppermute | solution.py:226
  89.9 2.2 %copy-done.1 = bf16[32,256,256]{2,1,0:T(8,128)(2,1)S(1)} copy-done((bf16[32,256,256]{2,1,0:T(8,128)(2,1)S(1)}, bf16[32,256,256]{2,1,0:T(8,128)(2,1)}, u32[]{:S(2)}) %copy-start.1) | copy-done | bytes 4194328
  92.1 0.5 shard_map.61
  92.6 1.1 collective-permute-done.16.refs_6_
  93.6 1.0 collective-permute-done.15.refs_5_
  94.6 6.4 %shard_map.62 = (f32[2,512,128]{2,1,0:T(8,128)S(1)}, f32[2,512,128]{2,1,0:T(8,128)S(1)}) custom-call(s32[3,4,32]{2,1,0:T(4,128)S(1)} %get-tuple-element.51.meta, s32[1]{0:T(128)} %bitcast.1.core_ref, bf16[4,256,128]{2,1,0:T(8,128)(2,1)S(1)} %bitcast.11, bf16[4,256,128]{2,1,0:T(8,128)(2,1)S(1)} %collective-permute-done.11.refs_1_, ...), custom_call_target="tpu_custom_call" | custom-call | tf_op jit(solution)/shard_map/pallas_call | solution.py:89
  101.1 1.9 %collective-permute-done.20.got = f32[2,512,128]{2,1,0:T(8,128)S(1)} collective-permute-done((f32[2,512,128]{2,1,0:T(8,128)S(1)}, f32[2,512,128]{2,1,0:T(8,128)S(1)}, u32[]{:S(2)}, u32[]{:S(2)}) %collective-permute-start.20) | collective-permute-done | bytes 524320 | tf_op jit(solution)/shard_map/ppermute | solution.py:222
  103.0 1.0 shard_map.63
  104.0 5.2 %all-to-all-start.2 = ((f32[16,64,128]{2,1,0:T(8,128)}), f32[16,64,128]{2,1,0:T(8,128)S(1)}, u32[]{:S(2)}, u32[]{:S(2)}) async-start(f32[16,64,128]{2,1,0:T(8,128)} %get-tuple-element.41), calls=%async_computation.2 | async-start | bytes 1048576 | tf_op jit(solution)/shard_map/all_to_all | solution.py:237
  109.1 0.5 collective-permute-start.23
  109.7 0.9 collective-permute-start.22
  110.6 0.4 collective-permute-start.21
  111.0 1.2 collective-permute-done.23
  112.2 1.1 collective-permute-done.22
  113.3 3.0 %collective-permute-start.26 = (f32[8,128]{1,0:T(8,128)S(1)}, f32[8,128]{1,0:T(8,128)S(1)}, u32[]{:S(2)}, u32[]{:S(2)}) collective-permute-start(f32[8,128]{1,0:T(8,128)S(1)} %add_add_fusion.1), channel_id=1, source_target_pairs={{0,12},{1,13},{2,14},{3,15},{4,8},{5,9},{6,10},{7,11},{8,4},{9,5},... | collective-permute-start | bytes 12296 | tf_op jit(solution)/shard_map/ppermute | solution.py:222
  116.3 1.7 %collective-permute-start.24 = (f32[8,128]{1,0:T(8,128)S(1)}, f32[8,128]{1,0:T(8,128)S(1)}, u32[]{:S(2)}, u32[]{:S(2)}) collective-permute-start(f32[8,128]{1,0:T(8,128)S(1)} %add_add_fusion.1), channel_id=1, source_target_pairs={{0,8},{1,9},{2,10},{3,11},{4,12},{5,13},{6,14},{7,15},{8,0},{9,1},... | collective-permute-start | bytes 12296 | tf_op jit(solution)/shard_map/ppermute | solution.py:222
  118.2 1.7 %collective-permute-done.25 = f32[8,128]{1,0:T(8,128)S(1)} collective-permute-done((f32[8,128]{1,0:T(8,128)S(1)}, f32[8,128]{1,0:T(8,128)S(1)}, u32[]{:S(2)}, u32[]{:S(2)}) %collective-permute-start.25) | collective-permute-done | bytes 4128 | tf_op jit(solution)/shard_map/ppermute | solution.py:222
  119.9 1.5 %collective-permute-done.24 = f32[8,128]{1,0:T(8,128)S(1)} collective-permute-done((f32[8,128]{1,0:T(8,128)S(1)}, f32[8,128]{1,0:T(8,128)S(1)}, u32[]{:S(2)}, u32[]{:S(2)}) %collective-permute-start.24) | collective-permute-done | bytes 4128 | tf_op jit(solution)/shard_map/ppermute | solution.py:222
  121.5 4.1 %all-to-all-done.2.parts = f32[16,64,128]{2,1,0:T(8,128)S(1)} async-done(((f32[16,64,128]{2,1,0:T(8,128)}), f32[16,64,128]{2,1,0:T(8,128)S(1)}, u32[]{:S(2)}, u32[]{:S(2)}) %all-to-all-start.2) | async-done | bytes 524320 | tf_op jit(solution)/shard_map/all_to_all | solution.py:237
  125.7 18.1 %all_to_all.22.whole = bf16[16,80,128]{2,1,0:T(8,128)(2,1)S(1)} all-to-all(bf16[16,80,128]{2,1,0:T(8,128)(2,1)S(1)} %shard_map.64), channel_id=1, replica_groups=mesh['op'=16,'qn'=16] {'op'}, dimensions={0} | all-to-all | bytes 655360 | tf_op jit(solution)/shard_map/all_to_all | solution.py:237
  143.8 1.4 shard_map.65
  (40 shorter events, 1.3 us)
Async XLA Ops:
  1.7 1.4 collective-permute-start.1
  3.2 9.7 %collective-permute-start.8 = (bf16[4,256,128]{2,1,0:T(8,128)(2,1)S(1)}, bf16[4,256,128]{2,1,0:T(8,128)(2,1)S(1)}, u32[]{:S(2)}, u32[]{:S(2)}) collective-permute-start(bf16[4,256,128]{2,1,0:T(8,128)(2,1)S(1)} %maximum_select_fusion.refs_0_), channel_id=1, source_target_pairs={{0,12},{1,13},{2,14},{3,15},{4,8},{5,9},{6,10},{7,11},{8,4},{9,5},... | collective-permute-start | bytes 786440 | tf_op jit(solution)/shard_map/ppermute | solution.py:222
  6.3 9.4 %collective-permute-start.3 = (bf16[4,256,128]{2,1,0:T(8,128)(2,1)S(1)}, bf16[4,256,128]{2,1,0:T(8,128)(2,1)S(1)}, u32[]{:S(2)}, u32[]{:S(2)}) collective-permute-start(bf16[4,256,128]{2,1,0:T(8,128)(2,1)S(1)} %maximum_select_fusion.refs_0_), channel_id=1, source_target_pairs={{0,4},{1,5},{2,6},{3,7},{4,0},{5,1},{6,2},{7,3},{8,12},{9,13},{10,... | collective-permute-start | bytes 786440 | tf_op jit(solution)/shard_map/ppermute | solution.py:222
  6.5 13.4 %collective-permute-start.5 = (bf16[4,256,128]{2,1,0:T(8,128)(2,1)S(1)}, bf16[4,256,128]{2,1,0:T(8,128)(2,1)S(1)}, u32[]{:S(2)}, u32[]{:S(2)}) collective-permute-start(bf16[4,256,128]{2,1,0:T(8,128)(2,1)S(1)} %maximum_select_fusion.refs_0_), channel_id=1, source_target_pairs={{0,8},{1,9},{2,10},{3,11},{4,12},{5,13},{6,14},{7,15},{8,0},{9,1},... | collective-permute-start | bytes 786440 | tf_op jit(solution)/shard_map/ppermute | solution.py:222
  8.0 19.7 %copy-start = (bf16[32,256,256]{2,1,0:T(8,128)(2,1)S(1)}, bf16[32,256,256]{2,1,0:T(8,128)(2,1)}, u32[]{:S(2)}) copy-start(bf16[32,256,256]{2,1,0:T(8,128)(2,1)} %left.1) | copy-start | bytes 12582916
  8.8 13.9 %collective-permute-start = (s32[3,2,32]{2,1,0:T(2,128)S(1)}, s32[3,2,32]{2,1,0:T(2,128)S(1)}, u32[]{:S(2)}, u32[]{:S(2)}) collective-permute-start(s32[3,2,32]{2,1,0:T(2,128)S(1)} %xor_bitcast_fusion), channel_id=1, source_target_pairs={{0,1},{1,0},{2,3},{3,2},{4,5},{5,4},{6,7},{7,6},{8,9},{9,8},{10,11... | collective-permute-start | bytes 2312 | tf_op jit(solution)/shard_map/ppermute | solution.py:222
  8.8 17.7 %collective-permute-start.2 = (bf16[4,256,128]{2,1,0:T(8,128)(2,1)S(1)}, bf16[4,256,128]{2,1,0:T(8,128)(2,1)S(1)}, u32[]{:S(2)}, u32[]{:S(2)}) collective-permute-start(bf16[4,256,128]{2,1,0:T(8,128)(2,1)S(1)} %maximum_select_fusion.refs_0_), channel_id=1, source_target_pairs={{0,2},{1,3},{2,0},{3,1},{4,6},{5,7},{6,4},{7,5},{8,10},{9,11},{10,... | collective-permute-start | bytes 786440 | tf_op jit(solution)/shard_map/ppermute | solution.py:222
  12.9 14.7 %collective-permute-start.9 = (bf16[4,256,128]{2,1,0:T(8,128)(2,1)S(1)}, bf16[4,256,128]{2,1,0:T(8,128)(2,1)S(1)}, u32[]{:S(2)}, u32[]{:S(2)}) collective-permute-start(bf16[4,256,128]{2,1,0:T(8,128)(2,1)S(1)} %collective-permute-done.8.refs_7_), channel_id=1, source_target_pairs={{0,130},{1,131},{2,128},{3,129},{4,134},{5,135},{6,132},{7,133},{8... | collective-permute-start | bytes 786440 | tf_op jit(solution)/shard_map/ppermute | solution.py:226
  15.7 12.0 %collective-permute-start.4 = (bf16[4,256,128]{2,1,0:T(8,128)(2,1)S(1)}, bf16[4,256,128]{2,1,0:T(8,128)(2,1)S(1)}, u32[]{:S(2)}, u32[]{:S(2)}) collective-permute-start(bf16[4,256,128]{2,1,0:T(8,128)(2,1)S(1)} %collective-permute-done.3.refs_2_), channel_id=1, source_target_pairs={{0,2},{1,3},{2,0},{3,1},{4,6},{5,7},{6,4},{7,5},{8,10},{9,11},{10,... | collective-permute-start | bytes 786440 | tf_op jit(solution)/shard_map/ppermute | solution.py:222
  19.9 6.7 %collective-permute-start.7 = (bf16[2,256,128]{2,1,0:T(8,128)(2,1)S(1)}, bf16[2,256,128]{2,1,0:T(8,128)(2,1)S(1)}, u32[]{:S(2)}, u32[]{:S(2)}) collective-permute-start(bf16[2,256,128]{2,1,0:T(8,128)(2,1)S(1)} %get-tuple-element.46), channel_id=1, source_target_pairs={{0,130},{1,131},{2,128},{3,129},{4,134},{5,135},{6,132},{7,133},{8... | collective-permute-start | bytes 393224 | tf_op jit(solution)/shard_map/ppermute | solution.py:226
  22.7 5.0 %collective-permute-start.6 = (bf16[2,256,128]{2,1,0:T(8,128)(2,1)S(1)}, bf16[2,256,128]{2,1,0:T(8,128)(2,1)S(1)}, u32[]{:S(2)}, u32[]{:S(2)}) collective-permute-start(bf16[2,256,128]{2,1,0:T(8,128)(2,1)S(1)} %get-tuple-element.47), channel_id=1, source_target_pairs={{0,2},{1,3},{2,0},{3,1},{4,6},{5,7},{6,4},{7,5},{8,10},{9,11},{10,... | collective-permute-start | bytes 393224 | tf_op jit(solution)/shard_map/ppermute | solution.py:222
  22.9 2.2 %copy-start.3 = (bf16[32,256,256]{2,1,0:T(8,128)(2,1)S(1)}, bf16[32,256,256]{2,1,0:T(8,128)(2,1)}, u32[]{:S(2)}) copy-start(bf16[32,256,256]{2,1,0:T(8,128)(2,1)} %r_ref.1) | copy-start | bytes 12582916
  34.0 55.9 %copy-start.2 = (f32[2,256,256]{2,1,0:T(8,128)S(1)}, f32[2,256,256]{2,1,0:T(8,128)}, u32[]{:S(2)}) copy-start(f32[2,256,256]{2,1,0:T(8,128)} %p_ref.1) | copy-start | bytes 1572868
  34.0 2.0 %collective-permute-start.10 = (f32[1024,128]{1,0:T(8,128)S(1)}, f32[1024,128]{1,0:T(8,128)S(1)}, u32[]{:S(2)}, u32[]{:S(2)}) collective-permute-start(f32[1024,128]{1,0:T(8,128)S(1)} %get-tuple-element.23), channel_id=1, source_target_pairs={{0,1},{1,0},{2,3},{3,2},{4,5},{5,4},{6,7},{7,6},{8,9},{9,8},{10,11... | collective-permute-start | bytes 1572872 | tf_op jit(solution)/shard_map/ppermute | solution.py:222
  73.0 10.2 %collective-permute-start.17 = (bf16[4,256,128]{2,1,0:T(8,128)(2,1)S(1)}, bf16[4,256,128]{2,1,0:T(8,128)(2,1)S(1)}, u32[]{:S(2)}, u32[]{:S(2)}) collective-permute-start(bf16[4,256,128]{2,1,0:T(8,128)(2,1)S(1)} %bitcast.7), channel_id=1, source_target_pairs={{0,12},{1,13},{2,14},{3,15},{4,8},{5,9},{6,10},{7,11},{8,4},{9,5},... | collective-permute-start | bytes 786440 | tf_op jit(solution)/shard_map/ppermute | solution.py:222
  76.0 8.5 %collective-permute-start.12 = (bf16[4,256,128]{2,1,0:T(8,128)(2,1)S(1)}, bf16[4,256,128]{2,1,0:T(8,128)(2,1)S(1)}, u32[]{:S(2)}, u32[]{:S(2)}) collective-permute-start(bf16[4,256,128]{2,1,0:T(8,128)(2,1)S(1)} %bitcast.8), channel_id=1, source_target_pairs={{0,4},{1,5},{2,6},{3,7},{4,0},{5,1},{6,2},{7,3},{8,12},{9,13},{10,... | collective-permute-start | bytes 786440 | tf_op jit(solution)/shard_map/ppermute | solution.py:222
  76.0 11.0 %collective-permute-start.14 = (bf16[4,256,128]{2,1,0:T(8,128)(2,1)S(1)}, bf16[4,256,128]{2,1,0:T(8,128)(2,1)S(1)}, u32[]{:S(2)}, u32[]{:S(2)}) collective-permute-start(bf16[4,256,128]{2,1,0:T(8,128)(2,1)S(1)} %bitcast.9), channel_id=1, source_target_pairs={{0,8},{1,9},{2,10},{3,11},{4,12},{5,13},{6,14},{7,15},{8,0},{9,1},... | collective-permute-start | bytes 786440 | tf_op jit(solution)/shard_map/ppermute | solution.py:222
  77.7 14.9 %collective-permute-start.11 = (bf16[4,256,128]{2,1,0:T(8,128)(2,1)S(1)}, bf16[4,256,128]{2,1,0:T(8,128)(2,1)S(1)}, u32[]{:S(2)}, u32[]{:S(2)}) collective-permute-start(bf16[4,256,128]{2,1,0:T(8,128)(2,1)S(1)} %bitcast.10), channel_id=1, source_target_pairs={{0,2},{1,3},{2,0},{3,1},{4,6},{5,7},{6,4},{7,5},{8,10},{9,11},{10,... | collective-permute-start | bytes 786440 | tf_op jit(solution)/shard_map/ppermute | solution.py:222
  78.5 11.2 %collective-permute-start.19 = (bf16[2,256,128]{2,1,0:T(8,128)(2,1)S(1)}, bf16[2,256,128]{2,1,0:T(8,128)(2,1)S(1)}, u32[]{:S(2)}, u32[]{:S(2)}) collective-permute-start(bf16[2,256,128]{2,1,0:T(8,128)(2,1)S(1)} %bitcast.14), channel_id=1, source_target_pairs={{0,1},{1,0},{2,3},{3,2},{4,5},{5,4},{6,7},{7,6},{8,9},{9,8},{10,11... | collective-permute-start | bytes 393224 | tf_op jit(solution)/shard_map/ppermute | solution.py:222
  83.3 11.4 %collective-permute-start.18 = (bf16[4,256,128]{2,1,0:T(8,128)(2,1)S(1)}, bf16[4,256,128]{2,1,0:T(8,128)(2,1)S(1)}, u32[]{:S(2)}, u32[]{:S(2)}) collective-permute-start(bf16[4,256,128]{2,1,0:T(8,128)(2,1)S(1)} %collective-permute-done.17.refs_7_), channel_id=1, source_target_pairs={{0,130},{1,131},{2,128},{3,129},{4,134},{5,135},{6,132},{7,133},{8... | collective-permute-start | bytes 786440 | tf_op jit(solution)/shard_map/ppermute | solution.py:226
  84.5 10.1 %collective-permute-start.13 = (bf16[4,256,128]{2,1,0:T(8,128)(2,1)S(1)}, bf16[4,256,128]{2,1,0:T(8,128)(2,1)S(1)}, u32[]{:S(2)}, u32[]{:S(2)}) collective-permute-start(bf16[4,256,128]{2,1,0:T(8,128)(2,1)S(1)} %collective-permute-done.12.refs_2_), channel_id=1, source_target_pairs={{0,2},{1,3},{2,0},{3,1},{4,6},{5,7},{6,4},{7,5},{8,10},{9,11},{10,... | collective-permute-start | bytes 786440 | tf_op jit(solution)/shard_map/ppermute | solution.py:222
  87.1 6.6 %collective-permute-start.16 = (bf16[2,256,128]{2,1,0:T(8,128)(2,1)S(1)}, bf16[2,256,128]{2,1,0:T(8,128)(2,1)S(1)}, u32[]{:S(2)}, u32[]{:S(2)}) collective-permute-start(bf16[2,256,128]{2,1,0:T(8,128)(2,1)S(1)} %get-tuple-element.44), channel_id=1, source_target_pairs={{0,130},{1,131},{2,128},{3,129},{4,134},{5,135},{6,132},{7,133},{8... | collective-permute-start | bytes 393224 | tf_op jit(solution)/shard_map/ppermute | solution.py:226
  89.7 5.0 %collective-permute-start.15 = (bf16[2,256,128]{2,1,0:T(8,128)(2,1)S(1)}, bf16[2,256,128]{2,1,0:T(8,128)(2,1)S(1)}, u32[]{:S(2)}, u32[]{:S(2)}) collective-permute-start(bf16[2,256,128]{2,1,0:T(8,128)(2,1)S(1)} %get-tuple-element.45), channel_id=1, source_target_pairs={{0,2},{1,3},{2,0},{3,1},{4,6},{5,7},{6,4},{7,5},{8,10},{9,11},{10,... | collective-permute-start | bytes 393224 | tf_op jit(solution)/shard_map/ppermute | solution.py:222
  89.9 2.2 %copy-start.1 = (bf16[32,256,256]{2,1,0:T(8,128)(2,1)S(1)}, bf16[32,256,256]{2,1,0:T(8,128)(2,1)}, u32[]{:S(2)}) copy-start(bf16[32,256,256]{2,1,0:T(8,128)(2,1)} %left.1) | copy-start | bytes 12582916
  101.0 2.0 %collective-permute-start.20 = (f32[2,512,128]{2,1,0:T(8,128)S(1)}, f32[2,512,128]{2,1,0:T(8,128)S(1)}, u32[]{:S(2)}, u32[]{:S(2)}) collective-permute-start(f32[2,512,128]{2,1,0:T(8,128)S(1)} %get-tuple-element.37), channel_id=1, source_target_pairs={{0,1},{1,0},{2,3},{3,2},{4,5},{5,4},{6,7},{7,6},{8,9},{9,8},{10,11... | collective-permute-start | bytes 1572872 | tf_op jit(solution)/shard_map/ppermute | solution.py:222
  104.0 21.6 %all-to-all-start.2 = ((f32[16,64,128]{2,1,0:T(8,128)}), f32[16,64,128]{2,1,0:T(8,128)S(1)}, u32[]{:S(2)}, u32[]{:S(2)}) async-start(f32[16,64,128]{2,1,0:T(8,128)} %get-tuple-element.41), calls=%async_computation.2 | async-start | bytes 1048576 | tf_op jit(solution)/shard_map/all_to_all | solution.py:237
  109.1 3.0 %collective-permute-start.23 = (f32[8,128]{1,0:T(8,128)S(1)}, f32[8,128]{1,0:T(8,128)S(1)}, u32[]{:S(2)}, u32[]{:S(2)}) collective-permute-start(f32[8,128]{1,0:T(8,128)S(1)} %get-tuple-element.40), channel_id=1, source_target_pairs={{0,3},{1,2},{2,1},{3,0},{4,7},{5,6},{6,5},{7,4},{8,11},{9,10},{10,... | collective-permute-start | bytes 12296 | tf_op jit(solution)/shard_map/ppermute | solution.py:222
  109.7 3.6 %collective-permute-start.22 = (f32[8,128]{1,0:T(8,128)S(1)}, f32[8,128]{1,0:T(8,128)S(1)}, u32[]{:S(2)}, u32[]{:S(2)}) collective-permute-start(f32[8,128]{1,0:T(8,128)S(1)} %get-tuple-element.40), channel_id=1, source_target_pairs={{0,2},{1,3},{2,0},{3,1},{4,6},{5,7},{6,4},{7,5},{8,10},{9,11},{10,... | collective-permute-start | bytes 12296 | tf_op jit(solution)/shard_map/ppermute | solution.py:222
  110.6 2.7 %collective-permute-start.21 = (f32[8,128]{1,0:T(8,128)S(1)}, f32[8,128]{1,0:T(8,128)S(1)}, u32[]{:S(2)}, u32[]{:S(2)}) collective-permute-start(f32[8,128]{1,0:T(8,128)S(1)} %get-tuple-element.40), channel_id=1, source_target_pairs={{0,1},{1,0},{2,3},{3,2},{4,5},{5,4},{6,7},{7,6},{8,9},{9,8},{10,11... | collective-permute-start | bytes 12296 | tf_op jit(solution)/shard_map/ppermute | solution.py:222
  113.3 4.9 %collective-permute-start.26 = (f32[8,128]{1,0:T(8,128)S(1)}, f32[8,128]{1,0:T(8,128)S(1)}, u32[]{:S(2)}, u32[]{:S(2)}) collective-permute-start(f32[8,128]{1,0:T(8,128)S(1)} %add_add_fusion.1), channel_id=1, source_target_pairs={{0,12},{1,13},{2,14},{3,15},{4,8},{5,9},{6,10},{7,11},{8,4},{9,5},... | collective-permute-start | bytes 12296 | tf_op jit(solution)/shard_map/ppermute | solution.py:222
  116.3 3.6 %collective-permute-start.25 = (f32[8,128]{1,0:T(8,128)S(1)}, f32[8,128]{1,0:T(8,128)S(1)}, u32[]{:S(2)}, u32[]{:S(2)}) collective-permute-start(f32[8,128]{1,0:T(8,128)S(1)} %add_add_fusion.1), channel_id=1, source_target_pairs={{0,4},{1,5},{2,6},{3,7},{4,0},{5,1},{6,2},{7,3},{8,12},{9,13},{10,... | collective-permute-start | bytes 12296 | tf_op jit(solution)/shard_map/ppermute | solution.py:222
  116.3 5.1 %collective-permute-start.24 = (f32[8,128]{1,0:T(8,128)S(1)}, f32[8,128]{1,0:T(8,128)S(1)}, u32[]{:S(2)}, u32[]{:S(2)}) collective-permute-start(f32[8,128]{1,0:T(8,128)S(1)} %add_add_fusion.1), channel_id=1, source_target_pairs={{0,8},{1,9},{2,10},{3,11},{4,12},{5,13},{6,14},{7,15},{8,0},{9,1},... | collective-permute-start | bytes 12296 | tf_op jit(solution)/shard_map/ppermute | solution.py:222

commit v6 on v4

--- a/solution.py
+++ b/solution.py
@@ -9,7 +9,7 @@
 
 epsilon = 1e-06
 BF, F32 = jnp.bfloat16, jnp.float32
-GROUP = 8
+GROUP = 4
 HALF = 128
 VMEM = pl.BlockSpec(memory_space=pltpu.VMEM)
 SMEM = pl.BlockSpec(memory_space=pltpu.SMEM)
@@ -77,11 +77,11 @@
         core = core_ref[0]
         mine[core] = acc[:512, :HALF]
         mine[1 - core] = acc[:512, HALF:]
-        other[core] = acc[512:, :HALF]
-        other[1 - core] = acc[512:, HALF:]
+        other[core] = acc[512:, :HALF].astype(BF)
+        other[1 - core] = acc[512:, HALF:].astype(BF)
     else:
         mine[...] = acc[:, :HALF]
-        other[...] = acc[:, HALF:]
+        other[...] = acc[:, HALF:].astype(BF)
 
 
 def apply_ham(by_block, meta, core, pieces, left, right):
@@ -90,7 +90,7 @@
         functools.partial(ham_kernel, by_block),
         in_specs=[SMEM, SMEM] + [VMEM] * (len(pieces) + 2),
         out_specs=[VMEM] * 2,
-        out_shape=[jax.ShapeDtypeStruct(shape, F32)] * 2,
+        out_shape=[jax.ShapeDtypeStruct(shape, F32), jax.ShapeDtypeStruct(shape, BF)],
         scratch_shapes=[
             pltpu.VMEM((32, 256, HALF), BF),
             pltpu.VMEM((1024, GROUP * HALF), BF),
@@ -98,6 +98,43 @@
         ],
         compiler_params=limit(8),
     )(meta, core, *pieces, left, right)
+
+
+def square_kernel(p, out):
+    x = p[...]
+    out[...] = jnp.full(out.shape, jnp.sum(x * x))
+
+
+def square(p):
+    return pl.pallas_call(
+        square_kernel,
+        in_specs=[VMEM],
+        out_specs=VMEM,
+        out_shape=jax.ShapeDtypeStruct((16, 8, 128), F32),
+        compiler_params=limit(2),
+    )(p)
+
+
+def scale_kernel(count, rows, p, kept, got, core_ref, first, own):
+    total = rows[0]
+    for i in range(1, 16):
+        total += rows[i]
+    s = lax.rsqrt(total[:1] / count + epsilon)
+    wide = jnp.concatenate([s, s], axis=1)
+    first[...] = p[...] * wide
+    core = core_ref[0]
+    own[pl.ds(2 * core, 2)] = (kept[...] * s).astype(BF)
+    own[pl.ds(2 * (1 - core), 2)] = (got[...] * s).astype(BF)
+
+
+def scale(count, rows, p, kept, got, core):
+    return pl.pallas_call(
+        functools.partial(scale_kernel, count),
+        in_specs=[VMEM] * 4 + [SMEM],
+        out_specs=[VMEM] * 2,
+        out_shape=[jax.ShapeDtypeStruct(p.shape, F32), jax.ShapeDtypeStruct((4, 256, HALF), BF)],
+        compiler_params=limit(2),
+    )(rows, p, kept, got, core)
 
 
 def between_kernel(p, u, left, out, left_out):
@@ -121,7 +158,7 @@
 
 
 def pack_kernel(mine, got, p, u, early, out, stats):
-    total = mine[...] + got[...]
+    total = mine[...] + got[...].astype(F32)
     out[...] = total.astype(BF).reshape(16, 64, HALF)
     pw = uw = 0.0
     for i in range(2):
@@ -188,15 +225,13 @@
     pp, pu, uu = (scalar(jnp.sum(jnp.where((lane == i) & (row == 0), stats[...], 0.0))) for i in range(3))
     pw = scalar(jnp.sum(jnp.where((wide < 3) & (tall == 0), rows, 0.0)))
     uw = scalar(jnp.sum(jnp.where((wide >= 3) & (wide < 6) & (tall == 0), rows, 0.0)))
-    s = lax.rsqrt(pp + epsilon)
-    energy = s * s * pu
-    t = lax.rsqrt(s * s * (uu - 2.0 * energy * pu + energy * energy * pp) + epsilon)
-    ts = t * s
-    diag_d = ts * ts * (uw - energy * (uu + pw) + energy * energy * pu)
-    coupling = 0.5 * ts * s * ((pw - energy * pu) + (uu - energy * pu))
+    energy = pu
+    t = lax.rsqrt(uu - 2.0 * energy * pu + energy * energy * pp + epsilon)
+    diag_d = t * t * (uw - energy * (uu + pw) + energy * energy * pu)
+    coupling = 0.5 * t * ((pw - energy * pu) + (uu - energy * pu))
     gap = energy - diag_d
     theta = 0.5 * (energy + diag_d) - jnp.sqrt(0.25 * gap * gap + coupling * coupling)
-    one, two = (diag_d - theta) * s, coupling * ts
+    one, two = diag_d - theta, coupling * t
     block = pl.program_id(0)
     p, u = p_ref[0], u_ref[0].astype(F32)
     w = [whole[pl.ds(8 * half + 4 * block, 4), :64, :].reshape(256, HALF) for half in range(2)]
@@ -249,8 +284,10 @@
     def in_order(a, b, axis=0):
         return pick(jnp.concatenate([a, b], axis), jnp.concatenate([b, a], axis))
 
-    low, high = psi_start[:, :, :HALF].astype(BF), psi_start[:, :, HALF:].astype(BF)
-    own = in_order(pick(low, high), swap(pick(high, low), 1))
+    low, high = psi_start[:, :, :HALF], psi_start[:, :, HALF:]
+    kept, got = pick(low, high), swap(pick(high, low), 1)
+    rows = lax.all_to_all(square(psi_start), "qn", 0, 0, tiled=True)
+    first, own = scale(count, rows, psi_start, kept, got, core.reshape(1))
     sources = jnp.transpose(sources, (2, 1, 0)) ^ (chip * 4)
     theirs = swap(sources, 1)
     by_chip, own_first = in_order(sources, theirs, 1), jnp.concatenate([sources, theirs], 1)
@@ -259,7 +296,7 @@
     pieces = gather_chips(own)
     right = prepare(core, right_ops)
     mine, other = apply_ham(False, by_chip, core, pieces, left_ops, right)
-    parts = op_exchange((mine + swap(other, 1)).astype(BF).reshape(16, 64, HALF))
+    parts = op_exchange((mine + swap(other, 1).astype(F32)).astype(BF).reshape(16, 64, HALF))
     piece = jnp.sum(parts.astype(F32), axis=0).astype(BF)
     u_half = op_exchange(jnp.broadcast_to(piece[None], (16, 64, HALF))).reshape(4, 256, HALF)
 
@@ -268,15 +305,14 @@
     core0 = core[0] == 0
     kept, got = jnp.where(core0, low, high), swap(jnp.where(core0, high, low), 1)
     u = jnp.where(core0, jnp.concatenate([kept, got], 2), jnp.concatenate([got, kept], 2))
-    early, left = between(psi_start, u, left_ops)
+    early, left = between(first, u, left_ops)
     pieces, u, early, left = lax.optimization_barrier((pieces, u, early, left))
     mine, other = apply_ham(True, own_first, core, pieces, left, right)
-    packed, stats = pack(mine, swap(other, 1), psi_start, u, early)
+    packed, stats = pack(mine, swap(other, 1), first, u, early)
     parts = op_exchange(packed)
-    for bits in (1, 2):
-        stats = stats + swap(stats, bits)
+    stats = (stats + swap(stats, 1)) + (swap(stats, 2) + swap(stats, 3))
     stats = (stats + swap(stats, 8)) + (swap(stats, 4) + swap(stats, 12))
-    return tuple(finish(count, stats, op_exchange(relay(parts, stats)), psi_start, u))
+    return tuple(finish(count, stats, op_exchange(relay(parts, stats)), first, u))
 
 
 def solution(mesh):

time: 145 us -> 154 us (1.062)
  blocking collectives: 57.6 us -> 69.8 us
  starting transfers between devices: 34.1 us -> 31.5 us
  waiting for transfers between devices: 28.2 us -> 26.4 us
    all_to_all x0 -> x1, blocking collectives: none -> 11.6 us  [shards(): rows = lax.all_to_all(square(psi_start), 'qn', 0, 0, tiled=True)]
    ppermute x22 -> x23, waiting for transfers between devices: 27.1 us -> 24.5 us  [swap(): return lax.ppermute(x, 'qn', [(i, i ^ bits) for i in range(16)])]
    ppermute x4, starting transfers between devices: 8.59 us -> 5.96 us  [swap_other_x(): lax.ppermute(x, ('op', 'qn'), [(i, i ^ 8 * 16 + 2) for i in range(256)])]
    ppermute x22 -> x23, starting transfers between devices: 20.4 us -> 19.8 us  [swap(): return lax.ppermute(x, 'qn', [(i, i ^ bits) for i in range(16)])]
  transfers between devices with their start and end apart: 27 -> 28, of which waited for: 16 -> 14; matrix products, arithmetic and copies ran while one was open for 1% -> 1% of each run, Pallas kernels for 1% -> 1%
where the time goes in v6:
time: 154 us
  blocking collectives  69.8 us (45%)
  starting transfers between devices  31.5 us (20%)
  waiting for transfers between devices  26.4 us (17%)
  Pallas kernels  17.6 us (11%)
  local copies, waits for them, and re-layouts  5.49 us (4%)
  other arithmetic  2.15 us (1%)
    all_to_all x3, blocking collectives, op_exchange(): return lax.all_to_all(x, 'op', 0, 0, tiled=True)  58.2 us
    ppermute x23, waiting for transfers between devices, swap(): return lax.ppermute(x, 'qn', [(i, i ^ bits) for i in range(16)])  24.5 us
    ppermute x23, starting transfers between devices, swap(): return lax.ppermute(x, 'qn', [(i, i ^ bits) for i in range(16)])  19.8 us
    pallas_call x2, Pallas kernels, apply_ham(): pl.pallas_call(functools.partial(ham_kernel, by_block), in_specs=[SMEM, S...  13 us
    all_to_all x1, blocking collectives, shards(): rows = lax.all_to_all(square(psi_start), 'qn', 0, 0, tiled=True)  11.6 us
    ppermute x4, starting transfers between devices, swap_other_x(): lax.ppermute(x, ('op', 'qn'), [(i, i ^ 8 * 16 + 2) for i in range(256)])  5.96 us
    all_to_all x1, starting transfers between devices, op_exchange(): return lax.all_to_all(x, 'op', 0, 0, tiled=True)  5.71 us
    unnamed x8, local copies, waits for them, and re-layouts  5.41 us
  transfers between devices with their start and end apart: 28, of which 14 were waited for; matrix products, arithmetic and copies ran while one was open for 1% of the time, Pallas kernels for 1%

profile of v6, /device:TPU:32, one launch (start us, length us, event | category | flops | bytes accessed | tf_op | source)
XLA Modules:
  0.0 153.8 jit_solution(16242333989763556070)
XLA Ops:
  0.6 1.1 slice_select_fusion
  1.8 1.0 copy-done.2
  2.9 0.3 shard_map.59
  3.1 11.6 %all_to_all.25.rows = f32[16,8,128]{2,1,0:T(8,128)S(1)} all-to-all(f32[16,8,128]{2,1,0:T(8,128)S(1)} %shard_map.59), channel_id=1, replica_groups=mesh['op'=16,'qn'=16] {'qn'}, dimensions={0} | all-to-all | bytes 131072 | tf_op jit(solution)/shard_map/all_to_all | solution.py:289
  14.8 1.2 collective-permute-start.8
  16.0 3.6 %collective-permute-start.5 = (bf16[4,256,128]{2,1,0:T(8,128)(2,1)S(1)}, bf16[4,256,128]{2,1,0:T(8,128)(2,1)S(1)}, u32[]{:S(2)}, u32[]{:S(2)}) collective-permute-start(bf16[4,256,128]{2,1,0:T(8,128)(2,1)S(1)} %get-tuple-element.24.refs_0_), channel_id=1, source_target_pairs={{0,8},{1,9},{2,10},{3,11},{4,12},{5,13},{6,14},{7,15},{8,0},{9,1},... | collective-permute-start | bytes 786440 | tf_op jit(solution)/shard_map/ppermute | solution.py:257
  19.6 0.8 xor_bitcast_fusion
  20.4 0.7 collective-permute-start.2
  21.1 3.3 %collective-permute-done.8.refs_7_ = bf16[4,256,128]{2,1,0:T(8,128)(2,1)S(1)} collective-permute-done((bf16[4,256,128]{2,1,0:T(8,128)(2,1)S(1)}, bf16[4,256,128]{2,1,0:T(8,128)(2,1)S(1)}, u32[]{:S(2)}, u32[]{:S(2)}) %collective-permute-start.8) | collective-permute-done | bytes 262176 | tf_op jit(solution)/shard_map/ppermute | solution.py:257
  24.4 2.0 %collective-permute-start.9 = (bf16[4,256,128]{2,1,0:T(8,128)(2,1)S(1)}, bf16[4,256,128]{2,1,0:T(8,128)(2,1)S(1)}, u32[]{:S(2)}, u32[]{:S(2)}) collective-permute-start(bf16[4,256,128]{2,1,0:T(8,128)(2,1)S(1)} %collective-permute-done.8.refs_7_), channel_id=1, source_target_pairs={{0,130},{1,131},{2,128},{3,129},{4,134},{5,135},{6,132},{7,133},{8... | collective-permute-start | bytes 786440 | tf_op jit(solution)/shard_map/ppermute | solution.py:261
  26.3 0.7 collective-permute-start.4
  27.1 4.1 %collective-permute-done.5.refs_4_ = bf16[4,256,128]{2,1,0:T(8,128)(2,1)S(1)} collective-permute-done((bf16[4,256,128]{2,1,0:T(8,128)(2,1)S(1)}, bf16[4,256,128]{2,1,0:T(8,128)(2,1)S(1)}, u32[]{:S(2)}, u32[]{:S(2)}) %collective-permute-start.5) | collective-permute-done | bytes 262176 | tf_op jit(solution)/shard_map/ppermute | solution.py:257
  31.2 2.0 %collective-permute-start.7 = (bf16[2,256,128]{2,1,0:T(8,128)(2,1)S(1)}, bf16[2,256,128]{2,1,0:T(8,128)(2,1)S(1)}, u32[]{:S(2)}, u32[]{:S(2)}) collective-permute-start(bf16[2,256,128]{2,1,0:T(8,128)(2,1)S(1)} %get-tuple-element.52), channel_id=1, source_target_pairs={{0,130},{1,131},{2,128},{3,129},{4,134},{5,135},{6,132},{7,133},{8... | collective-permute-start | bytes 393224 | tf_op jit(solution)/shard_map/ppermute | solution.py:261
  33.2 0.7 collective-permute-start.6
  34.0 2.2 %copy-done.3 = bf16[32,256,256]{2,1,0:T(8,128)(2,1)S(1)} copy-done((bf16[32,256,256]{2,1,0:T(8,128)(2,1)S(1)}, bf16[32,256,256]{2,1,0:T(8,128)(2,1)}, u32[]{:S(2)}) %copy-start.3) | copy-done | bytes 4194328
  36.2 1.4 shard_map.61.refs_10_
  37.6 0.6 collective-permute-done.6.refs_5_
  38.2 6.6 %shard_map.62 = (f32[1024,128]{1,0:T(8,128)S(1)}, bf16[1024,128]{1,0:T(8,128)(2,1)S(1)}) custom-call(s32[3,4,32]{2,1,0:T(4,128)S(1)} %get-tuple-element.54.meta, s32[1]{0:T(128)} %bitcast.1.core_ref, bf16[4,256,128]{2,1,0:T(8,128)(2,1)S(1)} %get-tuple-element.24.refs_0_, bf16[4,256,128]{2,1,0:T(8,128)(2,1)S(1)} %collective-permute-done.2.refs_1_, ...), custom_call_target="tpu_custom_call" | custom-call | tf_op jit(solution)/shard_map/pallas_call | solution.py:89
  45.0 1.5 collective-permute-done.10
  46.5 21.8 %all_to_all.26 = bf16[16,64,128]{2,1,0:T(8,128)(2,1)S(1)} all-to-all(bf16[16,64,128]{2,1,0:T(8,128)(2,1)S(1)} %bitcast.12), channel_id=1, replica_groups=mesh['op'=16,'qn'=16] {'op'}, dimensions={0} | all-to-all | bytes 524288 | tf_op jit(solution)/shard_map/all_to_all | solution.py:272
  68.4 15.8 %all_to_all.27 = bf16[16,64,128]{2,1,0:T(8,128)(2,1)S(1)} all-to-all(bf16[16,64,128]{2,1,0:T(8,128)(2,1)S(1)} %broadcast_in_dim.2), channel_id=1, replica_groups=mesh['op'=16,'qn'=16] {'op'}, dimensions={0} | all-to-all | bytes 524288 | tf_op jit(solution)/shard_map/all_to_all | solution.py:272
  84.2 1.1 collective-permute-start.17
  85.4 3.6 %collective-permute-start.14 = (bf16[4,256,128]{2,1,0:T(8,128)(2,1)S(1)}, bf16[4,256,128]{2,1,0:T(8,128)(2,1)S(1)}, u32[]{:S(2)}, u32[]{:S(2)}) collective-permute-start(bf16[4,256,128]{2,1,0:T(8,128)(2,1)S(1)} %bitcast.9), channel_id=1, source_target_pairs={{0,8},{1,9},{2,10},{3,11},{4,12},{5,13},{6,14},{7,15},{8,0},{9,1},... | collective-permute-start | bytes 786440 | tf_op jit(solution)/shard_map/ppermute | solution.py:257
  89.1 5.5 %collective-permute-done.17.refs_7_ = bf16[4,256,128]{2,1,0:T(8,128)(2,1)S(1)} collective-permute-done((bf16[4,256,128]{2,1,0:T(8,128)(2,1)S(1)}, bf16[4,256,128]{2,1,0:T(8,128)(2,1)S(1)}, u32[]{:S(2)}, u32[]{:S(2)}) %collective-permute-start.17) | collective-permute-done | bytes 262176 | tf_op jit(solution)/shard_map/ppermute | solution.py:257
  94.6 0.4 collective-permute-start.13
  95.0 3.3 %collective-permute-done.14.refs_4_ = bf16[4,256,128]{2,1,0:T(8,128)(2,1)S(1)} collective-permute-done((bf16[4,256,128]{2,1,0:T(8,128)(2,1)S(1)}, bf16[4,256,128]{2,1,0:T(8,128)(2,1)S(1)}, u32[]{:S(2)}, u32[]{:S(2)}) %collective-permute-start.14) | collective-permute-done | bytes 262176 | tf_op jit(solution)/shard_map/ppermute | solution.py:257
  98.2 2.0 %collective-permute-start.16 = (bf16[2,256,128]{2,1,0:T(8,128)(2,1)S(1)}, bf16[2,256,128]{2,1,0:T(8,128)(2,1)S(1)}, u32[]{:S(2)}, u32[]{:S(2)}) collective-permute-start(bf16[2,256,128]{2,1,0:T(8,128)(2,1)S(1)} %get-tuple-element.50), channel_id=1, source_target_pairs={{0,130},{1,131},{2,128},{3,129},{4,134},{5,135},{6,132},{7,133},{8... | collective-permute-start | bytes 393224 | tf_op jit(solution)/shard_map/ppermute | solution.py:261
  100.2 0.8 collective-permute-start.15
  101.1 2.2 %copy-done.1 = bf16[32,256,256]{2,1,0:T(8,128)(2,1)S(1)} copy-done((bf16[32,256,256]{2,1,0:T(8,128)(2,1)S(1)}, bf16[32,256,256]{2,1,0:T(8,128)(2,1)}, u32[]{:S(2)}) %copy-start.1) | copy-done | bytes 4194328
  103.2 0.5 shard_map.63
  103.7 1.0 collective-permute-done.16.refs_6_
  104.7 0.4 collective-permute-done.15.refs_5_
  105.2 6.3 %shard_map.64 = (f32[2,512,128]{2,1,0:T(8,128)S(1)}, bf16[2,512,128]{2,1,0:T(8,128)(2,1)S(1)}) custom-call(s32[3,4,32]{2,1,0:T(4,128)S(1)} %get-tuple-element.55.meta, s32[1]{0:T(128)} %bitcast.1.core_ref, bf16[4,256,128]{2,1,0:T(8,128)(2,1)S(1)} %bitcast.11, bf16[4,256,128]{2,1,0:T(8,128)(2,1)S(1)} %collective-permute-done.11.refs_1_, ...), custom_call_target="tpu_custom_call" | custom-call | tf_op jit(solution)/shard_map/pallas_call | solution.py:89
  111.6 1.5 collective-permute-done.20.got
  113.1 0.9 shard_map.65
  114.0 5.7 %all-to-all-start.3 = ((bf16[16,64,128]{2,1,0:T(8,128)(2,1)}), bf16[16,64,128]{2,1,0:T(8,128)(2,1)S(1)}, u32[]{:S(2)}, u32[]{:S(2)}) async-start(bf16[16,64,128]{2,1,0:T(8,128)(2,1)} %get-tuple-element.45), calls=%async_computation.3 | async-start | bytes 524288 | tf_op jit(solution)/shard_map/all_to_all | solution.py:272
  119.8 0.6 collective-permute-start.23
  120.4 0.9 collective-permute-start.22
  121.3 0.3 collective-permute-start.21
  121.6 1.2 collective-permute-done.23
  122.8 1.4 collective-permute-done.22
  124.2 1.2 collective-permute-start.26
  125.5 3.6 %collective-permute-start.24 = (f32[8,128]{1,0:T(8,128)S(1)}, f32[8,128]{1,0:T(8,128)S(1)}, u32[]{:S(2)}, u32[]{:S(2)}) collective-permute-start(f32[8,128]{1,0:T(8,128)S(1)} %add_add_fusion.1), channel_id=1, source_target_pairs={{0,8},{1,9},{2,10},{3,11},{4,12},{5,13},{6,14},{7,15},{8,0},{9,1},... | collective-permute-start | bytes 12296 | tf_op jit(solution)/shard_map/ppermute | solution.py:257
  129.2 1.5 collective-permute-done.24
  130.7 1.0 all-to-all-done.3.parts
  131.6 0.1 shard_map.66
  131.8 20.6 %all_to_all.28.whole = bf16[16,80,128]{2,1,0:T(8,128)(2,1)S(1)} all-to-all(bf16[16,80,128]{2,1,0:T(8,128)(2,1)S(1)} %shard_map.66), channel_id=1, replica_groups=mesh['op'=16,'qn'=16] {'op'}, dimensions={0} | all-to-all | bytes 655360 | tf_op jit(solution)/shard_map/all_to_all | solution.py:272
  152.4 1.4 shard_map.67
  (41 shorter events, 1.0 us)
Async XLA Ops:
  1.7 13.0 %collective-permute-start.1 = (f32[2,256,128]{2,1,0:T(8,128)S(1)}, f32[2,256,128]{2,1,0:T(8,128)S(1)}, u32[]{:S(2)}, u32[]{:S(2)}) collective-permute-start(f32[2,256,128]{2,1,0:T(8,128)S(1)} %get-tuple-element.46), channel_id=1, source_target_pairs={{0,1},{1,0},{2,3},{3,2},{4,5},{5,4},{6,7},{7,6},{8,9},{9,8},{10,11... | collective-permute-start | bytes 786440 | tf_op jit(solution)/shard_map/ppermute | solution.py:257
  1.8 1.0 copy-start.2
  14.8 9.6 %collective-permute-start.8 = (bf16[4,256,128]{2,1,0:T(8,128)(2,1)S(1)}, bf16[4,256,128]{2,1,0:T(8,128)(2,1)S(1)}, u32[]{:S(2)}, u32[]{:S(2)}) collective-permute-start(bf16[4,256,128]{2,1,0:T(8,128)(2,1)S(1)} %get-tuple-element.24.refs_0_), channel_id=1, source_target_pairs={{0,12},{1,13},{2,14},{3,15},{4,8},{5,9},{6,10},{7,11},{8,4},{9,5},... | collective-permute-start | bytes 786440 | tf_op jit(solution)/shard_map/ppermute | solution.py:257
  16.0 10.3 %collective-permute-start.3 = (bf16[4,256,128]{2,1,0:T(8,128)(2,1)S(1)}, bf16[4,256,128]{2,1,0:T(8,128)(2,1)}, u32[]{:S(2)}, u32[]{:S(2)}) collective-permute-start(bf16[4,256,128]{2,1,0:T(8,128)(2,1)S(1)} %get-tuple-element.24.refs_0_), channel_id=1, source_target_pairs={{0,4},{1,5},{2,6},{3,7},{4,0},{5,1},{6,2},{7,3},{8,12},{9,13},{10,... | collective-permute-start | bytes 786440 | tf_op jit(solution)/shard_map/ppermute | solution.py:257
  16.0 15.2 %collective-permute-start.5 = (bf16[4,256,128]{2,1,0:T(8,128)(2,1)S(1)}, bf16[4,256,128]{2,1,0:T(8,128)(2,1)S(1)}, u32[]{:S(2)}, u32[]{:S(2)}) collective-permute-start(bf16[4,256,128]{2,1,0:T(8,128)(2,1)S(1)} %get-tuple-element.24.refs_0_), channel_id=1, source_target_pairs={{0,8},{1,9},{2,10},{3,11},{4,12},{5,13},{6,14},{7,15},{8,0},{9,1},... | collective-permute-start | bytes 786440 | tf_op jit(solution)/shard_map/ppermute | solution.py:257
  19.6 18.6 %copy-start = (bf16[32,256,256]{2,1,0:T(8,128)(2,1)S(1)}, bf16[32,256,256]{2,1,0:T(8,128)(2,1)}, u32[]{:S(2)}) copy-start(bf16[32,256,256]{2,1,0:T(8,128)(2,1)} %left.1) | copy-start | bytes 12582916
  20.4 12.8 %collective-permute-start = (s32[3,2,32]{2,1,0:T(2,128)S(1)}, s32[3,2,32]{2,1,0:T(2,128)S(1)}, u32[]{:S(2)}, u32[]{:S(2)}) collective-permute-start(s32[3,2,32]{2,1,0:T(2,128)S(1)} %xor_bitcast_fusion), channel_id=1, source_target_pairs={{0,1},{1,0},{2,3},{3,2},{4,5},{5,4},{6,7},{7,6},{8,9},{9,8},{10,11... | collective-permute-start | bytes 2312 | tf_op jit(solution)/shard_map/ppermute | solution.py:257
  20.4 17.2 %collective-permute-start.2 = (bf16[4,256,128]{2,1,0:T(8,128)(2,1)S(1)}, bf16[4,256,128]{2,1,0:T(8,128)(2,1)S(1)}, u32[]{:S(2)}, u32[]{:S(2)}) collective-permute-start(bf16[4,256,128]{2,1,0:T(8,128)(2,1)S(1)} %get-tuple-element.24.refs_0_), channel_id=1, source_target_pairs={{0,2},{1,3},{2,0},{3,1},{4,6},{5,7},{6,4},{7,5},{8,10},{9,11},{10,... | collective-permute-start | bytes 786440 | tf_op jit(solution)/shard_map/ppermute | solution.py:257
  24.4 13.8 %collective-permute-start.9 = (bf16[4,256,128]{2,1,0:T(8,128)(2,1)S(1)}, bf16[4,256,128]{2,1,0:T(8,128)(2,1)S(1)}, u32[]{:S(2)}, u32[]{:S(2)}) collective-permute-start(bf16[4,256,128]{2,1,0:T(8,128)(2,1)S(1)} %collective-permute-done.8.refs_7_), channel_id=1, source_target_pairs={{0,130},{1,131},{2,128},{3,129},{4,134},{5,135},{6,132},{7,133},{8... | collective-permute-start | bytes 786440 | tf_op jit(solution)/shard_map/ppermute | solution.py:261
  26.3 11.9 %collective-permute-start.4 = (bf16[4,256,128]{2,1,0:T(8,128)(2,1)}, bf16[4,256,128]{2,1,0:T(8,128)(2,1)S(1)}, u32[]{:S(2)}, u32[]{:S(2)}) collective-permute-start(bf16[4,256,128]{2,1,0:T(8,128)(2,1)} %collective-permute-done.3.refs_2_), channel_id=1, source_target_pairs={{0,2},{1,3},{2,0},{3,1},{4,6},{5,7},{6,4},{7,5},{8,10},{9,11},{10,... | collective-permute-start | bytes 786440 | tf_op jit(solution)/shard_map/ppermute | solution.py:257
  31.2 6.4 %collective-permute-start.7 = (bf16[2,256,128]{2,1,0:T(8,128)(2,1)S(1)}, bf16[2,256,128]{2,1,0:T(8,128)(2,1)S(1)}, u32[]{:S(2)}, u32[]{:S(2)}) collective-permute-start(bf16[2,256,128]{2,1,0:T(8,128)(2,1)S(1)} %get-tuple-element.52), channel_id=1, source_target_pairs={{0,130},{1,131},{2,128},{3,129},{4,134},{5,135},{6,132},{7,133},{8... | collective-permute-start | bytes 393224 | tf_op jit(solution)/shard_map/ppermute | solution.py:261
  33.2 5.0 %collective-permute-start.6 = (bf16[2,256,128]{2,1,0:T(8,128)(2,1)S(1)}, bf16[2,256,128]{2,1,0:T(8,128)(2,1)S(1)}, u32[]{:S(2)}, u32[]{:S(2)}) collective-permute-start(bf16[2,256,128]{2,1,0:T(8,128)(2,1)S(1)} %get-tuple-element.53), channel_id=1, source_target_pairs={{0,2},{1,3},{2,0},{3,1},{4,6},{5,7},{6,4},{7,5},{8,10},{9,11},{10,... | collective-permute-start | bytes 393224 | tf_op jit(solution)/shard_map/ppermute | solution.py:257
  34.0 2.2 %copy-start.3 = (bf16[32,256,256]{2,1,0:T(8,128)(2,1)S(1)}, bf16[32,256,256]{2,1,0:T(8,128)(2,1)}, u32[]{:S(2)}) copy-start(bf16[32,256,256]{2,1,0:T(8,128)(2,1)} %r_ref.1) | copy-start | bytes 12582916
  44.9 1.6 %collective-permute-start.10 = (bf16[1024,128]{1,0:T(8,128)(2,1)S(1)}, bf16[1024,128]{1,0:T(8,128)(2,1)S(1)}, u32[]{:S(2)}, u32[]{:S(2)}) collective-permute-start(bf16[1024,128]{1,0:T(8,128)(2,1)S(1)} %get-tuple-element.26), channel_id=1, source_target_pairs={{0,1},{1,0},{2,3},{3,2},{4,5},{5,4},{6,7},{7,6},{8,9},{9,8},{10,11... | collective-permute-start | bytes 786440 | tf_op jit(solution)/shard_map/ppermute | solution.py:257
  84.2 10.3 %collective-permute-start.17 = (bf16[4,256,128]{2,1,0:T(8,128)(2,1)S(1)}, bf16[4,256,128]{2,1,0:T(8,128)(2,1)S(1)}, u32[]{:S(2)}, u32[]{:S(2)}) collective-permute-start(bf16[4,256,128]{2,1,0:T(8,128)(2,1)S(1)} %bitcast.7), channel_id=1, source_target_pairs={{0,12},{1,13},{2,14},{3,15},{4,8},{5,9},{6,10},{7,11},{8,4},{9,5},... | collective-permute-start | bytes 786440 | tf_op jit(solution)/shard_map/ppermute | solution.py:257
  85.4 9.2 %collective-permute-start.12 = (bf16[4,256,128]{2,1,0:T(8,128)(2,1)S(1)}, bf16[4,256,128]{2,1,0:T(8,128)(2,1)S(1)}, u32[]{:S(2)}, u32[]{:S(2)}) collective-permute-start(bf16[4,256,128]{2,1,0:T(8,128)(2,1)S(1)} %bitcast.8), channel_id=1, source_target_pairs={{0,4},{1,5},{2,6},{3,7},{4,0},{5,1},{6,2},{7,3},{8,12},{9,13},{10,... | collective-permute-start | bytes 786440 | tf_op jit(solution)/shard_map/ppermute | solution.py:257
  85.4 12.9 %collective-permute-start.14 = (bf16[4,256,128]{2,1,0:T(8,128)(2,1)S(1)}, bf16[4,256,128]{2,1,0:T(8,128)(2,1)S(1)}, u32[]{:S(2)}, u32[]{:S(2)}) collective-permute-start(bf16[4,256,128]{2,1,0:T(8,128)(2,1)S(1)} %bitcast.9), channel_id=1, source_target_pairs={{0,8},{1,9},{2,10},{3,11},{4,12},{5,13},{6,14},{7,15},{8,0},{9,1},... | collective-permute-start | bytes 786440 | tf_op jit(solution)/shard_map/ppermute | solution.py:257
  88.9 14.8 %collective-permute-start.11 = (bf16[4,256,128]{2,1,0:T(8,128)(2,1)S(1)}, bf16[4,256,128]{2,1,0:T(8,128)(2,1)S(1)}, u32[]{:S(2)}, u32[]{:S(2)}) collective-permute-start(bf16[4,256,128]{2,1,0:T(8,128)(2,1)S(1)} %bitcast.10), channel_id=1, source_target_pairs={{0,2},{1,3},{2,0},{3,1},{4,6},{5,7},{6,4},{7,5},{8,10},{9,11},{10,... | collective-permute-start | bytes 786440 | tf_op jit(solution)/shard_map/ppermute | solution.py:257
  89.0 11.2 %collective-permute-start.19 = (bf16[2,256,128]{2,1,0:T(8,128)(2,1)S(1)}, bf16[2,256,128]{2,1,0:T(8,128)(2,1)S(1)}, u32[]{:S(2)}, u32[]{:S(2)}) collective-permute-start(bf16[2,256,128]{2,1,0:T(8,128)(2,1)S(1)} %bitcast.14), channel_id=1, source_target_pairs={{0,1},{1,0},{2,3},{3,2},{4,5},{5,4},{6,7},{7,6},{8,9},{9,8},{10,11... | collective-permute-start | bytes 393224 | tf_op jit(solution)/shard_map/ppermute | solution.py:257
  94.6 10.6 %collective-permute-start.18 = (bf16[4,256,128]{2,1,0:T(8,128)(2,1)S(1)}, bf16[4,256,128]{2,1,0:T(8,128)(2,1)S(1)}, u32[]{:S(2)}, u32[]{:S(2)}) collective-permute-start(bf16[4,256,128]{2,1,0:T(8,128)(2,1)S(1)} %collective-permute-done.17.refs_7_), channel_id=1, source_target_pairs={{0,130},{1,131},{2,128},{3,129},{4,134},{5,135},{6,132},{7,133},{8... | collective-permute-start | bytes 786440 | tf_op jit(solution)/shard_map/ppermute | solution.py:261
  94.6 10.6 %collective-permute-start.13 = (bf16[4,256,128]{2,1,0:T(8,128)(2,1)S(1)}, bf16[4,256,128]{2,1,0:T(8,128)(2,1)S(1)}, u32[]{:S(2)}, u32[]{:S(2)}) collective-permute-start(bf16[4,256,128]{2,1,0:T(8,128)(2,1)S(1)} %collective-permute-done.12.refs_2_), channel_id=1, source_target_pairs={{0,2},{1,3},{2,0},{3,1},{4,6},{5,7},{6,4},{7,5},{8,10},{9,11},{10,... | collective-permute-start | bytes 786440 | tf_op jit(solution)/shard_map/ppermute | solution.py:257
  98.2 6.5 %collective-permute-start.16 = (bf16[2,256,128]{2,1,0:T(8,128)(2,1)S(1)}, bf16[2,256,128]{2,1,0:T(8,128)(2,1)S(1)}, u32[]{:S(2)}, u32[]{:S(2)}) collective-permute-start(bf16[2,256,128]{2,1,0:T(8,128)(2,1)S(1)} %get-tuple-element.50), channel_id=1, source_target_pairs={{0,130},{1,131},{2,128},{3,129},{4,134},{5,135},{6,132},{7,133},{8... | collective-permute-start | bytes 393224 | tf_op jit(solution)/shard_map/ppermute | solution.py:261
  100.2 5.0 %collective-permute-start.15 = (bf16[2,256,128]{2,1,0:T(8,128)(2,1)S(1)}, bf16[2,256,128]{2,1,0:T(8,128)(2,1)S(1)}, u32[]{:S(2)}, u32[]{:S(2)}) collective-permute-start(bf16[2,256,128]{2,1,0:T(8,128)(2,1)S(1)} %get-tuple-element.51), channel_id=1, source_target_pairs={{0,2},{1,3},{2,0},{3,1},{4,6},{5,7},{6,4},{7,5},{8,10},{9,11},{10,... | collective-permute-start | bytes 393224 | tf_op jit(solution)/shard_map/ppermute | solution.py:257
  101.0 2.2 %copy-start.1 = (bf16[32,256,256]{2,1,0:T(8,128)(2,1)S(1)}, bf16[32,256,256]{2,1,0:T(8,128)(2,1)}, u32[]{:S(2)}) copy-start(bf16[32,256,256]{2,1,0:T(8,128)(2,1)} %left.1) | copy-start | bytes 12582916
  111.5 1.6 %collective-permute-start.20 = (bf16[2,512,128]{2,1,0:T(8,128)(2,1)S(1)}, bf16[2,512,128]{2,1,0:T(8,128)(2,1)S(1)}, u32[]{:S(2)}, u32[]{:S(2)}) collective-permute-start(bf16[2,512,128]{2,1,0:T(8,128)(2,1)S(1)} %get-tuple-element.41), channel_id=1, source_target_pairs={{0,1},{1,0},{2,3},{3,2},{4,5},{5,4},{6,7},{7,6},{8,9},{9,8},{10,11... | collective-permute-start | bytes 786440 | tf_op jit(solution)/shard_map/ppermute | solution.py:257
  114.0 17.6 %all-to-all-start.3 = ((bf16[16,64,128]{2,1,0:T(8,128)(2,1)}), bf16[16,64,128]{2,1,0:T(8,128)(2,1)S(1)}, u32[]{:S(2)}, u32[]{:S(2)}) async-start(bf16[16,64,128]{2,1,0:T(8,128)(2,1)} %get-tuple-element.45), calls=%async_computation.3 | async-start | bytes 524288 | tf_op jit(solution)/shard_map/all_to_all | solution.py:272
  119.8 3.1 %collective-permute-start.23 = (f32[8,128]{1,0:T(8,128)S(1)}, f32[8,128]{1,0:T(8,128)S(1)}, u32[]{:S(2)}, u32[]{:S(2)}) collective-permute-start(f32[8,128]{1,0:T(8,128)S(1)} %get-tuple-element.44), channel_id=1, source_target_pairs={{0,3},{1,2},{2,1},{3,0},{4,7},{5,6},{6,5},{7,4},{8,11},{9,10},{10,... | collective-permute-start | bytes 12296 | tf_op jit(solution)/shard_map/ppermute | solution.py:257
  120.4 3.9 %collective-permute-start.22 = (f32[8,128]{1,0:T(8,128)S(1)}, f32[8,128]{1,0:T(8,128)S(1)}, u32[]{:S(2)}, u32[]{:S(2)}) collective-permute-start(f32[8,128]{1,0:T(8,128)S(1)} %get-tuple-element.44), channel_id=1, source_target_pairs={{0,2},{1,3},{2,0},{3,1},{4,6},{5,7},{6,4},{7,5},{8,10},{9,11},{10,... | collective-permute-start | bytes 12296 | tf_op jit(solution)/shard_map/ppermute | solution.py:257
  121.3 3.0 %collective-permute-start.21 = (f32[8,128]{1,0:T(8,128)S(1)}, f32[8,128]{1,0:T(8,128)S(1)}, u32[]{:S(2)}, u32[]{:S(2)}) collective-permute-start(f32[8,128]{1,0:T(8,128)S(1)} %get-tuple-element.44), channel_id=1, source_target_pairs={{0,1},{1,0},{2,3},{3,2},{4,5},{5,4},{6,7},{7,6},{8,9},{9,8},{10,11... | collective-permute-start | bytes 12296 | tf_op jit(solution)/shard_map/ppermute | solution.py:257
  124.2 4.9 %collective-permute-start.26 = (f32[8,128]{1,0:T(8,128)S(1)}, f32[8,128]{1,0:T(8,128)S(1)}, u32[]{:S(2)}, u32[]{:S(2)}) collective-permute-start(f32[8,128]{1,0:T(8,128)S(1)} %add_add_fusion.1), channel_id=1, source_target_pairs={{0,12},{1,13},{2,14},{3,15},{4,8},{5,9},{6,10},{7,11},{8,4},{9,5},... | collective-permute-start | bytes 12296 | tf_op jit(solution)/shard_map/ppermute | solution.py:257
  125.5 3.7 %collective-permute-start.25 = (f32[8,128]{1,0:T(8,128)S(1)}, f32[8,128]{1,0:T(8,128)S(1)}, u32[]{:S(2)}, u32[]{:S(2)}) collective-permute-start(f32[8,128]{1,0:T(8,128)S(1)} %add_add_fusion.1), channel_id=1, source_target_pairs={{0,4},{1,5},{2,6},{3,7},{4,0},{5,1},{6,2},{7,3},{8,12},{9,13},{10,... | collective-permute-start | bytes 12296 | tf_op jit(solution)/shard_map/ppermute | solution.py:257
  125.5 5.2 %collective-permute-start.24 = (f32[8,128]{1,0:T(8,128)S(1)}, f32[8,128]{1,0:T(8,128)S(1)}, u32[]{:S(2)}, u32[]{:S(2)}) collective-permute-start(f32[8,128]{1,0:T(8,128)S(1)} %add_add_fusion.1), channel_id=1, source_target_pairs={{0,8},{1,9},{2,10},{3,11},{4,12},{5,13},{6,14},{7,15},{8,0},{9,1},... | collective-permute-start | bytes 12296 | tf_op jit(solution)/shard_map/ppermute | solution.py:257

commit v7 on v5

--- a/solution.py
+++ b/solution.py
@@ -77,8 +77,8 @@
         core = core_ref[0]
         mine[core] = acc[:512, :HALF]
         mine[1 - core] = acc[:512, HALF:]
-        other[core] = acc[512:, :HALF]
-        other[1 - core] = acc[512:, HALF:]
+        other[core] = acc[512:, :HALF].astype(BF)
+        other[1 - core] = acc[512:, HALF:].astype(BF)
     else:
         mine[...] = acc[:, :HALF]
         other[...] = acc[:, HALF:]
@@ -90,7 +90,7 @@
         functools.partial(ham_kernel, by_block),
         in_specs=[SMEM, SMEM] + [VMEM] * (len(pieces) + 2),
         out_specs=[VMEM] * 2,
-        out_shape=[jax.ShapeDtypeStruct(shape, F32)] * 2,
+        out_shape=[jax.ShapeDtypeStruct(shape, F32), jax.ShapeDtypeStruct(shape, BF if by_block else F32)],
         scratch_shapes=[
             pltpu.VMEM((32, 256, HALF), BF),
             pltpu.VMEM((1024, GROUP * HALF), BF),
@@ -121,7 +121,7 @@
 
 
 def pack_kernel(mine, got, p, u, early, out, stats):
-    total = mine[...] + got[...]
+    total = mine[...] + got[...].astype(F32)
     out[...] = total.reshape(16, 64, HALF)
     pw = uw = 0.0
     for i in range(2):

time: 146 us -> 145 us (level)
  no operation moved by 1% of the time
where the time goes in v7:
time: 145 us
  blocking collectives  55 us (38%)
  starting transfers between devices  34.7 us (24%)
  waiting for transfers between devices  30.6 us (21%)
  Pallas kernels  17 us (12%)
  local copies, waits for them, and re-layouts  4.46 us (3%)
  other arithmetic  2.21 us (2%)
    all_to_all x3, blocking collectives, op_exchange(): return lax.all_to_all(x, 'op', 0, 0, tiled=True)  55 us
    ppermute x23, waiting for transfers between devices, swap(): return lax.ppermute(x, 'qn', [(i, i ^ bits) for i in range(16)])  25.4 us
    ppermute x23, starting transfers between devices, swap(): return lax.ppermute(x, 'qn', [(i, i ^ bits) for i in range(16)])  21 us
    pallas_call x2, Pallas kernels, apply_ham(): pl.pallas_call(functools.partial(ham_kernel, by_block), in_specs=[SMEM, S...  12.6 us
    ppermute x4, starting transfers between devices, swap_other_x(): lax.ppermute(x, ('op', 'qn'), [(i, i ^ 8 * 16 + 2) for i in range(256)])  8.59 us
    all_to_all x1, starting transfers between devices, op_exchange(): return lax.all_to_all(x, 'op', 0, 0, tiled=True)  5.15 us
    unnamed x8, local copies, waits for them, and re-layouts  4.38 us
    all_to_all x1, waiting for transfers between devices, op_exchange(): return lax.all_to_all(x, 'op', 0, 0, tiled=True)  4.12 us
  transfers between devices with their start and end apart: 28, of which 17 were waited for; matrix products, arithmetic and copies ran while one was open for 1% of the time, Pallas kernels for 1%

profile of v7, /device:TPU:32, one launch (start us, length us, event | category | flops | bytes accessed | tf_op | source)
XLA Modules:
  0.0 144.8 jit_solution(11784909790355507402)
XLA Ops:
  0.6 1.1 convert.5
  1.9 1.3 collective-permute-done.1
  3.2 3.1 %collective-permute-start.8 = (bf16[4,256,128]{2,1,0:T(8,128)(2,1)S(1)}, bf16[4,256,128]{2,1,0:T(8,128)(2,1)S(1)}, u32[]{:S(2)}, u32[]{:S(2)}) collective-permute-start(bf16[4,256,128]{2,1,0:T(8,128)(2,1)S(1)} %maximum_select_fusion.refs_0_), channel_id=1, source_target_pairs={{0,12},{1,13},{2,14},{3,15},{4,8},{5,9},{6,10},{7,11},{8,4},{9,5},... | collective-permute-start | bytes 786440 | tf_op jit(solution)/shard_map/ppermute | solution.py:222
  6.5 1.5 %collective-permute-start.5 = (bf16[4,256,128]{2,1,0:T(8,128)(2,1)S(1)}, bf16[4,256,128]{2,1,0:T(8,128)(2,1)S(1)}, u32[]{:S(2)}, u32[]{:S(2)}) collective-permute-start(bf16[4,256,128]{2,1,0:T(8,128)(2,1)S(1)} %maximum_select_fusion.refs_0_), channel_id=1, source_target_pairs={{0,8},{1,9},{2,10},{3,11},{4,12},{5,13},{6,14},{7,15},{8,0},{9,1},... | collective-permute-start | bytes 786440 | tf_op jit(solution)/shard_map/ppermute | solution.py:222
  8.0 0.8 xor_bitcast_fusion
  8.8 1.5 %collective-permute-start.2 = (bf16[4,256,128]{2,1,0:T(8,128)(2,1)S(1)}, bf16[4,256,128]{2,1,0:T(8,128)(2,1)S(1)}, u32[]{:S(2)}, u32[]{:S(2)}) collective-permute-start(bf16[4,256,128]{2,1,0:T(8,128)(2,1)S(1)} %maximum_select_fusion.refs_0_), channel_id=1, source_target_pairs={{0,2},{1,3},{2,0},{3,1},{4,6},{5,7},{6,4},{7,5},{8,10},{9,11},{10,... | collective-permute-start | bytes 786440 | tf_op jit(solution)/shard_map/ppermute | solution.py:222
  10.3 2.6 %collective-permute-done.8.refs_7_ = bf16[4,256,128]{2,1,0:T(8,128)(2,1)S(1)} collective-permute-done((bf16[4,256,128]{2,1,0:T(8,128)(2,1)S(1)}, bf16[4,256,128]{2,1,0:T(8,128)(2,1)S(1)}, u32[]{:S(2)}, u32[]{:S(2)}) %collective-permute-start.8) | collective-permute-done | bytes 262176 | tf_op jit(solution)/shard_map/ppermute | solution.py:222
  12.9 2.8 %collective-permute-start.9 = (bf16[4,256,128]{2,1,0:T(8,128)(2,1)S(1)}, bf16[4,256,128]{2,1,0:T(8,128)(2,1)S(1)}, u32[]{:S(2)}, u32[]{:S(2)}) collective-permute-start(bf16[4,256,128]{2,1,0:T(8,128)(2,1)S(1)} %collective-permute-done.8.refs_7_), channel_id=1, source_target_pairs={{0,130},{1,131},{2,128},{3,129},{4,134},{5,135},{6,132},{7,133},{8... | collective-permute-start | bytes 786440 | tf_op jit(solution)/shard_map/ppermute | solution.py:226
  15.7 1.3 collective-permute-start.4
  17.0 2.8 %collective-permute-done.5.refs_4_ = bf16[4,256,128]{2,1,0:T(8,128)(2,1)S(1)} collective-permute-done((bf16[4,256,128]{2,1,0:T(8,128)(2,1)S(1)}, bf16[4,256,128]{2,1,0:T(8,128)(2,1)S(1)}, u32[]{:S(2)}, u32[]{:S(2)}) %collective-permute-start.5) | collective-permute-done | bytes 262176 | tf_op jit(solution)/shard_map/ppermute | solution.py:222
  19.9 2.8 %collective-permute-start.7 = (bf16[2,256,128]{2,1,0:T(8,128)(2,1)S(1)}, bf16[2,256,128]{2,1,0:T(8,128)(2,1)S(1)}, u32[]{:S(2)}, u32[]{:S(2)}) collective-permute-start(bf16[2,256,128]{2,1,0:T(8,128)(2,1)S(1)} %get-tuple-element.46), channel_id=1, source_target_pairs={{0,130},{1,131},{2,128},{3,129},{4,134},{5,135},{6,132},{7,133},{8... | collective-permute-start | bytes 393224 | tf_op jit(solution)/shard_map/ppermute | solution.py:226
  22.7 0.2 collective-permute-start.6
  22.9 2.2 %copy-done.3 = bf16[32,256,256]{2,1,0:T(8,128)(2,1)S(1)} copy-done((bf16[32,256,256]{2,1,0:T(8,128)(2,1)S(1)}, bf16[32,256,256]{2,1,0:T(8,128)(2,1)}, u32[]{:S(2)}) %copy-start.3) | copy-done | bytes 4194328
  25.1 1.4 shard_map.59.refs_10_
  26.6 1.1 collective-permute-done.6.refs_5_
  27.7 6.3 %shard_map.60 = (f32[1024,128]{1,0:T(8,128)S(1)}, f32[1024,128]{1,0:T(8,128)S(1)}) custom-call(s32[3,4,32]{2,1,0:T(4,128)S(1)} %get-tuple-element.50.meta, s32[1]{0:T(128)} %bitcast.1.core_ref, bf16[4,256,128]{2,1,0:T(8,128)(2,1)S(1)} %maximum_select_fusion.refs_0_, bf16[4,256,128]{2,1,0:T(8,128)(2,1)S(1)} %collective-permute-done.2.refs_1_, ...), custom_call_target="tpu_custom_call" | custom-call | tf_op jit(solution)/shard_map/pallas_call | solution.py:89
  34.1 1.9 %collective-permute-done.10 = f32[1024,128]{1,0:T(8,128)S(1)} collective-permute-done((f32[1024,128]{1,0:T(8,128)S(1)}, f32[1024,128]{1,0:T(8,128)S(1)}, u32[]{:S(2)}, u32[]{:S(2)}) %collective-permute-start.10) | collective-permute-done | bytes 524320 | tf_op jit(solution)/shard_map/ppermute | solution.py:222
  36.1 21.0 %all_to_all.20 = bf16[16,64,128]{2,1,0:T(8,128)(2,1)S(1)} all-to-all(bf16[16,64,128]{2,1,0:T(8,128)(2,1)S(1)} %bitcast.12), channel_id=1, replica_groups=mesh['op'=16,'qn'=16] {'op'}, dimensions={0} | all-to-all | bytes 524288 | tf_op jit(solution)/shard_map/all_to_all | solution.py:237
  57.2 15.8 %all_to_all.21 = bf16[16,64,128]{2,1,0:T(8,128)(2,1)S(1)} all-to-all(bf16[16,64,128]{2,1,0:T(8,128)(2,1)S(1)} %broadcast_in_dim.2), channel_id=1, replica_groups=mesh['op'=16,'qn'=16] {'op'}, dimensions={0} | all-to-all | bytes 524288 | tf_op jit(solution)/shard_map/all_to_all | solution.py:237
  73.0 3.0 %collective-permute-start.17 = (bf16[4,256,128]{2,1,0:T(8,128)(2,1)S(1)}, bf16[4,256,128]{2,1,0:T(8,128)(2,1)S(1)}, u32[]{:S(2)}, u32[]{:S(2)}) collective-permute-start(bf16[4,256,128]{2,1,0:T(8,128)(2,1)S(1)} %bitcast.7), channel_id=1, source_target_pairs={{0,12},{1,13},{2,14},{3,15},{4,8},{5,9},{6,10},{7,11},{8,4},{9,5},... | collective-permute-start | bytes 786440 | tf_op jit(solution)/shard_map/ppermute | solution.py:222
  76.0 1.7 %collective-permute-start.14 = (bf16[4,256,128]{2,1,0:T(8,128)(2,1)S(1)}, bf16[4,256,128]{2,1,0:T(8,128)(2,1)S(1)}, u32[]{:S(2)}, u32[]{:S(2)}) collective-permute-start(bf16[4,256,128]{2,1,0:T(8,128)(2,1)S(1)} %bitcast.9), channel_id=1, source_target_pairs={{0,8},{1,9},{2,10},{3,11},{4,12},{5,13},{6,14},{7,15},{8,0},{9,1},... | collective-permute-start | bytes 786440 | tf_op jit(solution)/shard_map/ppermute | solution.py:222
  77.7 0.7 collective-permute-start.11
  78.6 4.7 %collective-permute-done.17.refs_7_ = bf16[4,256,128]{2,1,0:T(8,128)(2,1)S(1)} collective-permute-done((bf16[4,256,128]{2,1,0:T(8,128)(2,1)S(1)}, bf16[4,256,128]{2,1,0:T(8,128)(2,1)S(1)}, u32[]{:S(2)}, u32[]{:S(2)}) %collective-permute-start.17) | collective-permute-done | bytes 262176 | tf_op jit(solution)/shard_map/ppermute | solution.py:222
  83.3 0.4 collective-permute-start.18
  83.7 0.9 collective-permute-done.12.refs_2_
  84.5 0.6 collective-permute-start.13
  85.1 1.9 %collective-permute-done.14.refs_4_ = bf16[4,256,128]{2,1,0:T(8,128)(2,1)S(1)} collective-permute-done((bf16[4,256,128]{2,1,0:T(8,128)(2,1)S(1)}, bf16[4,256,128]{2,1,0:T(8,128)(2,1)S(1)}, u32[]{:S(2)}, u32[]{:S(2)}) %collective-permute-start.14) | collective-permute-done | bytes 262176 | tf_op jit(solution)/shard_map/ppermute | solution.py:222
  87.1 2.6 %collective-permute-start.16 = (bf16[2,256,128]{2,1,0:T(8,128)(2,1)S(1)}, bf16[2,256,128]{2,1,0:T(8,128)(2,1)S(1)}, u32[]{:S(2)}, u32[]{:S(2)}) collective-permute-start(bf16[2,256,128]{2,1,0:T(8,128)(2,1)S(1)} %get-tuple-element.44), channel_id=1, source_target_pairs={{0,130},{1,131},{2,128},{3,129},{4,134},{5,135},{6,132},{7,133},{8... | collective-permute-start | bytes 393224 | tf_op jit(solution)/shard_map/ppermute | solution.py:226
  89.9 2.2 %copy-done.1 = bf16[32,256,256]{2,1,0:T(8,128)(2,1)S(1)} copy-done((bf16[32,256,256]{2,1,0:T(8,128)(2,1)S(1)}, bf16[32,256,256]{2,1,0:T(8,128)(2,1)}, u32[]{:S(2)}) %copy-start.1) | copy-done | bytes 4194328
  92.1 0.5 shard_map.61
  92.6 1.1 collective-permute-done.16.refs_6_
  93.6 1.0 collective-permute-done.15.refs_5_
  94.6 6.3 %shard_map.62 = (f32[2,512,128]{2,1,0:T(8,128)S(1)}, bf16[2,512,128]{2,1,0:T(8,128)(2,1)S(1)}) custom-call(s32[3,4,32]{2,1,0:T(4,128)S(1)} %get-tuple-element.51.meta, s32[1]{0:T(128)} %bitcast.1.core_ref, bf16[4,256,128]{2,1,0:T(8,128)(2,1)S(1)} %bitcast.11, bf16[4,256,128]{2,1,0:T(8,128)(2,1)S(1)} %collective-permute-done.11.refs_1_, ...), custom_call_target="tpu_custom_call" | custom-call | tf_op jit(solution)/shard_map/pallas_call | solution.py:89
  101.1 1.5 %collective-permute-done.20.got = bf16[2,512,128]{2,1,0:T(8,128)(2,1)S(1)} collective-permute-done((bf16[2,512,128]{2,1,0:T(8,128)(2,1)S(1)}, bf16[2,512,128]{2,1,0:T(8,128)(2,1)S(1)}, u32[]{:S(2)}, u32[]{:S(2)}) %collective-permute-start.20) | collective-permute-done | bytes 262176 | tf_op jit(solution)/shard_map/ppermute | solution.py:222
  102.6 1.0 shard_map.63
  103.6 5.2 %all-to-all-start.2 = ((f32[16,64,128]{2,1,0:T(8,128)}), f32[16,64,128]{2,1,0:T(8,128)S(1)}, u32[]{:S(2)}, u32[]{:S(2)}) async-start(f32[16,64,128]{2,1,0:T(8,128)} %get-tuple-element.41), calls=%async_computation.2 | async-start | bytes 1048576 | tf_op jit(solution)/shard_map/all_to_all | solution.py:237
  108.7 0.5 collective-permute-start.23
  109.3 0.9 collective-permute-start.22
  110.2 0.4 collective-permute-start.21
  110.6 1.2 collective-permute-done.23
  111.8 1.1 collective-permute-done.22
  112.9 3.0 %collective-permute-start.26 = (f32[8,128]{1,0:T(8,128)S(1)}, f32[8,128]{1,0:T(8,128)S(1)}, u32[]{:S(2)}, u32[]{:S(2)}) collective-permute-start(f32[8,128]{1,0:T(8,128)S(1)} %add_add_fusion.1), channel_id=1, source_target_pairs={{0,12},{1,13},{2,14},{3,15},{4,8},{5,9},{6,10},{7,11},{8,4},{9,5},... | collective-permute-start | bytes 12296 | tf_op jit(solution)/shard_map/ppermute | solution.py:222
  115.9 1.7 %collective-permute-start.24 = (f32[8,128]{1,0:T(8,128)S(1)}, f32[8,128]{1,0:T(8,128)S(1)}, u32[]{:S(2)}, u32[]{:S(2)}) collective-permute-start(f32[8,128]{1,0:T(8,128)S(1)} %add_add_fusion.1), channel_id=1, source_target_pairs={{0,8},{1,9},{2,10},{3,11},{4,12},{5,13},{6,14},{7,15},{8,0},{9,1},... | collective-permute-start | bytes 12296 | tf_op jit(solution)/shard_map/ppermute | solution.py:222
  117.8 1.7 %collective-permute-done.25 = f32[8,128]{1,0:T(8,128)S(1)} collective-permute-done((f32[8,128]{1,0:T(8,128)S(1)}, f32[8,128]{1,0:T(8,128)S(1)}, u32[]{:S(2)}, u32[]{:S(2)}) %collective-permute-start.25) | collective-permute-done | bytes 4128 | tf_op jit(solution)/shard_map/ppermute | solution.py:222
  119.5 1.5 %collective-permute-done.24 = f32[8,128]{1,0:T(8,128)S(1)} collective-permute-done((f32[8,128]{1,0:T(8,128)S(1)}, f32[8,128]{1,0:T(8,128)S(1)}, u32[]{:S(2)}, u32[]{:S(2)}) %collective-permute-start.24) | collective-permute-done | bytes 4128 | tf_op jit(solution)/shard_map/ppermute | solution.py:222
  121.0 4.1 %all-to-all-done.2.parts = f32[16,64,128]{2,1,0:T(8,128)S(1)} async-done(((f32[16,64,128]{2,1,0:T(8,128)}), f32[16,64,128]{2,1,0:T(8,128)S(1)}, u32[]{:S(2)}, u32[]{:S(2)}) %all-to-all-start.2) | async-done | bytes 524320 | tf_op jit(solution)/shard_map/all_to_all | solution.py:237
  125.3 18.1 %all_to_all.22.whole = bf16[16,80,128]{2,1,0:T(8,128)(2,1)S(1)} all-to-all(bf16[16,80,128]{2,1,0:T(8,128)(2,1)S(1)} %shard_map.64), channel_id=1, replica_groups=mesh['op'=16,'qn'=16] {'op'}, dimensions={0} | all-to-all | bytes 655360 | tf_op jit(solution)/shard_map/all_to_all | solution.py:237
  143.4 1.4 shard_map.65
  (40 shorter events, 1.3 us)
Async XLA Ops:
  1.7 1.4 collective-permute-start.1
  3.2 9.7 %collective-permute-start.8 = (bf16[4,256,128]{2,1,0:T(8,128)(2,1)S(1)}, bf16[4,256,128]{2,1,0:T(8,128)(2,1)S(1)}, u32[]{:S(2)}, u32[]{:S(2)}) collective-permute-start(bf16[4,256,128]{2,1,0:T(8,128)(2,1)S(1)} %maximum_select_fusion.refs_0_), channel_id=1, source_target_pairs={{0,12},{1,13},{2,14},{3,15},{4,8},{5,9},{6,10},{7,11},{8,4},{9,5},... | collective-permute-start | bytes 786440 | tf_op jit(solution)/shard_map/ppermute | solution.py:222
  6.3 9.4 %collective-permute-start.3 = (bf16[4,256,128]{2,1,0:T(8,128)(2,1)S(1)}, bf16[4,256,128]{2,1,0:T(8,128)(2,1)S(1)}, u32[]{:S(2)}, u32[]{:S(2)}) collective-permute-start(bf16[4,256,128]{2,1,0:T(8,128)(2,1)S(1)} %maximum_select_fusion.refs_0_), channel_id=1, source_target_pairs={{0,4},{1,5},{2,6},{3,7},{4,0},{5,1},{6,2},{7,3},{8,12},{9,13},{10,... | collective-permute-start | bytes 786440 | tf_op jit(solution)/shard_map/ppermute | solution.py:222
  6.5 13.4 %collective-permute-start.5 = (bf16[4,256,128]{2,1,0:T(8,128)(2,1)S(1)}, bf16[4,256,128]{2,1,0:T(8,128)(2,1)S(1)}, u32[]{:S(2)}, u32[]{:S(2)}) collective-permute-start(bf16[4,256,128]{2,1,0:T(8,128)(2,1)S(1)} %maximum_select_fusion.refs_0_), channel_id=1, source_target_pairs={{0,8},{1,9},{2,10},{3,11},{4,12},{5,13},{6,14},{7,15},{8,0},{9,1},... | collective-permute-start | bytes 786440 | tf_op jit(solution)/shard_map/ppermute | solution.py:222
  8.0 19.7 %copy-start = (bf16[32,256,256]{2,1,0:T(8,128)(2,1)S(1)}, bf16[32,256,256]{2,1,0:T(8,128)(2,1)}, u32[]{:S(2)}) copy-start(bf16[32,256,256]{2,1,0:T(8,128)(2,1)} %left.1) | copy-start | bytes 12582916
  8.8 13.9 %collective-permute-start = (s32[3,2,32]{2,1,0:T(2,128)S(1)}, s32[3,2,32]{2,1,0:T(2,128)S(1)}, u32[]{:S(2)}, u32[]{:S(2)}) collective-permute-start(s32[3,2,32]{2,1,0:T(2,128)S(1)} %xor_bitcast_fusion), channel_id=1, source_target_pairs={{0,1},{1,0},{2,3},{3,2},{4,5},{5,4},{6,7},{7,6},{8,9},{9,8},{10,11... | collective-permute-start | bytes 2312 | tf_op jit(solution)/shard_map/ppermute | solution.py:222
  8.8 17.7 %collective-permute-start.2 = (bf16[4,256,128]{2,1,0:T(8,128)(2,1)S(1)}, bf16[4,256,128]{2,1,0:T(8,128)(2,1)S(1)}, u32[]{:S(2)}, u32[]{:S(2)}) collective-permute-start(bf16[4,256,128]{2,1,0:T(8,128)(2,1)S(1)} %maximum_select_fusion.refs_0_), channel_id=1, source_target_pairs={{0,2},{1,3},{2,0},{3,1},{4,6},{5,7},{6,4},{7,5},{8,10},{9,11},{10,... | collective-permute-start | bytes 786440 | tf_op jit(solution)/shard_map/ppermute | solution.py:222
  12.9 14.7 %collective-permute-start.9 = (bf16[4,256,128]{2,1,0:T(8,128)(2,1)S(1)}, bf16[4,256,128]{2,1,0:T(8,128)(2,1)S(1)}, u32[]{:S(2)}, u32[]{:S(2)}) collective-permute-start(bf16[4,256,128]{2,1,0:T(8,128)(2,1)S(1)} %collective-permute-done.8.refs_7_), channel_id=1, source_target_pairs={{0,130},{1,131},{2,128},{3,129},{4,134},{5,135},{6,132},{7,133},{8... | collective-permute-start | bytes 786440 | tf_op jit(solution)/shard_map/ppermute | solution.py:226
  15.7 12.0 %collective-permute-start.4 = (bf16[4,256,128]{2,1,0:T(8,128)(2,1)S(1)}, bf16[4,256,128]{2,1,0:T(8,128)(2,1)S(1)}, u32[]{:S(2)}, u32[]{:S(2)}) collective-permute-start(bf16[4,256,128]{2,1,0:T(8,128)(2,1)S(1)} %collective-permute-done.3.refs_2_), channel_id=1, source_target_pairs={{0,2},{1,3},{2,0},{3,1},{4,6},{5,7},{6,4},{7,5},{8,10},{9,11},{10,... | collective-permute-start | bytes 786440 | tf_op jit(solution)/shard_map/ppermute | solution.py:222
  19.9 6.7 %collective-permute-start.7 = (bf16[2,256,128]{2,1,0:T(8,128)(2,1)S(1)}, bf16[2,256,128]{2,1,0:T(8,128)(2,1)S(1)}, u32[]{:S(2)}, u32[]{:S(2)}) collective-permute-start(bf16[2,256,128]{2,1,0:T(8,128)(2,1)S(1)} %get-tuple-element.46), channel_id=1, source_target_pairs={{0,130},{1,131},{2,128},{3,129},{4,134},{5,135},{6,132},{7,133},{8... | collective-permute-start | bytes 393224 | tf_op jit(solution)/shard_map/ppermute | solution.py:226
  22.7 5.0 %collective-permute-start.6 = (bf16[2,256,128]{2,1,0:T(8,128)(2,1)S(1)}, bf16[2,256,128]{2,1,0:T(8,128)(2,1)S(1)}, u32[]{:S(2)}, u32[]{:S(2)}) collective-permute-start(bf16[2,256,128]{2,1,0:T(8,128)(2,1)S(1)} %get-tuple-element.47), channel_id=1, source_target_pairs={{0,2},{1,3},{2,0},{3,1},{4,6},{5,7},{6,4},{7,5},{8,10},{9,11},{10,... | collective-permute-start | bytes 393224 | tf_op jit(solution)/shard_map/ppermute | solution.py:222
  22.9 2.2 %copy-start.3 = (bf16[32,256,256]{2,1,0:T(8,128)(2,1)S(1)}, bf16[32,256,256]{2,1,0:T(8,128)(2,1)}, u32[]{:S(2)}) copy-start(bf16[32,256,256]{2,1,0:T(8,128)(2,1)} %r_ref.1) | copy-start | bytes 12582916
  34.0 55.9 %copy-start.2 = (f32[2,256,256]{2,1,0:T(8,128)S(1)}, f32[2,256,256]{2,1,0:T(8,128)}, u32[]{:S(2)}) copy-start(f32[2,256,256]{2,1,0:T(8,128)} %p_ref.1) | copy-start | bytes 1572868
  34.0 2.0 %collective-permute-start.10 = (f32[1024,128]{1,0:T(8,128)S(1)}, f32[1024,128]{1,0:T(8,128)S(1)}, u32[]{:S(2)}, u32[]{:S(2)}) collective-permute-start(f32[1024,128]{1,0:T(8,128)S(1)} %get-tuple-element.23), channel_id=1, source_target_pairs={{0,1},{1,0},{2,3},{3,2},{4,5},{5,4},{6,7},{7,6},{8,9},{9,8},{10,11... | collective-permute-start | bytes 1572872 | tf_op jit(solution)/shard_map/ppermute | solution.py:222
  73.0 10.2 %collective-permute-start.17 = (bf16[4,256,128]{2,1,0:T(8,128)(2,1)S(1)}, bf16[4,256,128]{2,1,0:T(8,128)(2,1)S(1)}, u32[]{:S(2)}, u32[]{:S(2)}) collective-permute-start(bf16[4,256,128]{2,1,0:T(8,128)(2,1)S(1)} %bitcast.7), channel_id=1, source_target_pairs={{0,12},{1,13},{2,14},{3,15},{4,8},{5,9},{6,10},{7,11},{8,4},{9,5},... | collective-permute-start | bytes 786440 | tf_op jit(solution)/shard_map/ppermute | solution.py:222
  76.0 8.5 %collective-permute-start.12 = (bf16[4,256,128]{2,1,0:T(8,128)(2,1)S(1)}, bf16[4,256,128]{2,1,0:T(8,128)(2,1)S(1)}, u32[]{:S(2)}, u32[]{:S(2)}) collective-permute-start(bf16[4,256,128]{2,1,0:T(8,128)(2,1)S(1)} %bitcast.8), channel_id=1, source_target_pairs={{0,4},{1,5},{2,6},{3,7},{4,0},{5,1},{6,2},{7,3},{8,12},{9,13},{10,... | collective-permute-start | bytes 786440 | tf_op jit(solution)/shard_map/ppermute | solution.py:222
  76.0 11.0 %collective-permute-start.14 = (bf16[4,256,128]{2,1,0:T(8,128)(2,1)S(1)}, bf16[4,256,128]{2,1,0:T(8,128)(2,1)S(1)}, u32[]{:S(2)}, u32[]{:S(2)}) collective-permute-start(bf16[4,256,128]{2,1,0:T(8,128)(2,1)S(1)} %bitcast.9), channel_id=1, source_target_pairs={{0,8},{1,9},{2,10},{3,11},{4,12},{5,13},{6,14},{7,15},{8,0},{9,1},... | collective-permute-start | bytes 786440 | tf_op jit(solution)/shard_map/ppermute | solution.py:222
  77.7 14.9 %collective-permute-start.11 = (bf16[4,256,128]{2,1,0:T(8,128)(2,1)S(1)}, bf16[4,256,128]{2,1,0:T(8,128)(2,1)S(1)}, u32[]{:S(2)}, u32[]{:S(2)}) collective-permute-start(bf16[4,256,128]{2,1,0:T(8,128)(2,1)S(1)} %bitcast.10), channel_id=1, source_target_pairs={{0,2},{1,3},{2,0},{3,1},{4,6},{5,7},{6,4},{7,5},{8,10},{9,11},{10,... | collective-permute-start | bytes 786440 | tf_op jit(solution)/shard_map/ppermute | solution.py:222
  78.5 11.2 %collective-permute-start.19 = (bf16[2,256,128]{2,1,0:T(8,128)(2,1)S(1)}, bf16[2,256,128]{2,1,0:T(8,128)(2,1)S(1)}, u32[]{:S(2)}, u32[]{:S(2)}) collective-permute-start(bf16[2,256,128]{2,1,0:T(8,128)(2,1)S(1)} %bitcast.14), channel_id=1, source_target_pairs={{0,1},{1,0},{2,3},{3,2},{4,5},{5,4},{6,7},{7,6},{8,9},{9,8},{10,11... | collective-permute-start | bytes 393224 | tf_op jit(solution)/shard_map/ppermute | solution.py:222
  83.3 11.4 %collective-permute-start.18 = (bf16[4,256,128]{2,1,0:T(8,128)(2,1)S(1)}, bf16[4,256,128]{2,1,0:T(8,128)(2,1)S(1)}, u32[]{:S(2)}, u32[]{:S(2)}) collective-permute-start(bf16[4,256,128]{2,1,0:T(8,128)(2,1)S(1)} %collective-permute-done.17.refs_7_), channel_id=1, source_target_pairs={{0,130},{1,131},{2,128},{3,129},{4,134},{5,135},{6,132},{7,133},{8... | collective-permute-start | bytes 786440 | tf_op jit(solution)/shard_map/ppermute | solution.py:226
  84.5 10.1 %collective-permute-start.13 = (bf16[4,256,128]{2,1,0:T(8,128)(2,1)S(1)}, bf16[4,256,128]{2,1,0:T(8,128)(2,1)S(1)}, u32[]{:S(2)}, u32[]{:S(2)}) collective-permute-start(bf16[4,256,128]{2,1,0:T(8,128)(2,1)S(1)} %collective-permute-done.12.refs_2_), channel_id=1, source_target_pairs={{0,2},{1,3},{2,0},{3,1},{4,6},{5,7},{6,4},{7,5},{8,10},{9,11},{10,... | collective-permute-start | bytes 786440 | tf_op jit(solution)/shard_map/ppermute | solution.py:222
  87.1 6.6 %collective-permute-start.16 = (bf16[2,256,128]{2,1,0:T(8,128)(2,1)S(1)}, bf16[2,256,128]{2,1,0:T(8,128)(2,1)S(1)}, u32[]{:S(2)}, u32[]{:S(2)}) collective-permute-start(bf16[2,256,128]{2,1,0:T(8,128)(2,1)S(1)} %get-tuple-element.44), channel_id=1, source_target_pairs={{0,130},{1,131},{2,128},{3,129},{4,134},{5,135},{6,132},{7,133},{8... | collective-permute-start | bytes 393224 | tf_op jit(solution)/shard_map/ppermute | solution.py:226
  89.7 5.0 %collective-permute-start.15 = (bf16[2,256,128]{2,1,0:T(8,128)(2,1)S(1)}, bf16[2,256,128]{2,1,0:T(8,128)(2,1)S(1)}, u32[]{:S(2)}, u32[]{:S(2)}) collective-permute-start(bf16[2,256,128]{2,1,0:T(8,128)(2,1)S(1)} %get-tuple-element.45), channel_id=1, source_target_pairs={{0,2},{1,3},{2,0},{3,1},{4,6},{5,7},{6,4},{7,5},{8,10},{9,11},{10,... | collective-permute-start | bytes 393224 | tf_op jit(solution)/shard_map/ppermute | solution.py:222
  89.9 2.2 %copy-start.1 = (bf16[32,256,256]{2,1,0:T(8,128)(2,1)S(1)}, bf16[32,256,256]{2,1,0:T(8,128)(2,1)}, u32[]{:S(2)}) copy-start(bf16[32,256,256]{2,1,0:T(8,128)(2,1)} %left.1) | copy-start | bytes 12582916
  101.0 1.6 %collective-permute-start.20 = (bf16[2,512,128]{2,1,0:T(8,128)(2,1)S(1)}, bf16[2,512,128]{2,1,0:T(8,128)(2,1)S(1)}, u32[]{:S(2)}, u32[]{:S(2)}) collective-permute-start(bf16[2,512,128]{2,1,0:T(8,128)(2,1)S(1)} %get-tuple-element.37), channel_id=1, source_target_pairs={{0,1},{1,0},{2,3},{3,2},{4,5},{5,4},{6,7},{7,6},{8,9},{9,8},{10,11... | collective-permute-start | bytes 786440 | tf_op jit(solution)/shard_map/ppermute | solution.py:222
  103.6 21.6 %all-to-all-start.2 = ((f32[16,64,128]{2,1,0:T(8,128)}), f32[16,64,128]{2,1,0:T(8,128)S(1)}, u32[]{:S(2)}, u32[]{:S(2)}) async-start(f32[16,64,128]{2,1,0:T(8,128)} %get-tuple-element.41), calls=%async_computation.2 | async-start | bytes 1048576 | tf_op jit(solution)/shard_map/all_to_all | solution.py:237
  108.7 3.0 %collective-permute-start.23 = (f32[8,128]{1,0:T(8,128)S(1)}, f32[8,128]{1,0:T(8,128)S(1)}, u32[]{:S(2)}, u32[]{:S(2)}) collective-permute-start(f32[8,128]{1,0:T(8,128)S(1)} %get-tuple-element.40), channel_id=1, source_target_pairs={{0,3},{1,2},{2,1},{3,0},{4,7},{5,6},{6,5},{7,4},{8,11},{9,10},{10,... | collective-permute-start | bytes 12296 | tf_op jit(solution)/shard_map/ppermute | solution.py:222
  109.3 3.6 %collective-permute-start.22 = (f32[8,128]{1,0:T(8,128)S(1)}, f32[8,128]{1,0:T(8,128)S(1)}, u32[]{:S(2)}, u32[]{:S(2)}) collective-permute-start(f32[8,128]{1,0:T(8,128)S(1)} %get-tuple-element.40), channel_id=1, source_target_pairs={{0,2},{1,3},{2,0},{3,1},{4,6},{5,7},{6,4},{7,5},{8,10},{9,11},{10,... | collective-permute-start | bytes 12296 | tf_op jit(solution)/shard_map/ppermute | solution.py:222
  110.2 2.7 %collective-permute-start.21 = (f32[8,128]{1,0:T(8,128)S(1)}, f32[8,128]{1,0:T(8,128)S(1)}, u32[]{:S(2)}, u32[]{:S(2)}) collective-permute-start(f32[8,128]{1,0:T(8,128)S(1)} %get-tuple-element.40), channel_id=1, source_target_pairs={{0,1},{1,0},{2,3},{3,2},{4,5},{5,4},{6,7},{7,6},{8,9},{9,8},{10,11... | collective-permute-start | bytes 12296 | tf_op jit(solution)/shard_map/ppermute | solution.py:222
  112.9 4.9 %collective-permute-start.26 = (f32[8,128]{1,0:T(8,128)S(1)}, f32[8,128]{1,0:T(8,128)S(1)}, u32[]{:S(2)}, u32[]{:S(2)}) collective-permute-start(f32[8,128]{1,0:T(8,128)S(1)} %add_add_fusion.1), channel_id=1, source_target_pairs={{0,12},{1,13},{2,14},{3,15},{4,8},{5,9},{6,10},{7,11},{8,4},{9,5},... | collective-permute-start | bytes 12296 | tf_op jit(solution)/shard_map/ppermute | solution.py:222
  115.9 3.6 %collective-permute-start.25 = (f32[8,128]{1,0:T(8,128)S(1)}, f32[8,128]{1,0:T(8,128)S(1)}, u32[]{:S(2)}, u32[]{:S(2)}) collective-permute-start(f32[8,128]{1,0:T(8,128)S(1)} %add_add_fusion.1), channel_id=1, source_target_pairs={{0,4},{1,5},{2,6},{3,7},{4,0},{5,1},{6,2},{7,3},{8,12},{9,13},{10,... | collective-permute-start | bytes 12296 | tf_op jit(solution)/shard_map/ppermute | solution.py:222
  115.9 5.1 %collective-permute-start.24 = (f32[8,128]{1,0:T(8,128)S(1)}, f32[8,128]{1,0:T(8,128)S(1)}, u32[]{:S(2)}, u32[]{:S(2)}) collective-permute-start(f32[8,128]{1,0:T(8,128)S(1)} %add_add_fusion.1), channel_id=1, source_target_pairs={{0,8},{1,9},{2,10},{3,11},{4,12},{5,13},{6,14},{7,15},{8,0},{9,1},... | collective-permute-start | bytes 12296 | tf_op jit(solution)/shard_map/ppermute | solution.py:222
